TPU v7x, 32 devices: a whole 2x2x4 slice. The times are simulated.
32 devices in a mesh: trial: 2 (over x), dp: 4 (over z), tensor: 4 (over y, core).
Axes of the slice: x: 2, y: 2, z: 4, core: 2. Of those that a mesh axis runs over, the one named last changes fastest.
Arguments:
- residual_rows: bfloat16 [1024, 8192], P(('trial', 'dp', 'tensor'))
- input_norm_weight: float32 [8192], replicated, may hold values from 0.25 to 1.75
- trial_row_index: int32 [2, 512], P(None, 'dp'), may hold values from 0 to 31, as said below
- keyvalue_weight: bfloat16 [8192, 2048], P('tensor'), may hold values from -0.0625 to 0.0625
- adapter_down_weight: bfloat16 [2, 8192, 128], P('trial', 'tensor'), may hold values from -0.0625 to 0.0625
- adapter_up_weight: bfloat16 [2, 64, 2048], P('trial'), may hold values from -0.75 to 0.75
- keyvalue_gradient: bfloat16 [2, 512, 2048], P('trial', ('dp', 'tensor')), may hold values from -6 to 6
Outputs:
- keyvalue_output: float32 [2, 512, 2048], P('trial', ('dp', 'tensor'))
- grad_a: float32 [2, 128, 8192], P('trial', 'dp', 'tensor')
- grad_b: float32 [2, 64, 2048], P('trial', None, ('dp', 'tensor'))
Inputs may be any that keep to these rules, and one draw needn't show every extreme that they name: `trial_row_index`: within each trial, each index of dp and each block of 16 consecutive tokens taken from one source device, the rows named are distinct.
All inputs are finite; a program needn't handle non-finite values.
Results may differ from a plain program's by a relative error of at most 0.0041.
Values may be sent and summed in bfloat16 or wider, within the bound.
No kernel may reach another device: no remote copies, remote signals or barrier semaphores. Data moves between devices by JAX's collectives and lax.ppermute only.
A program may use at most 64 MiB of HBM per device.

v0:
```python
import jax
import jax.numpy as jnp
from jax import lax
from jax.sharding import PartitionSpec as P

adapter_scale = 2.0
norm_eps = 1e-05


def shards(
    residual_rows,
    input_norm_weight,
    trial_row_index,
    keyvalue_weight,
    adapter_down_weight,
    adapter_up_weight,
    keyvalue_gradient,
):
    trials = lax.axis_size("trial")
    tensors = lax.axis_size("tensor")
    tok_dev = trial_row_index.shape[1]
    select = tok_dev // (trials * tensors)
    normed_input = keyvalue_weight.shape[0]
    kv_width = keyvalue_weight.shape[1]
    keyvalue_half = kv_width // 2
    rank_index = adapter_up_weight.shape[1]
    highest_precision = lax.Precision.HIGHEST
    wide = residual_rows.astype(jnp.float32)
    msq = jnp.mean(wide * wide, axis=1, keepdims=True)
    normed = (wide * lax.rsqrt(msq + norm_eps) * input_norm_weight[None, :]).astype(jnp.bfloat16)
    source = lax.axis_index("trial") * tensors + lax.axis_index("tensor")
    picks = lax.dynamic_slice_in_dim(trial_row_index, source * select, select, 1)
    chosen = jnp.take(normed, picks.reshape(-1), axis=0)
    chosen = chosen.reshape(trials, select, tensors, normed_input).transpose(0, 2, 1, 3)
    arrived = lax.all_to_all(
        chosen.reshape(trials * tensors, select, normed_input),
        ("trial", "tensor"),
        split_axis=0,
        concat_axis=0,
        tiled=True,
    )
    rows = arrived.reshape(tok_dev, normed_input)
    down_weight = adapter_down_weight[0]
    keyval = jnp.dot(rows, keyvalue_weight, preferred_element_type=jnp.float32)
    ranks = jnp.dot(rows, down_weight, preferred_element_type=jnp.float32)
    summed = lax.psum_scatter(
        jnp.concatenate([keyval, ranks], axis=1), "tensor", scatter_dimension=0, tiled=True
    )
    frozen_output_local = summed[:, :kv_width]
    local_rank_rows = summed[:, kv_width:]
    up_weight = adapter_up_weight[0].astype(jnp.float32)
    adapter_key = jnp.dot(
        local_rank_rows[:, :rank_index], up_weight[:, :keyvalue_half], precision=highest_precision
    )
    adapter_value = jnp.dot(
        local_rank_rows[:, rank_index:], up_weight[:, keyvalue_half:], precision=highest_precision
    )
    keyvalue_output = frozen_output_local + adapter_scale * jnp.concatenate(
        [adapter_key, adapter_value], axis=1
    )
    grad_in = keyvalue_gradient[0].astype(jnp.float32)
    key_gradient_full = jnp.dot(
        grad_in[:, :keyvalue_half], up_weight[:, :keyvalue_half].T, precision=highest_precision
    )
    value_gradient_full = jnp.dot(
        grad_in[:, keyvalue_half:], up_weight[:, keyvalue_half:].T, precision=highest_precision
    )
    rank_gradient = (
        adapter_scale * jnp.concatenate([key_gradient_full, value_gradient_full], axis=1)
    ).astype(jnp.bfloat16)
    every_rank = lax.all_gather(rank_gradient, "tensor", axis=0, tiled=True)
    grad_a_term = lax.dot_general(
        every_rank, rows, (((0,), (0,)), ((), ())), preferred_element_type=jnp.float32
    )
    grad_a = lax.psum_scatter(grad_a_term, "dp", scatter_dimension=0, tiled=True)
    key_down_gradient = jnp.dot(
        local_rank_rows[:, :rank_index].T, grad_in[:, :keyvalue_half], precision=highest_precision
    )
    value_down_gradient = jnp.dot(
        local_rank_rows[:, rank_index:].T, grad_in[:, keyvalue_half:], precision=highest_precision
    )
    up_gradient_term = adapter_scale * jnp.concatenate(
        [key_down_gradient, value_down_gradient], axis=1
    )
    grad_b = lax.psum_scatter(up_gradient_term, ("dp", "tensor"), scatter_dimension=1, tiled=True)
    return (keyvalue_output[None], grad_a[None], grad_b[None])


def solution(mesh):
    return jax.shard_map(
        shards,
        mesh=mesh,
        in_specs=(
            P(("trial", "dp", "tensor"), None),
            P(),
            P(None, "dp"),
            P("tensor", None),
            P("trial", "tensor", None),
            P("trial", None, None),
            P("trial", ("dp", "tensor"), None),
        ),
        out_specs=(
            P("trial", ("dp", "tensor"), None),
            P("trial", "dp", "tensor"),
            P("trial", None, ("dp", "tensor")),
        ),
        check_vma=False,
    )
```

profile of v0, /device:TPU:0, one launch (start us, length us, event | category | flops | bytes accessed | tf_op | source)
XLA Modules:
  0.0 153.6 jit_solution(10854352971382477353)
XLA Ops:
  7.2 0.0 copy-start
  7.2 0.0 reduce-scatter.4.cloned.1.call-start
  7.2 1.3 fusion
  8.5 0.8 compare_and_fusion
  9.3 0.1 reshape.64
  9.4 1.2 fusion.2
  10.6 0.9 gather_fusion
  11.5 0.4 gather.7
  11.9 0.6 copy_select_fusion
  12.5 13.9 %all_to_all.5 = bf16[8,16,2048]{2,1,0:T(8,128)(2,1)S(1)} all-to-all(bf16[8,16,2048]{2,1,0:T(8,128)(2,1)S(1)} %bitcast.23), channel_id=1, replica_groups=mesh['trial'=2,'dp'=4,'tensor'=4] {'trial','tensor'}, dimensions={0} | all-to-all | bytes 1048576 | tf_op jit(solution)/shard_map/all_to_all | solution.py:35
  26.4 0.3 fusion.3
  26.7 4.7 %fusion.26 = f32[128,2048]{1,0:T(8,128)S(1)} fusion(bf16[128,2048]{1,0:T(8,128)(2,1)S(1)} %bitcast.21, bf16[2048,2048]{1,0:T(8,128)(2,1)} %param.10), kind=kOutput, calls=%fused_computation.41 | convolution fusion | flops 1073741824 | bytes 9961472 | tf_op jit(solution)/shard_map/dot_general | solution.py:44
  31.4 1.1 pad_maximum_fusion
  32.5 0.0 reduce-scatter.4.cloned.1.call-update
  32.5 0.0 reduce-scatter.6.cloned.1.call-start
  32.6 0.1 fusion.10
  32.7 0.2 fusion.6
  32.9 0.1 fusion.20
  33.0 5.2 %all_gather.3 = bf16[128,128]{1,0:T(8,128)(2,1)S(1)} all-gather(bf16[32,128]{1,0:T(8,128)(2,1)S(1)} %fusion.20), channel_id=1, replica_groups=mesh['trial'=2,'dp'=4,'tensor'=4] {'tensor'}, dimensions={0}, use_global_device_ids=true | all-gather | bytes 40960 | tf_op jit(solution)/shard_map/all_gather | solution.py:71
  38.2 1.3 fusion.27
  39.5 0.0 reduce-scatter.6.cloned.1.call-update
  39.5 0.0 reduce-scatter.8.cloned.1.call-start
  39.6 18.8 %reduce-scatter.4.cloned.1.call-done = f32[32,2176]{1,0:T(8,128)} async-done(((f32[128,2176]{1,0:T(8,128)}), f32[32,2176]{1,0:T(8,128)}) %reduce-scatter.4.cloned.1.call-update) | async-done | bytes 278544 | tf_op jit(solution)/shard_map/reduce_scatter | solution.py:46
  58.3 1.0 fusion.17
  59.4 1.1 fusion.14
  60.5 0.8 maximum_multiply_fusion
  61.3 0.0 reduce-scatter.8.cloned.1.call-update
  61.3 1.0 fusion.8
  62.3 0.9 fusion.12
  63.2 1.7 %fusion.5 = f32[1,32,2048]{2,1,0:T(8,128)} fusion(f32[32,2176]{1,0:T(8,128)} %reduce-scatter.4.cloned.1.call-done, f32[32,1024]{1,0:T(8,128)S(1)} %fusion.8, f32[32,1024]{1,0:T(8,128)S(1)} %fusion.12), kind=kLoop, calls=%fused_computation.12 | loop fusion | flops 196608 | bytes 786432 | tf_op jit(solution)/shard_map/broadcast_in_dim | solution.py:86
  64.9 23.6 %reduce-scatter.6.cloned.1.call-done = f32[32,2048]{1,0:T(8,128)} async-done(((f32[128,2048]{1,0:T(8,128)}), f32[32,2048]{1,0:T(8,128)}) %reduce-scatter.6.cloned.1.call-update) | async-done | bytes 262160 | tf_op jit(solution)/shard_map/reduce_scatter | solution.py:75
  88.5 58.6 %reduce-scatter.8.cloned.1.call-done = f32[64,128]{1,0:T(8,128)} async-done(((f32[64,2048]{1,0:T(8,128)}), f32[64,128]{1,0:T(8,128)}) %reduce-scatter.8.cloned.1.call-update) | async-done | bytes 32784 | tf_op jit(solution)/shard_map/reduce_scatter | solution.py:85
  (8 shorter events, 0.0 us)
Async XLA Ops:
  7.2 19.2 %copy-start = (bf16[1,2048,128]{2,1,0:T(8,128)(2,1)S(1)}, bf16[1,2048,128]{2,1,0:T(8,128)(2,1)}, u32[]{:S(2)}) copy-start(bf16[1,2048,128]{2,1,0:T(8,128)(2,1)} %param.11) | copy-start | bytes 1572868
  7.2 51.2 %reduce-scatter.4.cloned.1.call-start = ((), (), s32[]{:S(2)}) async-start(), calls=%async_computation.4 | async-start | bytes 1392640 | tf_op jit(solution)/shard_map/reduce_scatter | solution.py:46
  26.7 5.9 %copy-start.1 = (bf16[1,64,2048]{2,1,0:T(8,128)(2,1)S(1)}, bf16[1,64,2048]{2,1,0:T(8,128)(2,1)}, u32[]{:S(2)}) copy-start(bf16[1,64,2048]{2,1,0:T(8,128)(2,1)} %param.12) | copy-start | bytes 786436
  26.7 5.9 %copy-start.2 = (bf16[1,32,2048]{2,1,0:T(8,128)(2,1)S(1)}, bf16[1,32,2048]{2,1,0:T(8,128)(2,1)}, u32[]{:S(2)}) copy-start(bf16[1,32,2048]{2,1,0:T(8,128)(2,1)} %param.13) | copy-start | bytes 393220
  32.5 56.0 %reduce-scatter.6.cloned.1.call-start = ((), (), s32[]{:S(2)}) async-start(), calls=%async_computation.5 | async-start | bytes 1310720 | tf_op jit(solution)/shard_map/reduce_scatter | solution.py:75
  39.5 107.5 %reduce-scatter.8.cloned.1.call-start = ((), (), s32[]{:S(2)}) async-start(), calls=%async_computation.6 | async-start | bytes 557056 | tf_op jit(solution)/shard_map/reduce_scatter | solution.py:85
Sparse Core Ops, SparseCore 0:
  32.6 25.6 reduce-scatter.3
  61.3 27.1 reduce-scatter.5
  92.6 54.3 reduce-scatter.7
where the time goes:
time: 154 us
  waiting for transfers between devices  101 us (66%)
  blocking collectives  19.1 us (12%)
  between operations  13.9 us (9%)
  matrix products  10.6 us (7%)
  other arithmetic  7.62 us (5%)
    reduce_scatter x1, waiting for transfers between devices, shards(): lax.psum_scatter(up_gradient_term, ('dp', 'tensor'), scatter_dimension=1,...  58.6 us
    reduce_scatter x1, waiting for transfers between devices, shards(): lax.psum_scatter(grad_a_term, 'dp', scatter_dimension=0, tiled=True)  23.6 us
    reduce_scatter x1, waiting for transfers between devices, shards(): lax.psum_scatter(jnp.concatenate([keyval, ranks], axis=1), 'tensor', scat...  18.8 us
    all_to_all x1, blocking collectives, shards(): lax.all_to_all(chosen.reshape(trials * tensors, select, normed_input), ('...  13.9 us
    all_gather x1, blocking collectives, shards(): every_rank = lax.all_gather(rank_gradient, 'tensor', axis=0, tiled=True)  5.19 us
    dot_general x1, matrix products, shards(): keyval = jnp.dot(rows, keyvalue_weight, preferred_element_type=jnp.float32)  4.68 us
  transfers between devices with their start and end apart: 3, of which 3 were waited for; matrix products, arithmetic and copies ran while one was open for 5% of the time, Pallas kernels for 0%

commit v1 on v0

v1 whole, which is shorter than its diff:
```python
import functools

import jax
import jax.numpy as jnp
from jax import lax
from jax.experimental import pallas as pl
from jax.experimental.pallas import tpu as pltpu
from jax.sharding import PartitionSpec as P

adapter_scale = 2.0
norm_eps = 1e-05
lanes = 128
f32 = jnp.float32
bf16 = jnp.bfloat16


def whole_vmem(count):
    return [pl.BlockSpec(memory_space=pltpu.VMEM)] * count


def params(mib):
    return pltpu.CompilerParams(vmem_limit_bytes=mib * 1024 * 1024)


def two_terms(value):
    high = value.astype(bf16)
    return high, (value - high.astype(f32)).astype(bf16)


def dot_rows(left, right):
    return lax.dot_general(left, right, (((0,), (0,)), ((), ())), preferred_element_type=f32)


def dot_last(left, right):
    return lax.dot_general(left, right, (((1,), (1,)), ((), ())), preferred_element_type=f32)


def pick_kernel(trials, ys, select, width, index_ref, rows_ref, gain_ref, grad_ref, up_ref, *rest):
    outs, chosen = rest[:-1], rest[-1]
    trial, tensor = lax.axis_index("trial"), lax.axis_index("tensor")
    tensors = 2 * ys
    y = tensor // 2
    pool, features = rows_ref.shape
    start = (trial * tensors + tensor) * select
    column = lax.broadcasted_iota(jnp.int32, (select, pool), 1)
    row = lax.broadcasted_iota(jnp.int32, (select, pool), 0)
    hots = []
    for a in range(trials):
        picked = jnp.zeros((select, pool), jnp.int32)
        for i in range(select):
            picked = jnp.where(row == i, index_ref[trial ^ a, start + i], picked)
        hots.append(jnp.where(column == picked, 1.0, 0.0).astype(bf16))
    hot = jnp.concatenate(hots, axis=0)
    square = jnp.zeros((trials * select, 1), f32)
    chunk = 1024
    for f in range(0, features, chunk):
        part = jnp.dot(hot, rows_ref[:, f : f + chunk], preferred_element_type=f32)
        chosen[:, f : f + chunk] = part
        square += jnp.sum(part * part, axis=1, keepdims=True)
    scale = lax.rsqrt(square / features + norm_eps)
    half = grad_ref.shape[2] // 2
    rank = up_ref.shape[1]
    keys = adapter_scale * dot_last(grad_ref[0, :, :half], up_ref[0, :, :half])
    values = adapter_scale * dot_last(grad_ref[0, :, half:], up_ref[0, :, half:])
    for a in range(trials):
        for b in range(ys):
            out = outs[a * ys + b]
            for core in range(2):
                for f in range(0, width, chunk):
                    at = pl.multiple_of((y ^ b) * (2 * width) + core * width + f, chunk)
                    part = chosen[a * select : (a + 1) * select, pl.ds(at, chunk)]
                    part = part * scale[a * select : (a + 1) * select] * gain_ref[:, pl.ds(at, chunk)]
                    out[core, :, f : f + chunk] = part.astype(bf16)
                if a == 0:
                    for j in range(trials // 2):
                        base = (2 * j + core) * select
                        lane = width + j * 2 * rank
                        out[core, :, lane : lane + rank] = keys[base : base + select].astype(bf16)
                        out[core, :, lane + rank : lane + 2 * rank] = values[base : base + select].astype(bf16)


def term_kernel(trials, ys, dps, select, width, *refs):
    count = trials * ys
    mine, other, down_ref = refs[:count], refs[count : 2 * count], refs[2 * count]
    rows_ref, rank_ref = refs[2 * count + 1], refs[2 * count + 2]
    terms, gradient = refs[2 * count + 3 : -1], refs[-1]
    trial, dp, tensor = lax.axis_index("trial"), lax.axis_index("dp"), lax.axis_index("tensor")
    tensors = 2 * ys
    y, core = tensor // 2, tensor % 2
    ranks = gradient.shape[1]
    local = trials * select
    for a in range(trials):
        for b in range(ys):
            for refs_at, from_core in ((mine, core), (other, 1 - core)):
                ref = refs_at[a * ys + b]
                member = 2 * (y ^ b) + from_core
                at = pl.multiple_of(((trial ^ a) * tensors + member) * select, select)
                rows_ref[pl.ds(at, select), :] = ref[core, :, :width]
                if a == 0:
                    for j in range(trials // 2):
                        for i in range(2):
                            to = pl.multiple_of(member * local + (2 * j + i) * select, select)
                            gradient[pl.ds(to, select), :] = ref[i, :, width + j * ranks : width + (j + 1) * ranks]
    rank_ref[...] = jnp.dot(rows_ref[...], down_ref[0], preferred_element_type=f32)
    block = ranks // dps
    turned = gradient[...].astype(f32).T.astype(bf16)
    chunk = 512
    for f in range(0, width, chunk):
        product = jnp.dot(turned, rows_ref[:, f : f + chunk], preferred_element_type=f32)
        terms[dps][:, f : f + chunk] = product
    full = terms[dps]
    for m in range(dps):
        at = pl.multiple_of((dp ^ m) * block, block)
        terms[m][...] = full[pl.ds(at, block), :].astype(terms[m].dtype)


def base_kernel(tensors, rows_ref, weight_ref, *refs):
    outs, total = refs[:-1], refs[-1]
    tensor = lax.axis_index("tensor")
    local = outs[0].shape[0]
    total[...] = jnp.dot(rows_ref[...], weight_ref[...], preferred_element_type=f32)
    for m in range(tensors):
        at = pl.multiple_of((tensor ^ m) * local, local)
        outs[m][...] = total[pl.ds(at, local), :].astype(outs[m].dtype)


def up_kernel(ys, dps, block, *refs):
    tensors = 2 * ys
    rank_refs, grads = refs[:ys], refs[ys : ys + tensors]
    outs, gradient, product = refs[ys + tensors : -2], refs[-2], refs[-1]
    dp, tensor = lax.axis_index("dp"), lax.axis_index("tensor")
    local, width = grads[0].shape[1], grads[0].shape[2]
    ranks = rank_refs[0].shape[1]
    ranks_sum = rank_refs[0][...]
    for ref in rank_refs[1:]:
        ranks_sum = ranks_sum + ref[...]
    high, low = two_terms(adapter_scale * ranks_sum.T)
    group = max(block, lanes)
    for m in range(tensors):
        at = pl.multiple_of((tensor ^ m) * local, local)
        for q in range(dps):
            place = pl.multiple_of((q * tensors + tensor) * block // group * group, group)
            gradient[pl.ds(at, local), q * group : (q + 1) * group] = grads[m][0, :, pl.ds(place, group)]
    values = gradient[...]
    product[...] = jnp.dot(high, values, preferred_element_type=f32) + jnp.dot(
        low, values, preferred_element_type=f32
    )
    for m in range(dps):
        for q in range(dps):

            @pl.when((dp ^ m) == q)
            def _():
                column = (q * tensors + tensor) * block
                upper = column // (width // 2)
                at = pl.multiple_of(upper * (ranks // 2), ranks // 2)
                part = product[pl.ds(at, ranks // 2), q * group : (q + 1) * group]
                if group > block:
                    inner = column % group
                    result = part[:, :block]
                    for i in range(1, group // block):
                        result = jnp.where(inner == i * block, part[:, i * block : (i + 1) * block], result)
                    part = result
                outs[m][...] = part.astype(outs[m].dtype)


def output_kernel(ys, *refs):
    tensors = 2 * ys
    rank_refs, terms, up_ref, out_ref = refs[:ys], refs[ys : ys + tensors], refs[-2], refs[-1]
    tensor = lax.axis_index("tensor")
    local, width = terms[0].shape
    half = width // 2
    rank = up_ref.shape[1]
    at = pl.multiple_of(tensor * local, local)
    ranks = rank_refs[0][pl.ds(at, local), :]
    for ref in rank_refs[1:]:
        ranks = ranks + ref[pl.ds(at, local), :]
    high, low = two_terms(adapter_scale * ranks)
    chunk = 512
    for f in range(0, width, chunk):
        side = rank * (f // half)
        up = up_ref[0, :, f : f + chunk]
        result = terms[0][:, f : f + chunk]
        for ref in terms[1:]:
            result = result + ref[:, f : f + chunk].astype(f32)
        result = result + jnp.dot(high[:, side : side + rank], up, preferred_element_type=f32)
        result = result + jnp.dot(low[:, side : side + rank], up, preferred_element_type=f32)
        out_ref[0, :, f : f + chunk] = result


def sum_kernel(count, *refs):
    for group in range(2):
        terms = refs[group * count : (group + 1) * count]
        out = refs[2 * count + group]
        result = terms[0][...]
        for ref in terms[1:]:
            result = result + ref[...].astype(f32)
        out[0] = result


def shards(
    residual_rows,
    input_norm_weight,
    trial_row_index,
    keyvalue_weight,
    adapter_down_weight,
    adapter_up_weight,
    keyvalue_gradient,
):
    trials, dps, tensors = lax.axis_size("trial"), lax.axis_size("dp"), lax.axis_size("tensor")
    ys = tensors // 2
    pool, features = residual_rows.shape
    tokens = trial_row_index.shape[1]
    select = tokens // (trials * tensors)
    local = tokens // tensors
    width, kv_width = keyvalue_weight.shape
    ranks = adapter_down_weight.shape[2]
    shape = jax.ShapeDtypeStruct

    def to_core(value):
        return lax.ppermute(value, "tensor", [(i, i ^ 1) for i in range(tensors)])

    def over(axis, size, mask, value):
        return lax.ppermute(value, axis, [(i, i ^ mask) for i in range(size)])

    extra = trials // 2 * ranks
    payload_shapes = [
        shape((2, select, width + (extra if a == 0 else 0)), bf16) for a in range(trials) for b in range(ys)
    ]
    payloads = pl.pallas_call(
        functools.partial(pick_kernel, trials, ys, select, width),
        out_shape=payload_shapes,
        in_specs=[pl.BlockSpec(memory_space=pltpu.SMEM)] + whole_vmem(4),
        out_specs=whole_vmem(len(payload_shapes)),
        scratch_shapes=[pltpu.VMEM((trials * select, features), f32)],
        compiler_params=params(32),
        name="pick",
    )(trial_row_index, residual_rows, input_norm_weight[None, :], keyvalue_gradient, adapter_up_weight)
    mine = [payloads[0]]
    for mask in range(1, trials * ys):
        a, b = mask // ys, mask % ys
        mine.append(over(("trial", "tensor"), trials * tensors, a * tensors + 2 * b, payloads[mask]))
    other = [to_core(value) for value in mine]

    block = ranks // dps
    rows, rank_term, *terms = pl.pallas_call(
        functools.partial(term_kernel, trials, ys, dps, select, width),
        out_shape=[shape((tokens, width), bf16), shape((tokens, ranks), f32), shape((block, width), f32)]
        + [shape((block, width), bf16)] * (dps - 1),
        in_specs=whole_vmem(2 * trials * ys + 1),
        out_specs=whole_vmem(2 + dps),
        scratch_shapes=[pltpu.VMEM((ranks, width), f32), pltpu.VMEM((tokens, ranks), bf16)],
        compiler_params=params(32),
        name="terms",
    )(*mine, *other, adapter_down_weight)
    down_terms = [terms[0]] + [over("dp", dps, m, terms[m]) for m in range(1, dps)]

    rank_pair = rank_term + to_core(rank_term)
    rank_sums = [rank_pair] + [over("tensor", tensors, 2 * b, rank_pair) for b in range(1, ys)]

    chunk = 512
    base_terms = pl.pallas_call(
        functools.partial(base_kernel, tensors),
        grid=(kv_width // chunk,),
        out_shape=[shape((local, kv_width), f32)] + [shape((local, kv_width), bf16)] * (tensors - 1),
        in_specs=[
            pl.BlockSpec((tokens, width), lambda n: (0, 0)),
            pl.BlockSpec((width, chunk), lambda n: (0, n)),
        ],
        out_specs=[pl.BlockSpec((local, chunk), lambda n: (0, n))] * tensors,
        scratch_shapes=[pltpu.VMEM((tokens, chunk), f32)],
        compiler_params=params(32),
        name="base",
    )(rows, keyvalue_weight)
    base_sums = [base_terms[0]] + [over("tensor", tensors, m, base_terms[m]) for m in range(1, tensors)]

    grads = [keyvalue_gradient] + [None] * (tensors - 1)
    for b in range(ys):
        if b:
            grads[2 * b] = over("tensor", tensors, 2 * b, keyvalue_gradient)
        grads[2 * b + 1] = to_core(grads[2 * b])
    column_block = kv_width // (dps * tensors)
    group = max(column_block, lanes)
    up_terms = pl.pallas_call(
        functools.partial(up_kernel, ys, dps, column_block),
        out_shape=[shape((ranks // 2, column_block), f32)] + [shape((ranks // 2, column_block), bf16)] * (dps - 1),
        in_specs=whole_vmem(ys + tensors),
        out_specs=whole_vmem(dps),
        scratch_shapes=[pltpu.VMEM((tokens, dps * group), bf16), pltpu.VMEM((ranks, dps * group), f32)],
        compiler_params=params(32),
        name="up_terms",
    )(*rank_sums, *grads)
    up_terms = [up_terms[0]] + [over("dp", dps, m, up_terms[m]) for m in range(1, dps)]

    output = pl.pallas_call(
        functools.partial(output_kernel, ys),
        out_shape=shape((1, local, kv_width), f32),
        in_specs=whole_vmem(ys + tensors + 1),
        out_specs=pl.BlockSpec(memory_space=pltpu.VMEM),
        compiler_params=params(32),
        name="output",
    )(*rank_sums, *base_sums, adapter_up_weight)
    grad_a, grad_b = pl.pallas_call(
        functools.partial(sum_kernel, dps),
        out_shape=[shape((1, block, width), f32), shape((1, ranks // 2, column_block), f32)],
        in_specs=whole_vmem(2 * dps),
        out_specs=whole_vmem(2),
        compiler_params=params(32),
        name="sums",
    )(*down_terms, *up_terms)
    return output, grad_a, grad_b


def solution(mesh):
    return jax.shard_map(
        shards,
        mesh=mesh,
        in_specs=(
            P(("trial", "dp", "tensor"), None),
            P(),
            P(None, "dp"),
            P("tensor", None),
            P("trial", "tensor", None),
            P("trial", None, None),
            P("trial", ("dp", "tensor"), None),
        ),
        out_specs=(
            P("trial", ("dp", "tensor"), None),
            P("trial", "dp", "tensor"),
            P("trial", None, ("dp", "tensor")),
        ),
        check_vma=False,
    )
```

time: 154 us -> 49.5 us (0.32)
  waiting for transfers between devices: 101 us -> 12.6 us
  starting transfers between devices: 0.12 us -> 20.3 us
  blocking collectives: 19.1 us -> 0 us
  between operations: 13.9 us -> 0.73 us
  matrix products: 10.6 us -> 0 us
  Pallas kernels: 0 us -> 7.65 us
  other arithmetic: 7.62 us -> 0.01 us
  local copies, waits for them, and re-layouts: 1.36 us -> 7.84 us
    reduce_scatter x3 -> x0, waiting for transfers between devices: 101 us -> none  [the longest x1 58.6 us: shards(): lax.psum_scatter(up_gradient_term, ('dp', 'tensor'), scatter_dimension=1,...]
    ppermute x0 -> x21, starting transfers between devices: none -> 20.3 us  [the longest x14 19.6 us: over(): return lax.ppermute(value, axis, [(i, i ^ mask) for i in range(size)])]
    all_to_all x1 -> x0, blocking collectives: 13.9 us -> none  [shards(): lax.all_to_all(chosen.reshape(trials * tensors, select, normed_input), ('...]
    ppermute x0 -> x21, waiting for transfers between devices: none -> 12.6 us  [the longest x14 12.6 us: over(): return lax.ppermute(value, axis, [(i, i ^ mask) for i in range(size)])]
    dot_general x9 -> x0, matrix products: 10.6 us -> none  [the longest x1 4.68 us: shards(): keyval = jnp.dot(rows, keyvalue_weight, preferred_element_type=jnp.float32)]
    unnamed x6 -> x14, local copies, waits for them, and re-layouts: 0.02 us -> 7.84 us
    pallas_call x0 -> x6, Pallas kernels: none -> 7.65 us  [the longest x1 2.65 us: shards(): pl.pallas_call(functools.partial(base_kernel, tensors), grid=(kv_width //...]
    all_gather x1 -> x0, blocking collectives: 5.19 us -> none  [shards(): every_rank = lax.all_gather(rank_gradient, 'tensor', axis=0, tiled=True)]
  transfers between devices with their start and end apart: 3 -> 21, of which waited for: 3 -> 6; matrix products, arithmetic and copies ran while one was open for 5% -> 0% of each run, Pallas kernels for 0% -> 11%
where the time goes in v1:
time: 49.5 us; the launch traced here: 49.1 us
  starting transfers between devices  20.3 us (41%)
  waiting for transfers between devices  12.6 us (25%)
  local copies, waits for them, and re-layouts  7.84 us (16%)
  Pallas kernels  7.65 us (15%)
  between operations  0.73 us (1%)
    ppermute x14, starting transfers between devices, over(): return lax.ppermute(value, axis, [(i, i ^ mask) for i in range(size)])  19.6 us
    ppermute x14, waiting for transfers between devices, over(): return lax.ppermute(value, axis, [(i, i ^ mask) for i in range(size)])  12.6 us
    unnamed x14, local copies, waits for them, and re-layouts  7.84 us
    pallas_call x1, Pallas kernels, shards(): pl.pallas_call(functools.partial(base_kernel, tensors), grid=(kv_width //...  2.65 us
    pallas_call x1, Pallas kernels, shards(): pl.pallas_call(functools.partial(pick_kernel, trials, ys, select, width),...  1.49 us
    pallas_call x1, Pallas kernels, shards(): pl.pallas_call(functools.partial(up_kernel, ys, dps, column_block), out_s...  1.27 us
  transfers between devices with their start and end apart: 21, of which 6 were waited for; matrix products, arithmetic and copies ran while one was open for 0% of the time, Pallas kernels for 11%

profile of v1, /device:TPU:0, one launch (start us, length us, event | category | flops | bytes accessed | tf_op | source)
XLA Modules:
  0.0 49.1 jit_solution(2277798557905851320)
XLA Ops:
  0.6 0.9 %copy-done.1 = bf16[1,64,2048]{2,1,0:T(8,128)(2,1)S(1)} copy-done((bf16[1,64,2048]{2,1,0:T(8,128)(2,1)S(1)}, bf16[1,64,2048]{2,1,0:T(8,128)(2,1)}, u32[]{:S(2)}) %copy-start.1) | copy-done | bytes 262168
  1.6 1.0 %copy-done.4 = bf16[32,8192]{1,0:T(8,128)(2,1)S(1)} copy-done((bf16[32,8192]{1,0:T(8,128)(2,1)S(1)}, bf16[32,8192]{1,0:T(8,128)(2,1)}, u32[]{:S(2)}) %copy-start.4) | copy-done | bytes 524312
  2.6 0.8 %copy-done.5 = f32[8192]{0:T(1024)S(1)} copy-done((f32[8192]{0:T(1024)S(1)}, f32[8192]{0:T(1024)}, u32[]{:S(2)}) %copy-start.5) | copy-done | bytes 32792
  3.4 0.7 %copy-done.6 = s32[2,128]{1,0:T(2,128)S(1)} copy-done((s32[2,128]{1,0:T(2,128)S(1)}, s32[2,128]{1,0:T(2,128)}, u32[]{:S(2)}) %copy-start.6) | copy-done | bytes 1048
  4.1 1.5 %pick.1 = (bf16[2,16,2176]{2,1,0:T(8,128)(2,1)S(1)}, bf16[2,16,2176]{2,1,0:T(8,128)(2,1)S(1)}, bf16[2,16,2048]{2,1,0:T(8,128)(2,1)S(1)}, bf16[2,16,2048]{2,1,0:T(8,128)(2,1)S(1)}) custom-call(s32[2,128]{1,0:T(2,128)S(1)} %copy-done.6, bf16[32,8192]{1,0:T(8,128)(2,1)S(1)} %copy-done.4, f32[1,8192]{1,0:T(1,128)S(1)} %bitcast.1, bf16[1,32,2048]{2,1,0:T(8,128)(2,1)} %refs_2_.1, ...), custom_call_target="tpu_custom_call" | custom-call | tf_op jit(solution)/shard_map/pick/pallas_call | solution.py:229
  5.6 3.0 %collective-permute-start = (bf16[2,16,2176]{2,1,0:T(8,128)(2,1)S(1)}, bf16[2,16,2176]{2,1,0:T(8,128)(2,1)S(1)}, u32[]{:S(2)}, u32[]{:S(2)}) collective-permute-start(bf16[2,16,2176]{2,1,0:T(8,128)(2,1)S(1)} %get-tuple-element.24), channel_id=1, source_target_pairs={{0,2},{1,3},{2,0},{3,1},{16,18},{17,19},{18,16},{19,17},{4,6},{5,7... | collective-permute-start | bytes 417800 | tf_op jit(solution)/shard_map/ppermute | solution.py:223
  8.6 1.5 %collective-permute-start.1 = (bf16[2,16,2048]{2,1,0:T(8,128)(2,1)S(1)}, bf16[2,16,2048]{2,1,0:T(8,128)(2,1)S(1)}, u32[]{:S(2)}, u32[]{:S(2)}) collective-permute-start(bf16[2,16,2048]{2,1,0:T(8,128)(2,1)S(1)} %get-tuple-element.25), channel_id=1, source_target_pairs={{0,16},{1,17},{2,18},{3,19},{16,0},{17,1},{18,2},{19,3},{4,20},{5,... | collective-permute-start | bytes 393224 | tf_op jit(solution)/shard_map/ppermute | solution.py:223
  10.1 1.9 %collective-permute-start.16 = (bf16[1,32,2048]{2,1,0:T(8,128)(2,1)}, bf16[1,32,2048]{2,1,0:T(8,128)(2,1)S(1)}, u32[]{:S(2)}, u32[]{:S(2)}) collective-permute-start(bf16[1,32,2048]{2,1,0:T(8,128)(2,1)} %refs_2_.1), channel_id=1, source_target_pairs={{0,2},{1,3},{2,0},{3,1},{4,6},{5,7},{6,4},{7,5},{8,10},{9,11},{10,... | collective-permute-start | bytes 393224 | tf_op jit(solution)/shard_map/ppermute | solution.py:223
  12.1 0.2 collective-permute-done.refs_1_
  12.3 2.6 %collective-permute-done.1.refs_2_ = bf16[2,16,2048]{2,1,0:T(8,128)(2,1)S(1)} collective-permute-done((bf16[2,16,2048]{2,1,0:T(8,128)(2,1)S(1)}, bf16[2,16,2048]{2,1,0:T(8,128)(2,1)S(1)}, u32[]{:S(2)}, u32[]{:S(2)}) %collective-permute-start.1) | collective-permute-done | bytes 131104 | tf_op jit(solution)/shard_map/ppermute | solution.py:223
  15.0 1.3 %collective-permute-done.2.refs_3_ = bf16[2,16,2048]{2,1,0:T(8,128)(2,1)S(1)} collective-permute-done((bf16[2,16,2048]{2,1,0:T(8,128)(2,1)S(1)}, bf16[2,16,2048]{2,1,0:T(8,128)(2,1)S(1)}, u32[]{:S(2)}, u32[]{:S(2)}) %collective-permute-start.2) | collective-permute-done | bytes 131104 | tf_op jit(solution)/shard_map/ppermute | solution.py:223
  16.3 2.6 %collective-permute-done.16.refs_4_ = bf16[1,32,2048]{2,1,0:T(8,128)(2,1)S(1)} collective-permute-done((bf16[1,32,2048]{2,1,0:T(8,128)(2,1)}, bf16[1,32,2048]{2,1,0:T(8,128)(2,1)S(1)}, u32[]{:S(2)}, u32[]{:S(2)}) %collective-permute-start.16) | collective-permute-done | bytes 131104 | tf_op jit(solution)/shard_map/ppermute | solution.py:223
  18.9 0.5 %collective-permute-start.17 = (bf16[1,32,2048]{2,1,0:T(8,128)(2,1)S(1)}, bf16[1,32,2048]{2,1,0:T(8,128)(2,1)S(1)}, u32[]{:S(2)}, u32[]{:S(2)}) collective-permute-start(bf16[1,32,2048]{2,1,0:T(8,128)(2,1)S(1)} %collective-permute-done.16.refs_4_), channel_id=1, source_target_pairs={{0,1},{1,0},{2,3},{3,2},{4,5},{5,4},{6,7},{7,6},{8,9},{9,8},{10,11... | collective-permute-start | bytes 393224 | tf_op jit(solution)/shard_map/ppermute | solution.py:220
  19.4 1.0 %copy-done.3 = bf16[1,2048,128]{2,1,0:T(8,128)(2,1)S(1)} copy-done((bf16[1,2048,128]{2,1,0:T(8,128)(2,1)S(1)}, bf16[1,2048,128]{2,1,0:T(8,128)(2,1)}, u32[]{:S(2)}) %copy-start.3) | copy-done | bytes 524312
  20.5 0.5 %terms.1 = (bf16[128,2048]{1,0:T(8,128)(2,1)S(1)}, f32[128,128]{1,0:T(8,128)S(1)}, f32[32,2048]{1,0:T(8,128)S(1)}, bf16[32,2048]{1,0:T(8,128)(2,1)S(1)}, bf16[32...) custom-call(bf16[2,16,2176]{2,1,0:T(8,128)(2,1)S(1)} %get-tuple-element.23.refs_0_, ...), custom_call_target="tpu_custom_call" | custom-call | tf_op jit(solution)/shard_map/terms/pallas_call | solution.py:245
  21.1 1.7 %collective-permute-start.12 = (bf16[32,2048]{1,0:T(8,128)(2,1)S(1)}, bf16[32,2048]{1,0:T(8,128)(2,1)S(1)}, u32[]{:S(2)}, u32[]{:S(2)}) collective-permute-start(bf16[32,2048]{1,0:T(8,128)(2,1)S(1)} %get-tuple-element.34), channel_id=1, source_target_pairs={{0,4},{4,0},{8,12},{12,8},{1,5},{5,1},{9,13},{13,9},{2,6},{6,2},{1... | collective-permute-start | bytes 393224 | tf_op jit(solution)/shard_map/ppermute | solution.py:223
  22.8 1.2 %collective-permute-start.8 = (f32[128,128]{1,0:T(8,128)S(1)}, f32[128,128]{1,0:T(8,128)S(1)}, u32[]{:S(2)}, u32[]{:S(2)}) collective-permute-start(f32[128,128]{1,0:T(8,128)S(1)} %add.3.refs_0_), channel_id=1, source_target_pairs={{0,2},{1,3},{2,0},{3,1},{4,6},{5,7},{6,4},{7,5},{8,10},{9,11},{10,... | collective-permute-start | bytes 196616 | tf_op jit(solution)/shard_map/ppermute | solution.py:223
  24.0 3.4 %copy-done = bf16[2048,2048]{1,0:T(8,128)(2,1)S(1)} copy-done((bf16[2048,2048]{1,0:T(8,128)(2,1)S(1)}, bf16[2048,2048]{1,0:T(8,128)(2,1)}, u32[]{:S(2)}) %copy-start) | copy-done | bytes 8388632
  27.4 2.7 %base.1 = (f32[32,2048]{1,0:T(8,128)S(1)}, bf16[32,2048]{1,0:T(8,128)(2,1)S(1)}, bf16[32,2048]{1,0:T(8,128)(2,1)S(1)}, bf16[32,2048]{1,0:T(8,128)(2,1)S(1)}) custom-call(bf16[128,2048]{1,0:T(8,128)(2,1)S(1)} %get-tuple-element.28.rows_ref, bf16[2048,2048]{1,0:T(8,128)(2,1)S(1)} %copy-done), custom_call_target="tpu_custom_call" | custom-call | tf_op jit(solution)/shard_map/base/pallas_call | solution.py:261
  30.0 1.0 %collective-permute-start.10 = (bf16[32,2048]{1,0:T(8,128)(2,1)S(1)}, bf16[32,2048]{1,0:T(8,128)(2,1)S(1)}, u32[]{:S(2)}, u32[]{:S(2)}) collective-permute-start(bf16[32,2048]{1,0:T(8,128)(2,1)S(1)} %get-tuple-element.31), channel_id=1, source_target_pairs={{0,2},{1,3},{2,0},{3,1},{4,6},{5,7},{6,4},{7,5},{8,10},{9,11},{10,... | collective-permute-start | bytes 393224 | tf_op jit(solution)/shard_map/ppermute | solution.py:223
  31.0 0.3 collective-permute-start.11
  31.4 0.9 %collective-permute-start.9 = (bf16[32,2048]{1,0:T(8,128)(2,1)S(1)}, bf16[32,2048]{1,0:T(8,128)(2,1)S(1)}, u32[]{:S(2)}, u32[]{:S(2)}) collective-permute-start(bf16[32,2048]{1,0:T(8,128)(2,1)S(1)} %get-tuple-element.30), channel_id=1, source_target_pairs={{0,1},{1,0},{2,3},{3,2},{4,5},{5,4},{6,7},{7,6},{8,9},{9,8},{10,11... | collective-permute-start | bytes 393224 | tf_op jit(solution)/shard_map/ppermute | solution.py:223
  32.3 2.6 %collective-permute-start.13 = (bf16[32,2048]{1,0:T(8,128)(2,1)S(1)}, bf16[32,2048]{1,0:T(8,128)(2,1)S(1)}, u32[]{:S(2)}, u32[]{:S(2)}) collective-permute-start(bf16[32,2048]{1,0:T(8,128)(2,1)S(1)} %get-tuple-element.35), channel_id=1, source_target_pairs={{0,8},{4,12},{8,0},{12,4},{1,9},{5,13},{9,1},{13,5},{2,10},{6,14},... | collective-permute-start | bytes 393224 | tf_op jit(solution)/shard_map/ppermute | solution.py:223
  34.9 0.9 %collective-permute-start.14 = (bf16[32,2048]{1,0:T(8,128)(2,1)S(1)}, bf16[32,2048]{1,0:T(8,128)(2,1)S(1)}, u32[]{:S(2)}, u32[]{:S(2)}) collective-permute-start(bf16[32,2048]{1,0:T(8,128)(2,1)S(1)} %get-tuple-element.36), channel_id=1, source_target_pairs={{0,12},{4,8},{8,4},{12,0},{1,13},{5,9},{9,5},{13,1},{2,14},{6,10},... | collective-permute-start | bytes 393224 | tf_op jit(solution)/shard_map/ppermute | solution.py:223
  35.8 1.3 %up_terms.1 = (f32[64,128]{1,0:T(8,128)S(1)}, bf16[64,128]{1,0:T(8,128)(2,1)S(1)}, bf16[64,128]{1,0:T(8,128)(2,1)S(1)}, bf16[64,128]{1,0:T(8,128)(2,1)S(1)}) custom-call(f32[128,128]{1,0:T(8,128)S(1)} %add.3.refs_0_, f32[128,128]{1,0:T(8,128)S(1)} %collective-permute-done.8.refs_1_, bf16[1,32,2048]{2,1,0:T(8,128)(2,1)} %refs_2_.1, ...), custom_call_target="tpu_custom_call" | custom-call | tf_op jit(solution)/shard_map/up_terms/pallas_call | solution.py:283
  37.1 0.6 %collective-permute-start.18 = (bf16[64,128]{1,0:T(8,128)(2,1)S(1)}, bf16[64,128]{1,0:T(8,128)(2,1)S(1)}, u32[]{:S(2)}, u32[]{:S(2)}) collective-permute-start(bf16[64,128]{1,0:T(8,128)(2,1)S(1)} %get-tuple-element.38), channel_id=1, source_target_pairs={{0,4},{4,0},{8,12},{12,8},{1,5},{5,1},{9,13},{13,9},{2,6},{6,2},{1... | collective-permute-start | bytes 49160 | tf_op jit(solution)/shard_map/ppermute | solution.py:223
  37.7 3.0 %collective-permute-start.19 = (bf16[64,128]{1,0:T(8,128)(2,1)S(1)}, bf16[64,128]{1,0:T(8,128)(2,1)S(1)}, u32[]{:S(2)}, u32[]{:S(2)}) collective-permute-start(bf16[64,128]{1,0:T(8,128)(2,1)S(1)} %get-tuple-element.39), channel_id=1, source_target_pairs={{0,8},{4,12},{8,0},{12,4},{1,9},{5,13},{9,1},{13,5},{2,10},{6,14},... | collective-permute-start | bytes 49160 | tf_op jit(solution)/shard_map/ppermute | solution.py:223
  40.6 0.9 %collective-permute-start.20 = (bf16[64,128]{1,0:T(8,128)(2,1)S(1)}, bf16[64,128]{1,0:T(8,128)(2,1)S(1)}, u32[]{:S(2)}, u32[]{:S(2)}) collective-permute-start(bf16[64,128]{1,0:T(8,128)(2,1)S(1)} %get-tuple-element.40), channel_id=1, source_target_pairs={{0,12},{4,8},{8,4},{12,0},{1,13},{5,9},{9,5},{13,1},{2,14},{6,10},... | collective-permute-start | bytes 49160 | tf_op jit(solution)/shard_map/ppermute | solution.py:223
  41.6 0.9 %output.1 = f32[1,32,2048]{2,1,0:T(8,128)} custom-call(f32[128,128]{1,0:T(8,128)S(1)} %add.3.refs_0_, f32[128,128]{1,0:T(8,128)S(1)} %collective-permute-done.8.refs_1_, f32[32,2048]{1,0:T(8,128)S(1)} %get-tuple-element.29.refs_2_, bf16[32,2048]{1,0:T(8,128)(2,1)S(1)} %collective-permute-done.9.refs_3_, ...), custom_call_target="tpu_custom_call" | custom-call | tf_op jit(solution)/shard_map/output/pallas_call | solution.py:294
  42.5 3.0 %collective-permute-done.13.refs_2_ = bf16[32,2048]{1,0:T(8,128)(2,1)S(1)} collective-permute-done((bf16[32,2048]{1,0:T(8,128)(2,1)S(1)}, bf16[32,2048]{1,0:T(8,128)(2,1)S(1)}, u32[]{:S(2)}, u32[]{:S(2)}) %collective-permute-start.13) | collective-permute-done | bytes 131104 | tf_op jit(solution)/shard_map/ppermute | solution.py:223
  45.5 2.8 %collective-permute-done.19.refs_6_ = bf16[64,128]{1,0:T(8,128)(2,1)S(1)} collective-permute-done((bf16[64,128]{1,0:T(8,128)(2,1)S(1)}, bf16[64,128]{1,0:T(8,128)(2,1)S(1)}, u32[]{:S(2)}, u32[]{:S(2)}) %collective-permute-start.19) | collective-permute-done | bytes 16416 | tf_op jit(solution)/shard_map/ppermute | solution.py:223
  48.3 0.8 %sums.1 = (f32[1,32,2048]{2,1,0:T(8,128)}, f32[1,64,128]{2,1,0:T(8,128)}) custom-call(f32[32,2048]{1,0:T(8,128)S(1)} %get-tuple-element.33.refs_0_, bf16[32,2048]{1,0:T(8,128)(2,1)S(1)} %collective-permute-done.12.refs_1_, bf16[32,2048]{1,0:T(8,128)(2,1)S(1)} %collective-permute-done.13.refs_2_, bf16[32,2048]{1,0:T(8,128)(2,1)S(1)} %collective-permute-done.14.refs_3_, ...), custom_call_target="tpu_custom_call" | custom-call | tf_op jit(solution)/shard_map/sums/pallas_call | solution.py:302
  (31 shorter events, 0.3 us)
Async XLA Ops:
  0.6 1.0 %copy-start.1 = (bf16[1,64,2048]{2,1,0:T(8,128)(2,1)S(1)}, bf16[1,64,2048]{2,1,0:T(8,128)(2,1)}, u32[]{:S(2)}) copy-start(bf16[1,64,2048]{2,1,0:T(8,128)(2,1)} %refs_6_.1) | copy-start | bytes 786436
  1.6 1.0 %copy-start.4 = (bf16[32,8192]{1,0:T(8,128)(2,1)S(1)}, bf16[32,8192]{1,0:T(8,128)(2,1)}, u32[]{:S(2)}) copy-start(bf16[32,8192]{1,0:T(8,128)(2,1)} %rows_ref.1) | copy-start | bytes 1572868
  2.6 0.8 %copy-start.5 = (f32[8192]{0:T(1024)S(1)}, f32[8192]{0:T(1024)}, u32[]{:S(2)}) copy-start(f32[8192]{0:T(1024)} %param.8) | copy-start | bytes 98308
  3.4 0.7 %copy-start.6 = (s32[2,128]{1,0:T(2,128)S(1)}, s32[2,128]{1,0:T(2,128)}, u32[]{:S(2)}) copy-start(s32[2,128]{1,0:T(2,128)} %index_ref.1) | copy-start | bytes 3076
  4.1 37.5 %copy-start.2 = (bf16[1,64,2048]{2,1,0:T(8,128)(2,1)S(1)}, bf16[1,64,2048]{2,1,0:T(8,128)(2,1)}, u32[]{:S(2)}) copy-start(bf16[1,64,2048]{2,1,0:T(8,128)(2,1)} %refs_6_.1) | copy-start | bytes 786436
  5.6 6.7 %collective-permute-start = (bf16[2,16,2176]{2,1,0:T(8,128)(2,1)S(1)}, bf16[2,16,2176]{2,1,0:T(8,128)(2,1)S(1)}, u32[]{:S(2)}, u32[]{:S(2)}) collective-permute-start(bf16[2,16,2176]{2,1,0:T(8,128)(2,1)S(1)} %get-tuple-element.24), channel_id=1, source_target_pairs={{0,2},{1,3},{2,0},{3,1},{16,18},{17,19},{18,16},{19,17},{4,6},{5,7... | collective-permute-start | bytes 417800 | tf_op jit(solution)/shard_map/ppermute | solution.py:223
  8.6 6.4 %collective-permute-start.1 = (bf16[2,16,2048]{2,1,0:T(8,128)(2,1)S(1)}, bf16[2,16,2048]{2,1,0:T(8,128)(2,1)S(1)}, u32[]{:S(2)}, u32[]{:S(2)}) collective-permute-start(bf16[2,16,2048]{2,1,0:T(8,128)(2,1)S(1)} %get-tuple-element.25), channel_id=1, source_target_pairs={{0,16},{1,17},{2,18},{3,19},{16,0},{17,1},{18,2},{19,3},{4,20},{5,... | collective-permute-start | bytes 393224 | tf_op jit(solution)/shard_map/ppermute | solution.py:223
  10.1 6.2 %collective-permute-start.2 = (bf16[2,16,2048]{2,1,0:T(8,128)(2,1)S(1)}, bf16[2,16,2048]{2,1,0:T(8,128)(2,1)S(1)}, u32[]{:S(2)}, u32[]{:S(2)}) collective-permute-start(bf16[2,16,2048]{2,1,0:T(8,128)(2,1)S(1)} %get-tuple-element.26), channel_id=1, source_target_pairs={{0,18},{1,19},{2,16},{3,17},{16,2},{17,3},{18,0},{19,1},{4,22},{5,... | collective-permute-start | bytes 393224 | tf_op jit(solution)/shard_map/ppermute | solution.py:223
  10.1 8.8 %collective-permute-start.3 = (bf16[2,16,2176]{2,1,0:T(8,128)(2,1)S(1)}, bf16[2,16,2176]{2,1,0:T(8,128)(2,1)S(1)}, u32[]{:S(2)}, u32[]{:S(2)}) collective-permute-start(bf16[2,16,2176]{2,1,0:T(8,128)(2,1)S(1)} %get-tuple-element.23.refs_0_), channel_id=1, source_target_pairs={{0,1},{1,0},{2,3},{3,2},{4,5},{5,4},{6,7},{7,6},{8,9},{9,8},{10,11... | collective-permute-start | bytes 417800 | tf_op jit(solution)/shard_map/ppermute | solution.py:220
  10.1 8.7 %collective-permute-start.16 = (bf16[1,32,2048]{2,1,0:T(8,128)(2,1)}, bf16[1,32,2048]{2,1,0:T(8,128)(2,1)S(1)}, u32[]{:S(2)}, u32[]{:S(2)}) collective-permute-start(bf16[1,32,2048]{2,1,0:T(8,128)(2,1)} %refs_2_.1), channel_id=1, source_target_pairs={{0,2},{1,3},{2,0},{3,1},{4,6},{5,7},{6,4},{7,5},{8,10},{9,11},{10,... | collective-permute-start | bytes 393224 | tf_op jit(solution)/shard_map/ppermute | solution.py:223
  12.3 7.1 %collective-permute-start.4 = (bf16[2,16,2176]{2,1,0:T(8,128)(2,1)S(1)}, bf16[2,16,2176]{2,1,0:T(8,128)(2,1)S(1)}, u32[]{:S(2)}, u32[]{:S(2)}) collective-permute-start(bf16[2,16,2176]{2,1,0:T(8,128)(2,1)S(1)} %collective-permute-done.refs_1_), channel_id=1, source_target_pairs={{0,1},{1,0},{2,3},{3,2},{4,5},{5,4},{6,7},{7,6},{8,9},{9,8},{10,11... | collective-permute-start | bytes 417800 | tf_op jit(solution)/shard_map/ppermute | solution.py:220
  15.0 4.4 %collective-permute-start.5 = (bf16[2,16,2048]{2,1,0:T(8,128)(2,1)S(1)}, bf16[2,16,2048]{2,1,0:T(8,128)(2,1)S(1)}, u32[]{:S(2)}, u32[]{:S(2)}) collective-permute-start(bf16[2,16,2048]{2,1,0:T(8,128)(2,1)S(1)} %collective-permute-done.1.refs_2_), channel_id=1, source_target_pairs={{0,1},{1,0},{2,3},{3,2},{4,5},{5,4},{6,7},{7,6},{8,9},{9,8},{10,11... | collective-permute-start | bytes 393224 | tf_op jit(solution)/shard_map/ppermute | solution.py:220
  16.3 3.1 %collective-permute-start.6 = (bf16[2,16,2048]{2,1,0:T(8,128)(2,1)S(1)}, bf16[2,16,2048]{2,1,0:T(8,128)(2,1)S(1)}, u32[]{:S(2)}, u32[]{:S(2)}) collective-permute-start(bf16[2,16,2048]{2,1,0:T(8,128)(2,1)S(1)} %collective-permute-done.2.refs_3_), channel_id=1, source_target_pairs={{0,1},{1,0},{2,3},{3,2},{4,5},{5,4},{6,7},{7,6},{8,9},{9,8},{10,11... | collective-permute-start | bytes 393224 | tf_op jit(solution)/shard_map/ppermute | solution.py:220
  18.9 12.1 %collective-permute-start.15 = (bf16[1,32,2048]{2,1,0:T(8,128)(2,1)}, bf16[1,32,2048]{2,1,0:T(8,128)(2,1)S(1)}, u32[]{:S(2)}, u32[]{:S(2)}) collective-permute-start(bf16[1,32,2048]{2,1,0:T(8,128)(2,1)} %refs_2_.1), channel_id=1, source_target_pairs={{0,1},{1,0},{2,3},{3,2},{4,5},{5,4},{6,7},{7,6},{8,9},{9,8},{10,11... | collective-permute-start | bytes 393224 | tf_op jit(solution)/shard_map/ppermute | solution.py:220
  18.9 12.5 %collective-permute-start.17 = (bf16[1,32,2048]{2,1,0:T(8,128)(2,1)S(1)}, bf16[1,32,2048]{2,1,0:T(8,128)(2,1)S(1)}, u32[]{:S(2)}, u32[]{:S(2)}) collective-permute-start(bf16[1,32,2048]{2,1,0:T(8,128)(2,1)S(1)} %collective-permute-done.16.refs_4_), channel_id=1, source_target_pairs={{0,1},{1,0},{2,3},{3,2},{4,5},{5,4},{6,7},{7,6},{8,9},{9,8},{10,11... | collective-permute-start | bytes 393224 | tf_op jit(solution)/shard_map/ppermute | solution.py:220
  19.4 1.0 %copy-start.3 = (bf16[1,2048,128]{2,1,0:T(8,128)(2,1)S(1)}, bf16[1,2048,128]{2,1,0:T(8,128)(2,1)}, u32[]{:S(2)}) copy-start(bf16[1,2048,128]{2,1,0:T(8,128)(2,1)} %refs_8_.1) | copy-start | bytes 1572868
  21.0 1.8 %collective-permute-start.7 = (f32[128,128]{1,0:T(8,128)S(1)}, f32[128,128]{1,0:T(8,128)S(1)}, u32[]{:S(2)}, u32[]{:S(2)}) collective-permute-start(f32[128,128]{1,0:T(8,128)S(1)} %get-tuple-element.27), channel_id=1, source_target_pairs={{0,1},{1,0},{2,3},{3,2},{4,5},{5,4},{6,7},{7,6},{8,9},{9,8},{10,11... | collective-permute-start | bytes 196616 | tf_op jit(solution)/shard_map/ppermute | solution.py:220
  21.1 13.8 %collective-permute-start.12 = (bf16[32,2048]{1,0:T(8,128)(2,1)S(1)}, bf16[32,2048]{1,0:T(8,128)(2,1)S(1)}, u32[]{:S(2)}, u32[]{:S(2)}) collective-permute-start(bf16[32,2048]{1,0:T(8,128)(2,1)S(1)} %get-tuple-element.34), channel_id=1, source_target_pairs={{0,4},{4,0},{8,12},{12,8},{1,5},{5,1},{9,13},{13,9},{2,6},{6,2},{1... | collective-permute-start | bytes 393224 | tf_op jit(solution)/shard_map/ppermute | solution.py:223
  22.8 9.5 %collective-permute-start.8 = (f32[128,128]{1,0:T(8,128)S(1)}, f32[128,128]{1,0:T(8,128)S(1)}, u32[]{:S(2)}, u32[]{:S(2)}) collective-permute-start(f32[128,128]{1,0:T(8,128)S(1)} %add.3.refs_0_), channel_id=1, source_target_pairs={{0,2},{1,3},{2,0},{3,1},{4,6},{5,7},{6,4},{7,5},{8,10},{9,11},{10,... | collective-permute-start | bytes 196616 | tf_op jit(solution)/shard_map/ppermute | solution.py:223
  24.0 3.4 %copy-start = (bf16[2048,2048]{1,0:T(8,128)(2,1)S(1)}, bf16[2048,2048]{1,0:T(8,128)(2,1)}, u32[]{:S(2)}) copy-start(bf16[2048,2048]{1,0:T(8,128)(2,1)} %weight_ref.1) | copy-start | bytes 25165828
  30.0 7.0 %collective-permute-start.10 = (bf16[32,2048]{1,0:T(8,128)(2,1)S(1)}, bf16[32,2048]{1,0:T(8,128)(2,1)S(1)}, u32[]{:S(2)}, u32[]{:S(2)}) collective-permute-start(bf16[32,2048]{1,0:T(8,128)(2,1)S(1)} %get-tuple-element.31), channel_id=1, source_target_pairs={{0,2},{1,3},{2,0},{3,1},{4,6},{5,7},{6,4},{7,5},{8,10},{9,11},{10,... | collective-permute-start | bytes 393224 | tf_op jit(solution)/shard_map/ppermute | solution.py:223
  31.0 6.6 %collective-permute-start.11 = (bf16[32,2048]{1,0:T(8,128)(2,1)S(1)}, bf16[32,2048]{1,0:T(8,128)(2,1)S(1)}, u32[]{:S(2)}, u32[]{:S(2)}) collective-permute-start(bf16[32,2048]{1,0:T(8,128)(2,1)S(1)} %get-tuple-element.32), channel_id=1, source_target_pairs={{0,3},{1,2},{2,1},{3,0},{4,7},{5,6},{6,5},{7,4},{8,11},{9,10},{10,... | collective-permute-start | bytes 393224 | tf_op jit(solution)/shard_map/ppermute | solution.py:223
  31.4 9.3 %collective-permute-start.9 = (bf16[32,2048]{1,0:T(8,128)(2,1)S(1)}, bf16[32,2048]{1,0:T(8,128)(2,1)S(1)}, u32[]{:S(2)}, u32[]{:S(2)}) collective-permute-start(bf16[32,2048]{1,0:T(8,128)(2,1)S(1)} %get-tuple-element.30), channel_id=1, source_target_pairs={{0,1},{1,0},{2,3},{3,2},{4,5},{5,4},{6,7},{7,6},{8,9},{9,8},{10,11... | collective-permute-start | bytes 393224 | tf_op jit(solution)/shard_map/ppermute | solution.py:223
  32.3 13.3 %collective-permute-start.13 = (bf16[32,2048]{1,0:T(8,128)(2,1)S(1)}, bf16[32,2048]{1,0:T(8,128)(2,1)S(1)}, u32[]{:S(2)}, u32[]{:S(2)}) collective-permute-start(bf16[32,2048]{1,0:T(8,128)(2,1)S(1)} %get-tuple-element.35), channel_id=1, source_target_pairs={{0,8},{4,12},{8,0},{12,4},{1,9},{5,13},{9,1},{13,5},{2,10},{6,14},... | collective-permute-start | bytes 393224 | tf_op jit(solution)/shard_map/ppermute | solution.py:223
  34.9 10.6 %collective-permute-start.14 = (bf16[32,2048]{1,0:T(8,128)(2,1)S(1)}, bf16[32,2048]{1,0:T(8,128)(2,1)S(1)}, u32[]{:S(2)}, u32[]{:S(2)}) collective-permute-start(bf16[32,2048]{1,0:T(8,128)(2,1)S(1)} %get-tuple-element.36), channel_id=1, source_target_pairs={{0,12},{4,8},{8,4},{12,0},{1,13},{5,9},{9,5},{13,1},{2,14},{6,10},... | collective-permute-start | bytes 393224 | tf_op jit(solution)/shard_map/ppermute | solution.py:223
  37.1 8.4 %collective-permute-start.18 = (bf16[64,128]{1,0:T(8,128)(2,1)S(1)}, bf16[64,128]{1,0:T(8,128)(2,1)S(1)}, u32[]{:S(2)}, u32[]{:S(2)}) collective-permute-start(bf16[64,128]{1,0:T(8,128)(2,1)S(1)} %get-tuple-element.38), channel_id=1, source_target_pairs={{0,4},{4,0},{8,12},{12,8},{1,5},{5,1},{9,13},{13,9},{2,6},{6,2},{1... | collective-permute-start | bytes 49160 | tf_op jit(solution)/shard_map/ppermute | solution.py:223
  37.7 10.7 %collective-permute-start.19 = (bf16[64,128]{1,0:T(8,128)(2,1)S(1)}, bf16[64,128]{1,0:T(8,128)(2,1)S(1)}, u32[]{:S(2)}, u32[]{:S(2)}) collective-permute-start(bf16[64,128]{1,0:T(8,128)(2,1)S(1)} %get-tuple-element.39), channel_id=1, source_target_pairs={{0,8},{4,12},{8,0},{12,4},{1,9},{5,13},{9,1},{13,5},{2,10},{6,14},... | collective-permute-start | bytes 49160 | tf_op jit(solution)/shard_map/ppermute | solution.py:223
  40.6 7.7 %collective-permute-start.20 = (bf16[64,128]{1,0:T(8,128)(2,1)S(1)}, bf16[64,128]{1,0:T(8,128)(2,1)S(1)}, u32[]{:S(2)}, u32[]{:S(2)}) collective-permute-start(bf16[64,128]{1,0:T(8,128)(2,1)S(1)} %get-tuple-element.40), channel_id=1, source_target_pairs={{0,12},{4,8},{8,4},{12,0},{1,13},{5,9},{9,5},{13,1},{2,14},{6,10},... | collective-permute-start | bytes 49160 | tf_op jit(solution)/shard_map/ppermute | solution.py:223

commit v2 on v1

v2 whole, which is shorter than its diff:
```python
import functools

import jax
import jax.numpy as jnp
from jax import lax
from jax.experimental import pallas as pl
from jax.experimental.pallas import tpu as pltpu
from jax.sharding import PartitionSpec as P

adapter_scale = 2.0
norm_eps = 1e-05
lanes = 128
f32 = jnp.float32
bf16 = jnp.bfloat16


def whole_vmem(count):
    return [pl.BlockSpec(memory_space=pltpu.VMEM)] * count


def params(mib):
    return pltpu.CompilerParams(vmem_limit_bytes=mib * 1024 * 1024)


def in_hbm(count):
    return [pl.BlockSpec(memory_space=pltpu.HBM)] * count


def cost(flops, moved):
    return pl.CostEstimate(flops=flops, bytes_accessed=moved, transcendentals=0)


def two_terms(value):
    high = value.astype(bf16)
    return high, (value - high.astype(f32)).astype(bf16)


def dot_rows(left, right):
    return lax.dot_general(left, right, (((0,), (0,)), ((), ())), preferred_element_type=f32)


def dot_last(left, right):
    return lax.dot_general(left, right, (((1,), (1,)), ((), ())), preferred_element_type=f32)


def pick_kernel(trials, ys, dps, select, width, column_block, index_hbm, rows_hbm, gain_hbm, grad_hbm, up_hbm, down_hbm, *rest):
    outs, rest = rest[: trials * ys], rest[trials * ys :]
    downs = rest[:2]
    index_ref, rows_ref, gain_ref, grad_ref, up_ref, chosen, sems = rest[2:]
    copies = [
        pltpu.make_async_copy(source, target, sems.at[i])
        for i, (source, target) in enumerate(
            (
                (index_hbm, index_ref),
                (rows_hbm, rows_ref),
                (gain_hbm, gain_ref),
                (grad_hbm, grad_ref),
                (up_hbm, up_ref),
                (down_hbm.at[:, : width // 2], downs[0]),
                (down_hbm.at[:, width // 2 :], downs[1]),
            )
        )
    ]
    for copy in copies:
        copy.start()
    trial, tensor = lax.axis_index("trial"), lax.axis_index("tensor")
    tensors = 2 * ys
    y = tensor // 2
    pool, features = rows_ref.shape
    start = (trial * tensors + tensor) * select
    column = lax.broadcasted_iota(jnp.int32, (select, pool), 1)
    row = lax.broadcasted_iota(jnp.int32, (select, pool), 0)
    hots = []
    copies[0].wait()
    for a in range(trials):
        picked = jnp.zeros((select, pool), jnp.int32)
        for i in range(select):
            picked = jnp.where(row == i, index_ref[trial ^ a, start + i], picked)
        hots.append(jnp.where(column == picked, 1.0, 0.0).astype(bf16))
    hot = jnp.concatenate(hots, axis=0)
    square = jnp.zeros((trials * select, 1), f32)
    chunk = 1024
    copies[1].wait()
    for f in range(0, features, chunk):
        part = jnp.dot(hot, rows_ref[:, f : f + chunk], preferred_element_type=f32)
        chosen[:, f : f + chunk] = part
        square += jnp.sum(part * part, axis=1, keepdims=True)
    scale = lax.rsqrt(square / features + norm_eps)
    half = grad_ref.shape[2] // 2
    rank = up_ref.shape[1]
    for copy in copies[2:5]:
        copy.wait()
    keys = adapter_scale * dot_last(grad_ref[0, :, :half], up_ref[0, :, :half])
    values = adapter_scale * dot_last(grad_ref[0, :, half:], up_ref[0, :, half:])
    for a in range(trials):
        for b in range(ys):
            out = outs[a * ys + b]
            for core in range(2):
                for f in range(0, width, chunk):
                    at = pl.multiple_of((y ^ b) * (2 * width) + core * width + f, chunk)
                    part = chosen[a * select : (a + 1) * select, pl.ds(at, chunk)]
                    part = part * scale[a * select : (a + 1) * select] * gain_ref[:, pl.ds(at, chunk)]
                    out[core, :, f : f + chunk] = part.astype(bf16)
    group = max(column_block, lanes)
    for b in range(ys):
        for j in range(trials // 2):
            for core in range(2):
                token = (2 * j + core) * select
                at = slice(token, token + select)
                for i in range(2):
                    for q in range(dps):
                        member = 2 * (y ^ b) + i
                        place = pl.multiple_of((q * tensors + member) * column_block // group * group, group)
                        lane = width + ((2 * j + i) * dps + q) * group
                        outs[b][core, :, lane : lane + group] = grad_ref[0, at, pl.ds(place, group)]
                lane = width + trials * dps * group + j * 2 * rank
                outs[b][core, :, lane : lane + rank] = keys[at].astype(bf16)
                outs[b][core, :, lane + rank : lane + 2 * rank] = values[at].astype(bf16)
    copies[5].wait()
    copies[6].wait()


def term_kernel(trials, ys, dps, select, width, *refs):
    count = trials * ys
    far = dps // 2 - 1
    mine, other, refs = refs[:count], refs[count : 2 * count], refs[2 * count :]
    downs, refs = refs[:4], refs[4:]
    rows_ref, turned_ref, rank_ref = refs[:3]
    terms = refs[3 : 3 + far]
    pair, gradient, turned = refs[3 + far :]
    trial, dp, tensor = lax.axis_index("trial"), lax.axis_index("dp"), lax.axis_index("tensor")
    tensors = 2 * ys
    y, core = tensor // 2, tensor % 2
    ranks = gradient.shape[1]
    local = trials * select
    for a in range(trials):
        for b in range(ys):
            for refs_at, from_core in ((mine, core), (other, 1 - core)):
                ref = refs_at[a * ys + b]
                member = 2 * (y ^ b) + from_core
                at = pl.multiple_of(((trial ^ a) * tensors + member) * select, select)
                for i in range(2):
                    pair[i, pl.ds(at, select), :] = ref[i, :, :width]
                if a == 0:
                    for j in range(trials // 2):
                        lane = ref.shape[2] - (trials // 2 - j) * ranks
                        for i in range(2):
                            to = pl.multiple_of(member * local + (2 * j + i) * select, select)
                            gradient[pl.ds(to, select), :] = ref[i, :, lane : lane + ranks]
    block = ranks // dps
    turned[...] = gradient[...].astype(f32).T
    turned_ref[...] = turned[...].astype(bf16)
    for j in range(far):
        at = pl.multiple_of((dp ^ (2 * (j + 1) + core)) * block, block)
        part = turned[pl.ds(at, block), :].astype(bf16)
        for i in range(2):
            terms[j][i] = jnp.dot(part, pair[i], preferred_element_type=f32).astype(bf16)
    rows_ref[...] = pair[core]
    result = jnp.zeros(rank_ref.shape, f32)
    for n, ref in enumerate(downs):
        i = core if n < 2 else 1 - core
        at = slice(n % 2 * (width // 2), (n % 2 + 1) * (width // 2))
        result += jnp.dot(pair[i, :, at], ref[0], preferred_element_type=f32)
    rank_ref[...] = result


def base_kernel(ys, rows_ref, weight_ref, *refs):
    kept, sent, total = refs[:ys], refs[ys : 2 * ys], refs[-1]
    tensor = lax.axis_index("tensor")
    local, width = kept[0].shape
    chunk = 512
    for f in range(0, width, chunk):
        total[:, f : f + chunk] = jnp.dot(rows_ref[...], weight_ref[:, f : f + chunk], preferred_element_type=f32)
        for b in range(ys):
            for out, member in ((kept[b], tensor ^ (2 * b)), (sent[b], tensor ^ (2 * b + 1))):
                at = pl.multiple_of(member * local, local)
                out[:, f : f + chunk] = total[pl.ds(at, local), f : f + chunk].astype(out.dtype)


def pair_kernel(kept_ref, came_ref, out_ref):
    out_ref[...] = (kept_ref[...] + came_ref[...].astype(f32)).astype(bf16)


def up_kernel(trials, ys, dps, select, block, *refs):
    tensors = 2 * ys
    far = dps // 2 - 1
    rank_refs, mine, other = refs[:ys], refs[ys : 2 * ys], refs[2 * ys : 3 * ys]
    rows_ref, turned_ref = refs[3 * ys : 3 * ys + 2]
    down_own, up_own, near = refs[3 * ys + 2 : 3 * ys + 5]
    outs, gradient, product = refs[3 * ys + 5 : -2], refs[-2], refs[-1]
    dp, tensor = lax.axis_index("dp"), lax.axis_index("tensor")
    y, core = tensor // 2, tensor % 2
    local = trials * select
    half = dps * tensors * block // 2
    width = rows_ref.shape[1]
    ranks = rank_refs[0].shape[1]
    rank = ranks // 2
    down_block = ranks // dps
    group = max(block, lanes)
    ranks_sum = rank_refs[0][...]
    for ref in rank_refs[1:]:
        ranks_sum = ranks_sum + ref[...]
    high, low = two_terms(adapter_scale * ranks_sum.T)
    for i in range(2):
        for b in range(ys):
            for ref, from_core in ((mine[b], core), (other[b], 1 - core)):
                for j in range(trials // 2):
                    lane = width + (2 * j + i) * dps * group
                    for n in range(2):
                        token = (2 * (y ^ b) + from_core) * local + (2 * j + n) * select
                        at = pl.multiple_of(token, select)
                        gradient[i, pl.ds(at, select), :] = ref[n, :, lane : lane + dps * group]
    for i in range(2):
        values = gradient[i]
        product[i] = jnp.dot(high, values, preferred_element_type=f32) + jnp.dot(
            low, values, preferred_element_type=f32
        )

    def up_part(target, i):
        column = (target * tensors + 2 * y + i) * block
        upper = column // half
        at = pl.multiple_of(upper * rank, rank)
        part = product[i, pl.ds(at, rank), pl.ds(pl.multiple_of(target * group, group), group)]
        if group > block:
            inner = column % group
            result = part[:, :block]
            for n in range(1, group // block):
                result = jnp.where(inner == n * block, part[:, n * block : (n + 1) * block], result)
            part = result
        return part

    for j in range(far):
        for i in range(2):
            outs[j][i] = up_part(dp ^ (2 * (j + 1) + core), i).astype(bf16)
    for target, out in ((dp ^ 1, near), (dp, None)):
        at = pl.multiple_of(target * down_block, down_block)
        term = jnp.dot(turned_ref[pl.ds(at, down_block), :], rows_ref[...], preferred_element_type=f32)
        part = up_part(target, core)
        if out is None:
            down_own[...] = term
            up_own[...] = part
        else:
            out[:, :width] = term.astype(bf16)
            for n in range(rank // down_block):
                lane = width + n * block
                out[:, lane : lane + block] = part[n * down_block : (n + 1) * down_block].astype(bf16)


def output_kernel(ys, *refs):
    rank_refs, terms, up_ref, out_ref = refs[:ys], refs[ys:-2], refs[-2], refs[-1]
    tensor = lax.axis_index("tensor")
    local, width = terms[0].shape
    half = width // 2
    rank = up_ref.shape[1]
    at = pl.multiple_of(tensor * local, local)
    ranks = rank_refs[0][pl.ds(at, local), :]
    for ref in rank_refs[1:]:
        ranks = ranks + ref[pl.ds(at, local), :]
    high, low = two_terms(adapter_scale * ranks)
    chunk = 512
    for f in range(0, width, chunk):
        side = rank * (f // half)
        up = up_ref[0, :, f : f + chunk]
        result = terms[0][:, f : f + chunk]
        for ref in terms[1:]:
            result = result + ref[:, f : f + chunk].astype(f32)
        result = result + jnp.dot(high[:, side : side + rank], up, preferred_element_type=f32)
        result = result + jnp.dot(low[:, side : side + rank], up, preferred_element_type=f32)
        out_ref[0, :, f : f + chunk] = result


def split_kernel(pieces, term_ref, up_ref, _near, *outs):
    core = lax.axis_index("tensor") % 2
    down_block, width = term_ref.shape[1:]
    block = up_ref.shape[2]
    size = width // pieces
    for n in range(pieces):
        outs[n][:, :size] = term_ref[1 - core, :, n * size : (n + 1) * size]
    for n in range(up_ref.shape[1] // down_block):
        lane = size + n // pieces * block
        outs[n % pieces][:, lane : lane + block] = up_ref[1 - core, n * down_block : (n + 1) * down_block, :]


def sum_kernel(far, pieces, *refs):
    down_own, up_own, near = refs[:3]
    downs, refs = refs[3 : 3 + far], refs[3 + far :]
    ups, refs = refs[:far], refs[far:]
    others = refs[: far * pieces]
    down_out, up_out = refs[far * pieces :]
    core = lax.axis_index("tensor") % 2
    down_block, width = down_own.shape
    rank, block = up_own.shape
    size = width // pieces
    for n in range(pieces):
        at = slice(n * size, (n + 1) * size)
        result = down_own[:, at] + near[:, at].astype(f32)
        for j in range(far):
            result = result + downs[j][core, :, at].astype(f32)
            result = result + others[j * pieces + n][:, :size].astype(f32)
        down_out[0, :, at] = result
    for n in range(rank // down_block):
        at = slice(n * down_block, (n + 1) * down_block)
        result = up_own[at, :] + near[:, width + n * block : width + (n + 1) * block].astype(f32)
        lane = size + n // pieces * block
        for j in range(far):
            result = result + ups[j][core, at, :].astype(f32)
            result = result + others[j * pieces + n % pieces][:, lane : lane + block].astype(f32)
        up_out[0, at, :] = result


def shards(
    residual_rows,
    input_norm_weight,
    trial_row_index,
    keyvalue_weight,
    adapter_down_weight,
    adapter_up_weight,
    keyvalue_gradient,
):
    trials, dps, tensors = lax.axis_size("trial"), lax.axis_size("dp"), lax.axis_size("tensor")
    ys = tensors // 2
    pool, features = residual_rows.shape
    tokens = trial_row_index.shape[1]
    select = tokens // (trials * tensors)
    local = tokens // tensors
    width, kv_width = keyvalue_weight.shape
    ranks = adapter_down_weight.shape[2]
    shape = jax.ShapeDtypeStruct

    def to_core(value):
        return lax.ppermute(value, "tensor", [(i, i ^ 1) for i in range(tensors)])

    def over(axis, size, mask, value):
        return lax.ppermute(value, axis, [(i, i ^ mask) for i in range(size)])

    def far_dp(j, value):
        pairs = []
        for source in range(dps):
            for member in range(tensors):
                target = source ^ (2 * (j + 1) + member % 2)
                pairs.append((source * tensors + member, target * tensors + member))
        return lax.ppermute(value, ("dp", "tensor"), pairs)

    far = dps // 2 - 1
    block = ranks // dps
    column_block = kv_width // (dps * tensors)
    group = max(column_block, lanes)
    extra = trials * dps * group + trials // 2 * ranks
    payload_shapes = [
        shape((2, select, width + (extra if a == 0 else 0)), bf16) for a in range(trials) for b in range(ys)
    ]
    gain = input_norm_weight[None, :]
    pick_operands = (
        trial_row_index,
        residual_rows,
        gain,
        keyvalue_gradient,
        adapter_up_weight,
        adapter_down_weight,
    )
    picked = pl.pallas_call(
        functools.partial(pick_kernel, trials, ys, dps, select, width, column_block),
        out_shape=payload_shapes + [shape((1, width // 2, ranks), bf16)] * 2,
        in_specs=in_hbm(6),
        out_specs=whole_vmem(len(payload_shapes) + 2),
        scratch_shapes=[pltpu.SMEM(trial_row_index.shape, jnp.int32)]
        + [pltpu.VMEM(value.shape, value.dtype) for value in pick_operands[1:5]]
        + [pltpu.VMEM((trials * select, features), f32), pltpu.SemaphoreType.DMA((7,))],
        compiler_params=params(32),
        name="pick",
    )(*[pltpu.with_memory_space_constraint(value, pltpu.HBM) for value in pick_operands])
    payloads, downs = picked[:-2], picked[-2:]
    mine = [payloads[0]] + [None] * (trials * ys - 1)
    for mask in range(1, trials * ys):
        a, b = mask // ys, mask % ys
        mine[mask] = over(("trial", "tensor"), trials * tensors, a * tensors + 2 * b, payloads[mask])
    other = [to_core(value) for value in mine]
    downs = [*downs, *[to_core(value) for value in downs]]

    rows, turned, rank_term, *terms = pl.pallas_call(
        functools.partial(term_kernel, trials, ys, dps, select, width),
        out_shape=[shape((tokens, width), bf16), shape((ranks, tokens), bf16), shape((tokens, ranks), f32)]
        + [shape((2, block, width), bf16)] * far,
        in_specs=whole_vmem(2 * trials * ys + 4),
        out_specs=whole_vmem(3 + far),
        scratch_shapes=[
            pltpu.VMEM((2, tokens, width), bf16),
            pltpu.VMEM((tokens, ranks), bf16),
            pltpu.VMEM((ranks, tokens), f32),
        ],
        compiler_params=params(16),
        cost_estimate=cost(2 * 10**10, 2 * 10**7),
        name="terms",
    )(*mine, *other, *downs)
    down_far = [far_dp(j, terms[j]) for j in range(far)]
    rank_sums = [rank_term] + [over("tensor", tensors, 2 * b, rank_term) for b in range(1, ys)]

    base_terms = pl.pallas_call(
        functools.partial(base_kernel, ys),
        out_shape=[shape((local, kv_width), f32)] * ys + [shape((local, kv_width), bf16)] * ys,
        in_specs=whole_vmem(2),
        out_specs=whole_vmem(2 * ys),
        scratch_shapes=[pltpu.VMEM((tokens, kv_width), f32)],
        compiler_params=params(8),
        cost_estimate=cost(0, 0),
        name="base",
    )(rows, keyvalue_weight)
    kept = base_terms[:ys]
    came = [None] * ys
    for b in [*range(1, ys), 0]:
        came[b] = to_core(base_terms[ys + b])
    base_sums = [kept[0], came[0]]
    for b in range(1, ys):
        paired = pl.pallas_call(
            pair_kernel,
            out_shape=shape((local, kv_width), bf16),
            in_specs=whole_vmem(2),
            out_specs=pl.BlockSpec(memory_space=pltpu.VMEM),
            compiler_params=params(4),
            cost_estimate=cost(0, 0),
            name="pair",
        )(kept[b], came[b])
        base_sums.append(over("tensor", tensors, 2 * b, paired))

    down_own, up_own, near, *up_far = pl.pallas_call(
        functools.partial(up_kernel, trials, ys, dps, select, column_block),
        out_shape=[
            shape((block, width), f32),
            shape((ranks // 2, column_block), f32),
            shape((block, width + ranks // 2 // block * column_block), bf16),
        ]
        + [shape((2, ranks // 2, column_block), bf16)] * far,
        in_specs=whole_vmem(3 * ys + 2),
        out_specs=whole_vmem(3 + far),
        scratch_shapes=[pltpu.VMEM((2, tokens, dps * group), bf16), pltpu.VMEM((2, ranks, dps * group), f32)],
        compiler_params=params(8),
        cost_estimate=cost(0, 0),
        name="up_terms",
    )(*rank_sums, *mine[:ys], *other[:ys], rows, turned)
    near = over("dp", dps, 1, near)
    up_far = [far_dp(j, up_far[j]) for j in range(far)]
    output = pl.pallas_call(
        functools.partial(output_kernel, ys),
        out_shape=shape((1, local, kv_width), f32),
        in_specs=whole_vmem(2 * ys + 2),
        out_specs=pl.BlockSpec(memory_space=pltpu.VMEM),
        compiler_params=params(8),
        cost_estimate=cost(0, 0),
        name="output",
    )(*rank_sums, *base_sums, adapter_up_weight)
    pieces = 2
    up_lanes = ranks // 2 // block // pieces * column_block
    others = []
    for down_value, up_value in zip(down_far, up_far):
        parts = pl.pallas_call(
            functools.partial(split_kernel, pieces),
            out_shape=[shape((block, width // pieces + up_lanes), bf16)] * pieces,
            in_specs=whole_vmem(3),
            out_specs=whole_vmem(pieces),
            compiler_params=params(4),
            cost_estimate=cost(0, 0),
            name="split",
        )(down_value, up_value, near)
        others += [to_core(part) for part in parts]

    grad_a, grad_b = pl.pallas_call(
        functools.partial(sum_kernel, far, pieces),
        out_shape=[shape((1, block, width), f32), shape((1, ranks // 2, column_block), f32)],
        in_specs=whole_vmem(3 + (2 + pieces) * far),
        out_specs=whole_vmem(2),
        compiler_params=params(8),
        cost_estimate=cost(0, 0),
        name="sums",
    )(down_own, up_own, near, *down_far, *up_far, *others)
    return output, grad_a, grad_b


def solution(mesh):
    return jax.shard_map(
        shards,
        mesh=mesh,
        in_specs=(
            P(("trial", "dp", "tensor"), None),
            P(),
            P(None, "dp"),
            P("tensor", None),
            P("trial", "tensor", None),
            P("trial", None, None),
            P("trial", ("dp", "tensor"), None),
        ),
        out_specs=(
            P("trial", ("dp", "tensor"), None),
            P("trial", "dp", "tensor"),
            P("trial", None, ("dp", "tensor")),
        ),
        check_vma=False,
    )
```

time: 49.5 us -> 35.7 us (0.72)
  local copies, waits for them, and re-layouts: 7.84 us -> 0.01 us
  starting transfers between devices: 20.3 us -> 14.1 us
  waiting for transfers between devices: 12.6 us -> 14.5 us
  Pallas kernels: 7.65 us -> 6.16 us
    ppermute x14 -> x6, starting transfers between devices: 19.6 us -> 8.91 us  [over(): return lax.ppermute(value, axis, [(i, i ^ mask) for i in range(size)])]
    unnamed x14 -> x6, local copies, waits for them, and re-layouts: 7.84 us -> 0.01 us
    ppermute x0 -> x2, waiting for transfers between devices: none -> 5.57 us  [far_dp(): return lax.ppermute(value, ('dp', 'tensor'), pairs)]
    ppermute x14 -> x6, waiting for transfers between devices: 12.6 us -> 7.86 us  [over(): return lax.ppermute(value, axis, [(i, i ^ mask) for i in range(size)])]
    ppermute x0 -> x2, starting transfers between devices: none -> 3 us  [far_dp(): return lax.ppermute(value, ('dp', 'tensor'), pairs)]
    pallas_call x4 -> x6, Pallas kernels: 6.18 us -> 4.52 us  [the longest x1 1.87 us: shards(): pl.pallas_call(functools.partial(pick_kernel, trials, ys, dps, select, wi...]
    ppermute x7 -> x10, starting transfers between devices: 0.64 us -> 2.23 us  [to_core(): return lax.ppermute(value, 'tensor', [(i, i ^ 1) for i in range(tensors)])]
    ppermute x7 -> x10, waiting for transfers between devices: 0.02 us -> 1.04 us  [to_core(): return lax.ppermute(value, 'tensor', [(i, i ^ 1) for i in range(tensors)])]
  transfers between devices with their start and end apart: 21 -> 18, of which waited for: 6 -> 8; matrix products, arithmetic and copies ran while one was open for 0% -> 0% of each run, Pallas kernels for 11% -> 8%
where the time goes in v2:
time: 35.7 us; the launch traced here: 35.5 us
  waiting for transfers between devices  14.5 us (41%)
  starting transfers between devices  14.1 us (39%)
  Pallas kernels  6.16 us (17%)
  between operations  0.71 us (2%)
    ppermute x6, starting transfers between devices, over(): return lax.ppermute(value, axis, [(i, i ^ mask) for i in range(size)])  8.91 us
    ppermute x6, waiting for transfers between devices, over(): return lax.ppermute(value, axis, [(i, i ^ mask) for i in range(size)])  7.86 us
    ppermute x2, waiting for transfers between devices, far_dp(): return lax.ppermute(value, ('dp', 'tensor'), pairs)  5.57 us
    ppermute x2, starting transfers between devices, far_dp(): return lax.ppermute(value, ('dp', 'tensor'), pairs)  3 us
    ppermute x10, starting transfers between devices, to_core(): return lax.ppermute(value, 'tensor', [(i, i ^ 1) for i in range(tensors)])  2.23 us
    pallas_call x1, Pallas kernels, shards(): pl.pallas_call(functools.partial(pick_kernel, trials, ys, dps, select, wi...  1.87 us
    pallas_call x1, Pallas kernels, shards(): pl.pallas_call(functools.partial(base_kernel, ys), out_shape=[shape((loca...  1.37 us
    ppermute x10, waiting for transfers between devices, to_core(): return lax.ppermute(value, 'tensor', [(i, i ^ 1) for i in range(tensors)])  1.04 us
  transfers between devices with their start and end apart: 18, of which 8 were waited for; matrix products, arithmetic and copies ran while one was open for 0% of the time, Pallas kernels for 8%

profile of v2, /device:TPU:0, one launch (start us, length us, event | category | flops | bytes accessed | tf_op | source)
XLA Modules:
  0.0 35.5 jit_solution(5488915522710903416)
XLA Ops:
  0.6 1.9 %pick.1 = (bf16[2,16,3200]{2,1,0:T(8,128)(2,1)S(1)}, bf16[2,16,3200]{2,1,0:T(8,128)(2,1)S(1)}, bf16[2,16,2048]{2,1,0:T(8,128)(2,1)S(1)}, bf16[2,16,2048]{2,1,0:T...) custom-call(s32[2,128]{1,0:T(2,128)} %index_hbm.1, bf16[32,8192]{1,0:T(8,128)(2,1)} %rows_hbm.1, ...), custom_call_target="tpu_custom_call" | custom-call | tf_op jit(solution)/shard_map/pick/pallas_call | solution.py:361
  2.5 3.0 %collective-permute-start = (bf16[2,16,3200]{2,1,0:T(8,128)(2,1)S(1)}, bf16[2,16,3200]{2,1,0:T(8,128)(2,1)S(1)}, u32[]{:S(2)}, u32[]{:S(2)}) collective-permute-start(bf16[2,16,3200]{2,1,0:T(8,128)(2,1)S(1)} %get-tuple-element.26), channel_id=1, source_target_pairs={{0,2},{1,3},{2,0},{3,1},{16,18},{17,19},{18,16},{19,17},{4,6},{5,7... | collective-permute-start | bytes 614408 | tf_op jit(solution)/shard_map/ppermute | solution.py:334
  5.5 1.5 %collective-permute-start.1 = (bf16[2,16,2048]{2,1,0:T(8,128)(2,1)S(1)}, bf16[2,16,2048]{2,1,0:T(8,128)(2,1)S(1)}, u32[]{:S(2)}, u32[]{:S(2)}) collective-permute-start(bf16[2,16,2048]{2,1,0:T(8,128)(2,1)S(1)} %get-tuple-element.27), channel_id=1, source_target_pairs={{0,16},{1,17},{2,18},{3,19},{16,0},{17,1},{18,2},{19,3},{4,20},{5,... | collective-permute-start | bytes 393224 | tf_op jit(solution)/shard_map/ppermute | solution.py:334
  7.0 0.0 collective-permute-start.3
  7.0 0.1 collective-permute-start.2
  7.1 0.4 %collective-permute-start.7 = (bf16[1,1024,128]{2,1,0:T(8,128)(2,1)S(1)}, bf16[1,1024,128]{2,1,0:T(8,128)(2,1)S(1)}, u32[]{:S(2)}, u32[]{:S(2)}) collective-permute-start(bf16[1,1024,128]{2,1,0:T(8,128)(2,1)S(1)} %get-tuple-element.29.refs_8_), channel_id=1, source_target_pairs={{0,1},{1,0},{2,3},{3,2},{4,5},{5,4},{6,7},{7,6},{8,9},{9,8},{10,11... | collective-permute-start | bytes 786440 | tf_op jit(solution)/shard_map/ppermute | solution.py:331
  7.5 3.4 %collective-permute-done.1.refs_2_ = bf16[2,16,2048]{2,1,0:T(8,128)(2,1)S(1)} collective-permute-done((bf16[2,16,2048]{2,1,0:T(8,128)(2,1)S(1)}, bf16[2,16,2048]{2,1,0:T(8,128)(2,1)S(1)}, u32[]{:S(2)}, u32[]{:S(2)}) %collective-permute-start.1) | collective-permute-done | bytes 131104 | tf_op jit(solution)/shard_map/ppermute | solution.py:334
  11.0 1.7 %collective-permute-done.refs_1_.refs_3_ = bf16[2,16,3200]{2,1,0:T(8,128)(2,1)S(1)} collective-permute-done((bf16[2,16,3200]{2,1,0:T(8,128)(2,1)S(1)}, bf16[2,16,3200]{2,1,0:T(8,128)(2,1)S(1)}, u32[]{:S(2)}, u32[]{:S(2)}) %collective-permute-start) | collective-permute-done | bytes 204832 | tf_op jit(solution)/shard_map/ppermute | solution.py:334
  12.7 0.0 collective-permute-start.4
  12.7 1.1 %collective-permute-done.2.refs_3_ = bf16[2,16,2048]{2,1,0:T(8,128)(2,1)S(1)} collective-permute-done((bf16[2,16,2048]{2,1,0:T(8,128)(2,1)S(1)}, bf16[2,16,2048]{2,1,0:T(8,128)(2,1)S(1)}, u32[]{:S(2)}, u32[]{:S(2)}) %collective-permute-start.2) | collective-permute-done | bytes 131104 | tf_op jit(solution)/shard_map/ppermute | solution.py:334
  13.8 0.0 collective-permute-start.5
  13.8 0.0 collective-permute-done.3.refs_4_
  13.8 0.5 %collective-permute-start.6 = (bf16[2,16,2048]{2,1,0:T(8,128)(2,1)S(1)}, bf16[2,16,2048]{2,1,0:T(8,128)(2,1)S(1)}, u32[]{:S(2)}, u32[]{:S(2)}) collective-permute-start(bf16[2,16,2048]{2,1,0:T(8,128)(2,1)S(1)} %collective-permute-done.2.refs_3_), channel_id=1, source_target_pairs={{0,1},{1,0},{2,3},{3,2},{4,5},{5,4},{6,7},{7,6},{8,9},{9,8},{10,11... | collective-permute-start | bytes 393224 | tf_op jit(solution)/shard_map/ppermute | solution.py:331
  14.3 0.8 %collective-permute-done.5.refs_6_ = bf16[2,16,2048]{2,1,0:T(8,128)(2,1)S(1)} collective-permute-done((bf16[2,16,2048]{2,1,0:T(8,128)(2,1)S(1)}, bf16[2,16,2048]{2,1,0:T(8,128)(2,1)S(1)}, u32[]{:S(2)}, u32[]{:S(2)}) %collective-permute-start.5) | collective-permute-done | bytes 131104 | tf_op jit(solution)/shard_map/ppermute | solution.py:331
  15.2 0.2 collective-permute-done.6.refs_7_
  15.4 0.7 %terms.1 = (bf16[128,2048]{1,0:T(8,128)(2,1)S(1)}, bf16[128,128]{1,0:T(8,128)(2,1)S(1)}, f32[128,128]{1,0:T(8,128)S(1)}, bf16[2,32,2048]{2,1,0:T(8,128)(2,1)S(1)}) custom-call(bf16[2,16,3200]{2,1,0:T(8,128)(2,1)S(1)} %get-tuple-element.25.refs_0_.refs_2_, bf16[2,16,3200]{2,1,0:T(8,128)(2,1)S(1)} %collective-permute-done.refs_1_.refs_3_, ...), custom_call_target="tpu_custom_call" | custom-call | flops 20000000000 | bytes 20000000 | tf_op jit(solution)/shard_map/terms/pallas_call | solution.py:380
  16.1 0.0 copy-start
  16.1 2.7 %collective-permute-start.14 = (bf16[2,32,2048]{2,1,0:T(8,128)(2,1)S(1)}, bf16[2,32,2048]{2,1,0:T(8,128)(2,1)S(1)}, u32[]{:S(2)}, u32[]{:S(2)}) collective-permute-start(bf16[2,32,2048]{2,1,0:T(8,128)(2,1)S(1)} %get-tuple-element.41), channel_id=1, source_target_pairs={{0,8},{1,13},{2,10},{3,15},{4,12},{5,9},{6,14},{7,11},{8,0},{9,5},... | collective-permute-start | bytes 786440 | tf_op jit(solution)/shard_map/ppermute | solution.py:342
  18.8 1.6 %collective-permute-start.9 = (f32[128,128]{1,0:T(8,128)S(1)}, f32[128,128]{1,0:T(8,128)S(1)}, u32[]{:S(2)}, u32[]{:S(2)}) collective-permute-start(f32[128,128]{1,0:T(8,128)S(1)} %get-tuple-element.31.refs_0_), channel_id=1, source_target_pairs={{0,2},{1,3},{2,0},{3,1},{4,6},{5,7},{6,4},{7,5},{8,10},{9,11},{10,... | collective-permute-start | bytes 196616 | tf_op jit(solution)/shard_map/ppermute | solution.py:334
  20.4 1.4 %base.1 = (f32[32,2048]{1,0:T(8,128)S(1)}, f32[32,2048]{1,0:T(8,128)S(1)}, bf16[32,2048]{1,0:T(8,128)(2,1)S(1)}, bf16[32,2048]{1,0:T(8,128)(2,1)S(1)}) custom-call(bf16[128,2048]{1,0:T(8,128)(2,1)S(1)} %get-tuple-element.32.rows_ref.refs_6_, bf16[2048,2048]{1,0:T(8,128)(2,1)S(1)} %bitcast.2), custom_call_target="tpu_custom_call" | custom-call | tf_op jit(solution)/shard_map/base/pallas_call | solution.py:398
  21.8 0.7 %collective-permute-start.11 = (bf16[32,2048]{1,0:T(8,128)(2,1)S(1)}, bf16[32,2048]{1,0:T(8,128)(2,1)S(1)}, u32[]{:S(2)}, u32[]{:S(2)}) collective-permute-start(bf16[32,2048]{1,0:T(8,128)(2,1)S(1)} %get-tuple-element.36), channel_id=1, source_target_pairs={{0,1},{1,0},{2,3},{3,2},{4,5},{5,4},{6,7},{7,6},{8,9},{9,8},{10,11... | collective-permute-start | bytes 393224 | tf_op jit(solution)/shard_map/ppermute | solution.py:331
  22.5 1.2 %collective-permute-done.9.refs_1_ = f32[128,128]{1,0:T(8,128)S(1)} collective-permute-done((f32[128,128]{1,0:T(8,128)S(1)}, f32[128,128]{1,0:T(8,128)S(1)}, u32[]{:S(2)}, u32[]{:S(2)}) %collective-permute-start.9) | collective-permute-done | bytes 65568 | tf_op jit(solution)/shard_map/ppermute | solution.py:334
  23.6 0.5 %up_terms.1 = (f32[32,2048]{1,0:T(8,128)S(1)}, f32[64,128]{1,0:T(8,128)S(1)}, bf16[32,2304]{1,0:T(8,128)(2,1)S(1)}, bf16[2,64,128]{2,1,0:T(8,128)(2,1)S(1)}) custom-call(f32[128,128]{1,0:T(8,128)S(1)} %get-tuple-element.31.refs_0_, f32[128,128]{1,0:T(8,128)S(1)} %collective-permute-done.9.refs_1_, ...), custom_call_target="tpu_custom_call" | custom-call | tf_op jit(solution)/shard_map/up_terms/pallas_call | solution.py:425
  24.1 1.0 %collective-permute-start.13 = (bf16[32,2304]{1,0:T(8,128)(2,1)S(1)}, bf16[32,2304]{1,0:T(8,128)(2,1)S(1)}, u32[]{:S(2)}, u32[]{:S(2)}) collective-permute-start(bf16[32,2304]{1,0:T(8,128)(2,1)S(1)} %get-tuple-element.40), channel_id=1, source_target_pairs={{0,4},{4,0},{8,12},{12,8},{1,5},{5,1},{9,13},{13,9},{2,6},{6,2},{1... | collective-permute-start | bytes 442376 | tf_op jit(solution)/shard_map/ppermute | solution.py:334
  25.1 1.7 %collective-permute-start.12 = (bf16[32,2048]{1,0:T(8,128)(2,1)S(1)}, bf16[32,2048]{1,0:T(8,128)(2,1)S(1)}, u32[]{:S(2)}, u32[]{:S(2)}) collective-permute-start(bf16[32,2048]{1,0:T(8,128)(2,1)S(1)} %pair.1), channel_id=1, source_target_pairs={{0,2},{1,3},{2,0},{3,1},{4,6},{5,7},{6,4},{7,5},{8,10},{9,11},{10,... | collective-permute-start | bytes 393224 | tf_op jit(solution)/shard_map/ppermute | solution.py:334
  26.9 0.3 collective-permute-start.15
  27.2 5.6 %collective-permute-done.15.up_ref.refs_4_ = bf16[2,64,128]{2,1,0:T(8,128)(2,1)S(1)} collective-permute-done((bf16[2,64,128]{2,1,0:T(8,128)(2,1)S(1)}, bf16[2,64,128]{2,1,0:T(8,128)(2,1)S(1)}, u32[]{:S(2)}, u32[]{:S(2)}) %collective-permute-start.15) | collective-permute-done | bytes 32800 | tf_op jit(solution)/shard_map/ppermute | solution.py:342
  32.8 0.4 %collective-permute-done.13._near.refs_2_ = bf16[32,2304]{1,0:T(8,128)(2,1)S(1)} collective-permute-done((bf16[32,2304]{1,0:T(8,128)(2,1)S(1)}, bf16[32,2304]{1,0:T(8,128)(2,1)S(1)}, u32[]{:S(2)}, u32[]{:S(2)}) %collective-permute-start.13) | collective-permute-done | bytes 147488 | tf_op jit(solution)/shard_map/ppermute | solution.py:334
  33.2 0.1 collective-permute-start.16
  33.3 0.5 %collective-permute-start.17 = (bf16[32,1152]{1,0:T(8,128)(2,1)S(1)}, bf16[32,1152]{1,0:T(8,128)(2,1)S(1)}, u32[]{:S(2)}, u32[]{:S(2)}) collective-permute-start(bf16[32,1152]{1,0:T(8,128)(2,1)S(1)} %get-tuple-element.44), channel_id=1, source_target_pairs={{0,1},{1,0},{2,3},{3,2},{4,5},{5,4},{6,7},{7,6},{8,9},{9,8},{10,11... | collective-permute-start | bytes 221192 | tf_op jit(solution)/shard_map/ppermute | solution.py:331
  33.8 0.9 %output.1 = f32[1,32,2048]{2,1,0:T(8,128)} custom-call(f32[128,128]{1,0:T(8,128)S(1)} %get-tuple-element.31.refs_0_, f32[128,128]{1,0:T(8,128)S(1)} %collective-permute-done.9.refs_1_, f32[32,2048]{1,0:T(8,128)S(1)} %get-tuple-element.33.refs_2_, bf16[32,2048]{1,0:T(8,128)(2,1)S(1)} %collective-permute-done.10.refs_3_, ...), custom_call_target="tpu_custom_call" | custom-call | tf_op jit(solution)/shard_map/output/pallas_call | solution.py:442
  34.7 0.8 %sums.1 = (f32[1,32,2048]{2,1,0:T(8,128)}, f32[1,64,128]{2,1,0:T(8,128)}) custom-call(f32[32,2048]{1,0:T(8,128)S(1)} %get-tuple-element.38.refs_0_, f32[64,128]{1,0:T(8,128)S(1)} %get-tuple-element.39.refs_1_, bf16[32,2304]{1,0:T(8,128)(2,1)S(1)} %collective-permute-done.13._near.refs_2_, bf16[2,32,2048]{2,1,0:T(8,128)(2,1)S(1)} %collective-permute-done.14.term_ref.refs_3_, ...), custom_call_target="tpu_custom_call" | custom-call | tf_op jit(solution)/shard_map/sums/pallas_call | solution.py:466
  (19 shorter events, 0.1 us)
Async XLA Ops:
  2.5 10.2 %collective-permute-start = (bf16[2,16,3200]{2,1,0:T(8,128)(2,1)S(1)}, bf16[2,16,3200]{2,1,0:T(8,128)(2,1)S(1)}, u32[]{:S(2)}, u32[]{:S(2)}) collective-permute-start(bf16[2,16,3200]{2,1,0:T(8,128)(2,1)S(1)} %get-tuple-element.26), channel_id=1, source_target_pairs={{0,2},{1,3},{2,0},{3,1},{16,18},{17,19},{18,16},{19,17},{4,6},{5,7... | collective-permute-start | bytes 614408 | tf_op jit(solution)/shard_map/ppermute | solution.py:334
  5.5 5.4 %collective-permute-start.1 = (bf16[2,16,2048]{2,1,0:T(8,128)(2,1)S(1)}, bf16[2,16,2048]{2,1,0:T(8,128)(2,1)S(1)}, u32[]{:S(2)}, u32[]{:S(2)}) collective-permute-start(bf16[2,16,2048]{2,1,0:T(8,128)(2,1)S(1)} %get-tuple-element.27), channel_id=1, source_target_pairs={{0,16},{1,17},{2,18},{3,19},{16,0},{17,1},{18,2},{19,3},{4,20},{5,... | collective-permute-start | bytes 393224 | tf_op jit(solution)/shard_map/ppermute | solution.py:334
  7.0 6.8 %collective-permute-start.3 = (bf16[2,16,3200]{2,1,0:T(8,128)(2,1)S(1)}, bf16[2,16,3200]{2,1,0:T(8,128)(2,1)S(1)}, u32[]{:S(2)}, u32[]{:S(2)}) collective-permute-start(bf16[2,16,3200]{2,1,0:T(8,128)(2,1)S(1)} %get-tuple-element.25.refs_0_.refs_2_), channel_id=1, source_target_pairs={{0,1},{1,0},{2,3},{3,2},{4,5},{5,4},{6,7},{7,6},{8,9},{9,8},{10,11... | collective-permute-start | bytes 614408 | tf_op jit(solution)/shard_map/ppermute | solution.py:331
  7.0 6.8 %collective-permute-start.2 = (bf16[2,16,2048]{2,1,0:T(8,128)(2,1)S(1)}, bf16[2,16,2048]{2,1,0:T(8,128)(2,1)S(1)}, u32[]{:S(2)}, u32[]{:S(2)}) collective-permute-start(bf16[2,16,2048]{2,1,0:T(8,128)(2,1)S(1)} %get-tuple-element.28), channel_id=1, source_target_pairs={{0,18},{1,19},{2,16},{3,17},{16,2},{17,3},{18,0},{19,1},{4,22},{5,... | collective-permute-start | bytes 393224 | tf_op jit(solution)/shard_map/ppermute | solution.py:334
  7.1 8.3 %collective-permute-start.7 = (bf16[1,1024,128]{2,1,0:T(8,128)(2,1)S(1)}, bf16[1,1024,128]{2,1,0:T(8,128)(2,1)S(1)}, u32[]{:S(2)}, u32[]{:S(2)}) collective-permute-start(bf16[1,1024,128]{2,1,0:T(8,128)(2,1)S(1)} %get-tuple-element.29.refs_8_), channel_id=1, source_target_pairs={{0,1},{1,0},{2,3},{3,2},{4,5},{5,4},{6,7},{7,6},{8,9},{9,8},{10,11... | collective-permute-start | bytes 786440 | tf_op jit(solution)/shard_map/ppermute | solution.py:331
  11.0 9.4 %slice-start = ((s8[8388608]{0:T(1024)(128)(4,1)}), s8[4194304]{0:T(1024)(128)(4,1)S(1)}, s32[]{:S(2)}) async-start(s8[8388608]{0:T(1024)(128)(4,1)} %bitcast.1), calls=%async_computation | async-start | bytes 8388608
  11.0 9.4 %slice-start.1 = ((s8[8388608]{0:T(1024)(128)(4,1)}), s8[4194304]{0:T(1024)(128)(4,1)S(1)}, s32[]{:S(2)}) async-start(s8[8388608]{0:T(1024)(128)(4,1)} %bitcast.1), calls=%async_computation.1 | async-start | bytes 8388608
  11.0 4.4 %collective-permute-start.8 = (bf16[1,1024,128]{2,1,0:T(8,128)(2,1)S(1)}, bf16[1,1024,128]{2,1,0:T(8,128)(2,1)S(1)}, u32[]{:S(2)}, u32[]{:S(2)}) collective-permute-start(bf16[1,1024,128]{2,1,0:T(8,128)(2,1)S(1)} %get-tuple-element.30.refs_9_), channel_id=1, source_target_pairs={{0,1},{1,0},{2,3},{3,2},{4,5},{5,4},{6,7},{7,6},{8,9},{9,8},{10,11... | collective-permute-start | bytes 786440 | tf_op jit(solution)/shard_map/ppermute | solution.py:331
  12.7 2.7 %collective-permute-start.4 = (bf16[2,16,3200]{2,1,0:T(8,128)(2,1)S(1)}, bf16[2,16,3200]{2,1,0:T(8,128)(2,1)S(1)}, u32[]{:S(2)}, u32[]{:S(2)}) collective-permute-start(bf16[2,16,3200]{2,1,0:T(8,128)(2,1)S(1)} %collective-permute-done.refs_1_.refs_3_), channel_id=1, source_target_pairs={{0,1},{1,0},{2,3},{3,2},{4,5},{5,4},{6,7},{7,6},{8,9},{9,8},{10,11... | collective-permute-start | bytes 614408 | tf_op jit(solution)/shard_map/ppermute | solution.py:331
  13.8 1.3 %collective-permute-start.5 = (bf16[2,16,2048]{2,1,0:T(8,128)(2,1)S(1)}, bf16[2,16,2048]{2,1,0:T(8,128)(2,1)S(1)}, u32[]{:S(2)}, u32[]{:S(2)}) collective-permute-start(bf16[2,16,2048]{2,1,0:T(8,128)(2,1)S(1)} %collective-permute-done.1.refs_2_), channel_id=1, source_target_pairs={{0,1},{1,0},{2,3},{3,2},{4,5},{5,4},{6,7},{7,6},{8,9},{9,8},{10,11... | collective-permute-start | bytes 393224 | tf_op jit(solution)/shard_map/ppermute | solution.py:331
  13.8 1.5 %collective-permute-start.6 = (bf16[2,16,2048]{2,1,0:T(8,128)(2,1)S(1)}, bf16[2,16,2048]{2,1,0:T(8,128)(2,1)S(1)}, u32[]{:S(2)}, u32[]{:S(2)}) collective-permute-start(bf16[2,16,2048]{2,1,0:T(8,128)(2,1)S(1)} %collective-permute-done.2.refs_3_), channel_id=1, source_target_pairs={{0,1},{1,0},{2,3},{3,2},{4,5},{5,4},{6,7},{7,6},{8,9},{9,8},{10,11... | collective-permute-start | bytes 393224 | tf_op jit(solution)/shard_map/ppermute | solution.py:331
  16.1 17.7 %copy-start = (bf16[1,64,2048]{2,1,0:T(8,128)(2,1)S(1)}, bf16[1,64,2048]{2,1,0:T(8,128)(2,1)}, u32[]{:S(2)}) copy-start(bf16[1,64,2048]{2,1,0:T(8,128)(2,1)} %refs_5_.1) | copy-start | bytes 786436
  16.1 17.1 %collective-permute-start.14 = (bf16[2,32,2048]{2,1,0:T(8,128)(2,1)S(1)}, bf16[2,32,2048]{2,1,0:T(8,128)(2,1)S(1)}, u32[]{:S(2)}, u32[]{:S(2)}) collective-permute-start(bf16[2,32,2048]{2,1,0:T(8,128)(2,1)S(1)} %get-tuple-element.41), channel_id=1, source_target_pairs={{0,8},{1,13},{2,10},{3,15},{4,12},{5,9},{6,14},{7,11},{8,0},{9,5},... | collective-permute-start | bytes 786440 | tf_op jit(solution)/shard_map/ppermute | solution.py:342
  18.8 4.9 %collective-permute-start.9 = (f32[128,128]{1,0:T(8,128)S(1)}, f32[128,128]{1,0:T(8,128)S(1)}, u32[]{:S(2)}, u32[]{:S(2)}) collective-permute-start(f32[128,128]{1,0:T(8,128)S(1)} %get-tuple-element.31.refs_0_), channel_id=1, source_target_pairs={{0,2},{1,3},{2,0},{3,1},{4,6},{5,7},{6,4},{7,5},{8,10},{9,11},{10,... | collective-permute-start | bytes 196616 | tf_op jit(solution)/shard_map/ppermute | solution.py:334
  21.8 3.3 %collective-permute-start.11 = (bf16[32,2048]{1,0:T(8,128)(2,1)S(1)}, bf16[32,2048]{1,0:T(8,128)(2,1)S(1)}, u32[]{:S(2)}, u32[]{:S(2)}) collective-permute-start(bf16[32,2048]{1,0:T(8,128)(2,1)S(1)} %get-tuple-element.36), channel_id=1, source_target_pairs={{0,1},{1,0},{2,3},{3,2},{4,5},{5,4},{6,7},{7,6},{8,9},{9,8},{10,11... | collective-permute-start | bytes 393224 | tf_op jit(solution)/shard_map/ppermute | solution.py:331
  24.1 9.0 %collective-permute-start.13 = (bf16[32,2304]{1,0:T(8,128)(2,1)S(1)}, bf16[32,2304]{1,0:T(8,128)(2,1)S(1)}, u32[]{:S(2)}, u32[]{:S(2)}) collective-permute-start(bf16[32,2304]{1,0:T(8,128)(2,1)S(1)} %get-tuple-element.40), channel_id=1, source_target_pairs={{0,4},{4,0},{8,12},{12,8},{1,5},{5,1},{9,13},{13,9},{2,6},{6,2},{1... | collective-permute-start | bytes 442376 | tf_op jit(solution)/shard_map/ppermute | solution.py:334
  25.1 8.7 %collective-permute-start.10 = (bf16[32,2048]{1,0:T(8,128)(2,1)S(1)}, bf16[32,2048]{1,0:T(8,128)(2,1)S(1)}, u32[]{:S(2)}, u32[]{:S(2)}) collective-permute-start(bf16[32,2048]{1,0:T(8,128)(2,1)S(1)} %get-tuple-element.34), channel_id=1, source_target_pairs={{0,1},{1,0},{2,3},{3,2},{4,5},{5,4},{6,7},{7,6},{8,9},{9,8},{10,11... | collective-permute-start | bytes 393224 | tf_op jit(solution)/shard_map/ppermute | solution.py:331
  25.1 8.6 %collective-permute-start.12 = (bf16[32,2048]{1,0:T(8,128)(2,1)S(1)}, bf16[32,2048]{1,0:T(8,128)(2,1)S(1)}, u32[]{:S(2)}, u32[]{:S(2)}) collective-permute-start(bf16[32,2048]{1,0:T(8,128)(2,1)S(1)} %pair.1), channel_id=1, source_target_pairs={{0,2},{1,3},{2,0},{3,1},{4,6},{5,7},{6,4},{7,5},{8,10},{9,11},{10,... | collective-permute-start | bytes 393224 | tf_op jit(solution)/shard_map/ppermute | solution.py:334
  26.9 5.9 %collective-permute-start.15 = (bf16[2,64,128]{2,1,0:T(8,128)(2,1)S(1)}, bf16[2,64,128]{2,1,0:T(8,128)(2,1)S(1)}, u32[]{:S(2)}, u32[]{:S(2)}) collective-permute-start(bf16[2,64,128]{2,1,0:T(8,128)(2,1)S(1)} %get-tuple-element.42), channel_id=1, source_target_pairs={{0,8},{1,13},{2,10},{3,15},{4,12},{5,9},{6,14},{7,11},{8,0},{9,5},... | collective-permute-start | bytes 98312 | tf_op jit(solution)/shard_map/ppermute | solution.py:342
  33.2 1.5 %collective-permute-start.16 = (bf16[32,1152]{1,0:T(8,128)(2,1)S(1)}, bf16[32,1152]{1,0:T(8,128)(2,1)S(1)}, u32[]{:S(2)}, u32[]{:S(2)}) collective-permute-start(bf16[32,1152]{1,0:T(8,128)(2,1)S(1)} %get-tuple-element.43), channel_id=1, source_target_pairs={{0,1},{1,0},{2,3},{3,2},{4,5},{5,4},{6,7},{7,6},{8,9},{9,8},{10,11... | collective-permute-start | bytes 221192 | tf_op jit(solution)/shard_map/ppermute | solution.py:331
  33.3 1.5 %collective-permute-start.17 = (bf16[32,1152]{1,0:T(8,128)(2,1)S(1)}, bf16[32,1152]{1,0:T(8,128)(2,1)S(1)}, u32[]{:S(2)}, u32[]{:S(2)}) collective-permute-start(bf16[32,1152]{1,0:T(8,128)(2,1)S(1)} %get-tuple-element.44), channel_id=1, source_target_pairs={{0,1},{1,0},{2,3},{3,2},{4,5},{5,4},{6,7},{7,6},{8,9},{9,8},{10,11... | collective-permute-start | bytes 221192 | tf_op jit(solution)/shard_map/ppermute | solution.py:331

commit v3 on v2

--- a/solution.py
+++ b/solution.py
@@ -46,7 +46,7 @@
 def pick_kernel(trials, ys, dps, select, width, column_block, index_hbm, rows_hbm, gain_hbm, grad_hbm, up_hbm, down_hbm, *rest):
     outs, rest = rest[: trials * ys], rest[trials * ys :]
     downs = rest[:2]
-    index_ref, rows_ref, gain_ref, grad_ref, up_ref, chosen, sems = rest[2:]
+    index_ref, rows_ref, gain_ref, grad_ref, up_ref, sems = rest[2:]
     copies = [
         pltpu.make_async_copy(source, target, sems.at[i])
         for i, (source, target) in enumerate(
@@ -78,12 +78,11 @@
             picked = jnp.where(row == i, index_ref[trial ^ a, start + i], picked)
         hots.append(jnp.where(column == picked, 1.0, 0.0).astype(bf16))
     hot = jnp.concatenate(hots, axis=0)
-    square = jnp.zeros((trials * select, 1), f32)
+    square = jnp.zeros((pool, 1), f32)
     chunk = 1024
     copies[1].wait()
     for f in range(0, features, chunk):
-        part = jnp.dot(hot, rows_ref[:, f : f + chunk], preferred_element_type=f32)
-        chosen[:, f : f + chunk] = part
+        part = rows_ref[:, f : f + chunk].astype(f32)
         square += jnp.sum(part * part, axis=1, keepdims=True)
     scale = lax.rsqrt(square / features + norm_eps)
     half = grad_ref.shape[2] // 2
@@ -92,15 +91,14 @@
         copy.wait()
     keys = adapter_scale * dot_last(grad_ref[0, :, :half], up_ref[0, :, :half])
     values = adapter_scale * dot_last(grad_ref[0, :, half:], up_ref[0, :, half:])
-    for a in range(trials):
-        for b in range(ys):
-            out = outs[a * ys + b]
-            for core in range(2):
-                for f in range(0, width, chunk):
-                    at = pl.multiple_of((y ^ b) * (2 * width) + core * width + f, chunk)
-                    part = chosen[a * select : (a + 1) * select, pl.ds(at, chunk)]
-                    part = part * scale[a * select : (a + 1) * select] * gain_ref[:, pl.ds(at, chunk)]
-                    out[core, :, f : f + chunk] = part.astype(bf16)
+    for b in range(ys):
+        for core in range(2):
+            for f in range(0, width, chunk):
+                at = pl.multiple_of((y ^ b) * (2 * width) + core * width + f, chunk)
+                part = rows_ref[:, pl.ds(at, chunk)].astype(f32) * scale * gain_ref[:, pl.ds(at, chunk)]
+                part = jnp.dot(hot, part.astype(bf16), preferred_element_type=f32).astype(bf16)
+                for a in range(trials):
+                    outs[a * ys + b][core, :, f : f + chunk] = part[a * select : (a + 1) * select]
     group = max(column_block, lanes)
     for b in range(ys):
         for j in range(trials // 2):
@@ -124,10 +122,9 @@
     count = trials * ys
     far = dps // 2 - 1
     mine, other, refs = refs[:count], refs[count : 2 * count], refs[2 * count :]
-    downs, refs = refs[:4], refs[4:]
-    rows_ref, turned_ref, rank_ref = refs[:3]
-    terms = refs[3 : 3 + far]
-    pair, gradient, turned = refs[3 + far :]
+    pair, turned_ref = refs[:2]
+    terms = refs[2 : 2 + far]
+    gradient, turned = refs[2 + far :]
     trial, dp, tensor = lax.axis_index("trial"), lax.axis_index("dp"), lax.axis_index("tensor")
     tensors = 2 * ys
     y, core = tensor // 2, tensor % 2
@@ -154,23 +151,28 @@
         at = pl.multiple_of((dp ^ (2 * (j + 1) + core)) * block, block)
         part = turned[pl.ds(at, block), :].astype(bf16)
         for i in range(2):
-            terms[j][i] = jnp.dot(part, pair[i], preferred_element_type=f32).astype(bf16)
-    rows_ref[...] = pair[core]
+            first = terms[j].shape[2]
+            terms[j][i] = jnp.dot(part, pair[i, :, :first], preferred_element_type=f32).astype(bf16)
+
+
+def rank_kernel(pair, *refs):
+    downs, rank_ref = refs[:4], refs[4]
+    core = lax.axis_index("tensor") % 2
     result = jnp.zeros(rank_ref.shape, f32)
     for n, ref in enumerate(downs):
         i = core if n < 2 else 1 - core
-        at = slice(n % 2 * (width // 2), (n % 2 + 1) * (width // 2))
-        result += jnp.dot(pair[i, :, at], ref[0], preferred_element_type=f32)
+        size = ref.shape[1]
+        result += jnp.dot(pair[i, :, n % 2 * size : (n % 2 + 1) * size], ref[0], preferred_element_type=f32)
     rank_ref[...] = result
 
 
-def base_kernel(ys, rows_ref, weight_ref, *refs):
+def base_kernel(ys, pair, weight_ref, *refs):
     kept, sent, total = refs[:ys], refs[ys : 2 * ys], refs[-1]
     tensor = lax.axis_index("tensor")
     local, width = kept[0].shape
     chunk = 512
     for f in range(0, width, chunk):
-        total[:, f : f + chunk] = jnp.dot(rows_ref[...], weight_ref[:, f : f + chunk], preferred_element_type=f32)
+        total[:, f : f + chunk] = jnp.dot(pair[tensor % 2], weight_ref[:, f : f + chunk], preferred_element_type=f32)
         for b in range(ys):
             for out, member in ((kept[b], tensor ^ (2 * b)), (sent[b], tensor ^ (2 * b + 1))):
                 at = pl.multiple_of(member * local, local)
@@ -185,14 +187,14 @@
     tensors = 2 * ys
     far = dps // 2 - 1
     rank_refs, mine, other = refs[:ys], refs[ys : 2 * ys], refs[2 * ys : 3 * ys]
-    rows_ref, turned_ref = refs[3 * ys : 3 * ys + 2]
+    pair, turned_ref = refs[3 * ys : 3 * ys + 2]
     down_own, up_own, near = refs[3 * ys + 2 : 3 * ys + 5]
     outs, gradient, product = refs[3 * ys + 5 : -2], refs[-2], refs[-1]
     dp, tensor = lax.axis_index("dp"), lax.axis_index("tensor")
     y, core = tensor // 2, tensor % 2
     local = trials * select
     half = dps * tensors * block // 2
-    width = rows_ref.shape[1]
+    width = pair.shape[2]
     ranks = rank_refs[0].shape[1]
     rank = ranks // 2
     down_block = ranks // dps
@@ -230,11 +232,18 @@
         return part
 
     for j in range(far):
+        size = outs[j].shape[2] - rank // down_block * block
+        at = pl.multiple_of((dp ^ (2 * (j + 1) + core)) * down_block, down_block)
         for i in range(2):
-            outs[j][i] = up_part(dp ^ (2 * (j + 1) + core), i).astype(bf16)
+            term = jnp.dot(turned_ref[pl.ds(at, down_block), :], pair[i, :, width - size :], preferred_element_type=f32)
+            outs[j][i, :, :size] = term.astype(bf16)
+            part = up_part(dp ^ (2 * (j + 1) + core), i).astype(bf16)
+            for n in range(rank // down_block):
+                lane = size + n * block
+                outs[j][i, :, lane : lane + block] = part[n * down_block : (n + 1) * down_block]
     for target, out in ((dp ^ 1, near), (dp, None)):
         at = pl.multiple_of(target * down_block, down_block)
-        term = jnp.dot(turned_ref[pl.ds(at, down_block), :], rows_ref[...], preferred_element_type=f32)
+        term = jnp.dot(turned_ref[pl.ds(at, down_block), :], pair[core], preferred_element_type=f32)
         part = up_part(target, core)
         if out is None:
             down_own[...] = term
@@ -269,43 +278,38 @@
         out_ref[0, :, f : f + chunk] = result
 
 
-def split_kernel(pieces, term_ref, up_ref, _near, *outs):
-    core = lax.axis_index("tensor") % 2
-    down_block, width = term_ref.shape[1:]
-    block = up_ref.shape[2]
-    size = width // pieces
-    for n in range(pieces):
-        outs[n][:, :size] = term_ref[1 - core, :, n * size : (n + 1) * size]
-    for n in range(up_ref.shape[1] // down_block):
-        lane = size + n // pieces * block
-        outs[n % pieces][:, lane : lane + block] = up_ref[1 - core, n * down_block : (n + 1) * down_block, :]
-
-
-def sum_kernel(far, pieces, *refs):
+def split_kernel(*refs):
+    term_ref, out_ref = refs[0], refs[-1]
+    size = term_ref.shape[2]
+    out_ref[:, :size] = term_ref[1 - lax.axis_index("tensor") % 2]
+    if out_ref.shape[1] > size:
+        out_ref[:, size:] = jnp.zeros((out_ref.shape[0], out_ref.shape[1] - size), bf16)
+
+
+def sum_kernel(far, *refs):
     down_own, up_own, near = refs[:3]
-    downs, refs = refs[3 : 3 + far], refs[3 + far :]
-    ups, refs = refs[:far], refs[far:]
-    others = refs[: far * pieces]
-    down_out, up_out = refs[far * pieces :]
+    firsts, seconds = refs[3 : 3 + far], refs[3 + far : 3 + 2 * far]
+    others, (down_out, up_out) = refs[3 + 2 * far : -2], refs[-2:]
     core = lax.axis_index("tensor") % 2
     down_block, width = down_own.shape
     rank, block = up_own.shape
-    size = width // pieces
-    for n in range(pieces):
-        at = slice(n * size, (n + 1) * size)
-        result = down_own[:, at] + near[:, at].astype(f32)
+    first = firsts[0].shape[2]
+
+    def total(result, lane, size):
+        result = result + near[:, lane : lane + size].astype(f32)
         for j in range(far):
-            result = result + downs[j][core, :, at].astype(f32)
-            result = result + others[j * pieces + n][:, :size].astype(f32)
-        down_out[0, :, at] = result
+            if lane < first:
+                result = result + firsts[j][core].astype(f32) + others[j][...].astype(f32)
+            else:
+                at = slice(lane - first, lane - first + size)
+                result = result + seconds[j][core, :, at].astype(f32) + others[far + j][:, at].astype(f32)
+        return result
+
+    down_out[0, :, :first] = total(down_own[:, :first], 0, first)
+    down_out[0, :, first:] = total(down_own[:, first:], first, width - first)
     for n in range(rank // down_block):
         at = slice(n * down_block, (n + 1) * down_block)
-        result = up_own[at, :] + near[:, width + n * block : width + (n + 1) * block].astype(f32)
-        lane = size + n // pieces * block
-        for j in range(far):
-            result = result + ups[j][core, at, :].astype(f32)
-            result = result + others[j * pieces + n % pieces][:, lane : lane + block].astype(f32)
-        up_out[0, at, :] = result
+        up_out[0, at, :] = total(up_own[at, :], width + n * block, block)
 
 
 def shards(
@@ -342,6 +346,7 @@
         return lax.ppermute(value, ("dp", "tensor"), pairs)
 
     far = dps // 2 - 1
+    first = width * 14 // 16
     block = ranks // dps
     column_block = kv_width // (dps * tensors)
     group = max(column_block, lanes)
@@ -365,7 +370,7 @@
         out_specs=whole_vmem(len(payload_shapes) + 2),
         scratch_shapes=[pltpu.SMEM(trial_row_index.shape, jnp.int32)]
         + [pltpu.VMEM(value.shape, value.dtype) for value in pick_operands[1:5]]
-        + [pltpu.VMEM((trials * select, features), f32), pltpu.SemaphoreType.DMA((7,))],
+        + [pltpu.SemaphoreType.DMA((7,))],
         compiler_params=params(32),
         name="pick",
     )(*[pltpu.with_memory_space_constraint(value, pltpu.HBM) for value in pick_operands])
@@ -377,22 +382,27 @@
     other = [to_core(value) for value in mine]
     downs = [*downs, *[to_core(value) for value in downs]]
 
-    rows, turned, rank_term, *terms = pl.pallas_call(
+    pair, turned, *terms = pl.pallas_call(
         functools.partial(term_kernel, trials, ys, dps, select, width),
-        out_shape=[shape((tokens, width), bf16), shape((ranks, tokens), bf16), shape((tokens, ranks), f32)]
-        + [shape((2, block, width), bf16)] * far,
-        in_specs=whole_vmem(2 * trials * ys + 4),
-        out_specs=whole_vmem(3 + far),
-        scratch_shapes=[
-            pltpu.VMEM((2, tokens, width), bf16),
-            pltpu.VMEM((tokens, ranks), bf16),
-            pltpu.VMEM((ranks, tokens), f32),
-        ],
+        out_shape=[shape((2, tokens, width), bf16), shape((ranks, tokens), bf16)]
+        + [shape((2, block, first), bf16)] * far,
+        in_specs=whole_vmem(2 * trials * ys),
+        out_specs=whole_vmem(2 + far),
+        scratch_shapes=[pltpu.VMEM((tokens, ranks), bf16), pltpu.VMEM((ranks, tokens), f32)],
         compiler_params=params(16),
         cost_estimate=cost(2 * 10**10, 2 * 10**7),
         name="terms",
-    )(*mine, *other, *downs)
+    )(*mine, *other)
     down_far = [far_dp(j, terms[j]) for j in range(far)]
+    rank_term = pl.pallas_call(
+        rank_kernel,
+        out_shape=shape((tokens, ranks), f32),
+        in_specs=whole_vmem(5),
+        out_specs=pl.BlockSpec(memory_space=pltpu.VMEM),
+        compiler_params=params(4),
+        cost_estimate=cost(0, 0),
+        name="rank",
+    )(pair, *downs)
     rank_sums = [rank_term] + [over("tensor", tensors, 2 * b, rank_term) for b in range(1, ys)]
 
     base_terms = pl.pallas_call(
@@ -404,7 +414,7 @@
         compiler_params=params(8),
         cost_estimate=cost(0, 0),
         name="base",
-    )(rows, keyvalue_weight)
+    )(pair, keyvalue_weight)
     kept = base_terms[:ys]
     came = [None] * ys
     for b in [*range(1, ys), 0]:
@@ -422,21 +432,22 @@
         )(kept[b], came[b])
         base_sums.append(over("tensor", tensors, 2 * b, paired))
 
+    up_lanes = ranks // 2 // block * column_block
     down_own, up_own, near, *up_far = pl.pallas_call(
         functools.partial(up_kernel, trials, ys, dps, select, column_block),
         out_shape=[
             shape((block, width), f32),
             shape((ranks // 2, column_block), f32),
-            shape((block, width + ranks // 2 // block * column_block), bf16),
+            shape((block, width + up_lanes), bf16),
         ]
-        + [shape((2, ranks // 2, column_block), bf16)] * far,
+        + [shape((2, block, width - first + up_lanes), bf16)] * far,
         in_specs=whole_vmem(3 * ys + 2),
         out_specs=whole_vmem(3 + far),
         scratch_shapes=[pltpu.VMEM((2, tokens, dps * group), bf16), pltpu.VMEM((2, ranks, dps * group), f32)],
         compiler_params=params(8),
         cost_estimate=cost(0, 0),
         name="up_terms",
-    )(*rank_sums, *mine[:ys], *other[:ys], rows, turned)
+    )(*rank_sums, *mine[:ys], *other[:ys], pair, turned)
     near = over("dp", dps, 1, near)
     up_far = [far_dp(j, up_far[j]) for j in range(far)]
     output = pl.pallas_call(
@@ -448,25 +459,23 @@
         cost_estimate=cost(0, 0),
         name="output",
     )(*rank_sums, *base_sums, adapter_up_weight)
-    pieces = 2
-    up_lanes = ranks // 2 // block // pieces * column_block
     others = []
-    for down_value, up_value in zip(down_far, up_far):
-        parts = pl.pallas_call(
-            functools.partial(split_kernel, pieces),
-            out_shape=[shape((block, width // pieces + up_lanes), bf16)] * pieces,
-            in_specs=whole_vmem(3),
-            out_specs=whole_vmem(pieces),
+    for value, after in [(value, []) for value in down_far] + [(value, [near]) for value in up_far]:
+        part = pl.pallas_call(
+            split_kernel,
+            out_shape=shape((block, max(value.shape[2], width // 2)), bf16),
+            in_specs=whole_vmem(1 + len(after)),
+            out_specs=pl.BlockSpec(memory_space=pltpu.VMEM),
             compiler_params=params(4),
             cost_estimate=cost(0, 0),
             name="split",
-        )(down_value, up_value, near)
-        others += [to_core(part) for part in parts]
+        )(value, *after)
+        others.append(to_core(part))
 
     grad_a, grad_b = pl.pallas_call(
-        functools.partial(sum_kernel, far, pieces),
+        functools.partial(sum_kernel, far),
         out_shape=[shape((1, block, width), f32), shape((1, ranks // 2, column_block), f32)],
-        in_specs=whole_vmem(3 + (2 + pieces) * far),
+        in_specs=whole_vmem(3 + 4 * far),
         out_specs=whole_vmem(2),
         compiler_params=params(8),
         cost_estimate=cost(0, 0),

time: 35.7 us -> 35.1 us (0.983)
    ppermute x2, waiting for transfers between devices: 5.57 us -> 4.91 us  [far_dp(): return lax.ppermute(value, ('dp', 'tensor'), pairs)]
    ppermute x6, waiting for transfers between devices: 7.86 us -> 8.37 us  [over(): return lax.ppermute(value, axis, [(i, i ^ mask) for i in range(size)])]
    pallas_call x2 -> x4, Pallas kernels: 0.78 us -> 1.2 us  [the longest x1 0.76 us: shards(): pl.pallas_call(functools.partial(sum_kernel, far), out_shape=[shape((1, b...]
  transfers between devices with their start and end apart: 18 -> 18, of which waited for: 8 -> 8; matrix products, arithmetic and copies ran while one was open for 0% -> 0% of each run, Pallas kernels for 8% -> 10%
where the time goes in v3:
time: 35.1 us; the launch traced here: 35 us
  waiting for transfers between devices  14.3 us (41%)
  starting transfers between devices  13.9 us (40%)
  Pallas kernels  6.04 us (17%)
  between operations  0.74 us (2%)
    ppermute x6, starting transfers between devices, over(): return lax.ppermute(value, axis, [(i, i ^ mask) for i in range(size)])  8.75 us
    ppermute x6, waiting for transfers between devices, over(): return lax.ppermute(value, axis, [(i, i ^ mask) for i in range(size)])  8.37 us
    ppermute x2, waiting for transfers between devices, far_dp(): return lax.ppermute(value, ('dp', 'tensor'), pairs)  4.91 us
    ppermute x2, starting transfers between devices, far_dp(): return lax.ppermute(value, ('dp', 'tensor'), pairs)  3.21 us
    ppermute x10, starting transfers between devices, to_core(): return lax.ppermute(value, 'tensor', [(i, i ^ 1) for i in range(tensors)])  1.93 us
    pallas_call x1, Pallas kernels, shards(): pl.pallas_call(functools.partial(pick_kernel, trials, ys, dps, select, wi...  1.66 us
    pallas_call x1, Pallas kernels, shards(): pl.pallas_call(functools.partial(base_kernel, ys), out_shape=[shape((loca...  1.35 us
    ppermute x10, waiting for transfers between devices, to_core(): return lax.ppermute(value, 'tensor', [(i, i ^ 1) for i in range(tensors)])  1 us
  transfers between devices with their start and end apart: 18, of which 8 were waited for; matrix products, arithmetic and copies ran while one was open for 0% of the time, Pallas kernels for 10%

profile of v3, /device:TPU:0, one launch (start us, length us, event | category | flops | bytes accessed | tf_op | source)
XLA Modules:
  0.0 35.0 jit_solution(12370058997929642868)
XLA Ops:
  0.6 1.7 %pick.1 = (bf16[2,16,3200]{2,1,0:T(8,128)(2,1)S(1)}, bf16[2,16,3200]{2,1,0:T(8,128)(2,1)S(1)}, bf16[2,16,2048]{2,1,0:T(8,128)(2,1)S(1)}, bf16[2,16,2048]{2,1,0:T...) custom-call(s32[2,128]{1,0:T(2,128)} %index_hbm.1, bf16[32,8192]{1,0:T(8,128)(2,1)} %rows_hbm.1, ...), custom_call_target="tpu_custom_call" | custom-call | tf_op jit(solution)/shard_map/pick/pallas_call | solution.py:366
  2.3 3.0 %collective-permute-start = (bf16[2,16,3200]{2,1,0:T(8,128)(2,1)S(1)}, bf16[2,16,3200]{2,1,0:T(8,128)(2,1)S(1)}, u32[]{:S(2)}, u32[]{:S(2)}) collective-permute-start(bf16[2,16,3200]{2,1,0:T(8,128)(2,1)S(1)} %get-tuple-element.23), channel_id=1, source_target_pairs={{0,2},{1,3},{2,0},{3,1},{16,18},{17,19},{18,16},{19,17},{4,6},{5,7... | collective-permute-start | bytes 614408 | tf_op jit(solution)/shard_map/ppermute | solution.py:338
  5.3 1.5 %collective-permute-start.1 = (bf16[2,16,2048]{2,1,0:T(8,128)(2,1)S(1)}, bf16[2,16,2048]{2,1,0:T(8,128)(2,1)S(1)}, u32[]{:S(2)}, u32[]{:S(2)}) collective-permute-start(bf16[2,16,2048]{2,1,0:T(8,128)(2,1)S(1)} %get-tuple-element.24), channel_id=1, source_target_pairs={{0,16},{1,17},{2,18},{3,19},{16,0},{17,1},{18,2},{19,3},{4,20},{5,... | collective-permute-start | bytes 393224 | tf_op jit(solution)/shard_map/ppermute | solution.py:338
  6.8 0.1 collective-permute-start.2
  6.9 0.0 collective-permute-start.3
  6.9 6.3 %collective-permute-done.refs_1_.refs_3_ = bf16[2,16,3200]{2,1,0:T(8,128)(2,1)S(1)} collective-permute-done((bf16[2,16,3200]{2,1,0:T(8,128)(2,1)S(1)}, bf16[2,16,3200]{2,1,0:T(8,128)(2,1)S(1)}, u32[]{:S(2)}, u32[]{:S(2)}) %collective-permute-start) | collective-permute-done | bytes 204832 | tf_op jit(solution)/shard_map/ppermute | solution.py:338
  13.2 0.5 %collective-permute-start.5 = (bf16[2,16,2048]{2,1,0:T(8,128)(2,1)S(1)}, bf16[2,16,2048]{2,1,0:T(8,128)(2,1)S(1)}, u32[]{:S(2)}, u32[]{:S(2)}) collective-permute-start(bf16[2,16,2048]{2,1,0:T(8,128)(2,1)S(1)} %collective-permute-done.1.refs_2_), channel_id=1, source_target_pairs={{0,1},{1,0},{2,3},{3,2},{4,5},{5,4},{6,7},{7,6},{8,9},{9,8},{10,11... | collective-permute-start | bytes 393224 | tf_op jit(solution)/shard_map/ppermute | solution.py:335
  13.7 0.0 collective-permute-done.2.refs_3_
  13.7 0.1 collective-permute-start.6
  13.8 0.4 %collective-permute-start.7 = (bf16[1,1024,128]{2,1,0:T(8,128)(2,1)S(1)}, bf16[1,1024,128]{2,1,0:T(8,128)(2,1)S(1)}, u32[]{:S(2)}, u32[]{:S(2)}) collective-permute-start(bf16[1,1024,128]{2,1,0:T(8,128)(2,1)S(1)} %get-tuple-element.27.refs_0_), channel_id=1, source_target_pairs={{0,1},{1,0},{2,3},{3,2},{4,5},{5,4},{6,7},{7,6},{8,9},{9,8},{10,11... | collective-permute-start | bytes 786440 | tf_op jit(solution)/shard_map/ppermute | solution.py:335
  14.3 0.1 collective-permute-start.8
  14.4 0.5 %collective-permute-done.5.refs_6_ = bf16[2,16,2048]{2,1,0:T(8,128)(2,1)S(1)} collective-permute-done((bf16[2,16,2048]{2,1,0:T(8,128)(2,1)S(1)}, bf16[2,16,2048]{2,1,0:T(8,128)(2,1)S(1)}, u32[]{:S(2)}, u32[]{:S(2)}) %collective-permute-start.5) | collective-permute-done | bytes 131104 | tf_op jit(solution)/shard_map/ppermute | solution.py:335
  14.9 0.2 collective-permute-done.6.refs_7_
  15.1 0.4 %terms.1 = (bf16[2,128,2048]{2,1,0:T(8,128)(2,1)S(1)}, bf16[128,128]{1,0:T(8,128)(2,1)S(1)}, bf16[2,32,1792]{2,1,0:T(8,128)(2,1)S(1)}) custom-call(bf16[2,16,3200]{2,1,0:T(8,128)(2,1)S(1)} %get-tuple-element.22.refs_0_.refs_2_, bf16[2,16,3200]{2,1,0:T(8,128)(2,1)S(1)} %collective-permute-done.refs_1_.refs_3_, ...), custom_call_target="tpu_custom_call" | custom-call | flops 20000000000 | bytes 20000000 | tf_op jit(solution)/shard_map/terms/pallas_call | solution.py:385
  15.5 0.0 copy-start
  15.5 2.9 %collective-permute-start.14 = (bf16[2,32,1792]{2,1,0:T(8,128)(2,1)S(1)}, bf16[2,32,1792]{2,1,0:T(8,128)(2,1)S(1)}, u32[]{:S(2)}, u32[]{:S(2)}) collective-permute-start(bf16[2,32,1792]{2,1,0:T(8,128)(2,1)S(1)} %get-tuple-element.37), channel_id=1, source_target_pairs={{0,8},{1,13},{2,10},{3,15},{4,12},{5,9},{6,14},{7,11},{8,0},{9,5},... | collective-permute-start | bytes 688136 | tf_op jit(solution)/shard_map/ppermute | solution.py:346
  18.3 0.4 %rank.1.refs_0_ = f32[128,128]{1,0:T(8,128)S(1)} custom-call(bf16[2,128,2048]{2,1,0:T(8,128)(2,1)S(1)} %get-tuple-element.26.pair.refs_6_, bf16[1,1024,128]{2,1,0:T(8,128)(2,1)S(1)} %get-tuple-element.27.refs_0_, bf16[1,1024,128]{2,1,0:T(8,128)(2,1)S(1)} %get-tuple-element.28.refs_1_, bf16[1,1024,128]{2,1,0:T(8,128)(2,1)S(1)} %collective-permute-done.7.refs_2_, ...), custom_call_target="tpu_custom_call" | custom-call | tf_op jit(solution)/shard_map/rank/pallas_call | solution.py:397
  18.8 1.6 %collective-permute-start.9 = (f32[128,128]{1,0:T(8,128)S(1)}, f32[128,128]{1,0:T(8,128)S(1)}, u32[]{:S(2)}, u32[]{:S(2)}) collective-permute-start(f32[128,128]{1,0:T(8,128)S(1)} %rank.1.refs_0_), channel_id=1, source_target_pairs={{0,2},{1,3},{2,0},{3,1},{4,6},{5,7},{6,4},{7,5},{8,10},{9,11},{10,... | collective-permute-start | bytes 196616 | tf_op jit(solution)/shard_map/ppermute | solution.py:338
  20.4 1.4 %base.1 = (f32[32,2048]{1,0:T(8,128)S(1)}, f32[32,2048]{1,0:T(8,128)S(1)}, bf16[32,2048]{1,0:T(8,128)(2,1)S(1)}, bf16[32,2048]{1,0:T(8,128)(2,1)S(1)}) custom-call(bf16[2,128,2048]{2,1,0:T(8,128)(2,1)S(1)} %get-tuple-element.26.pair.refs_6_, bf16[2048,2048]{1,0:T(8,128)(2,1)S(1)} %bitcast.2), custom_call_target="tpu_custom_call" | custom-call | tf_op jit(solution)/shard_map/base/pallas_call | solution.py:408
  21.7 0.7 %collective-permute-start.11 = (bf16[32,2048]{1,0:T(8,128)(2,1)S(1)}, bf16[32,2048]{1,0:T(8,128)(2,1)S(1)}, u32[]{:S(2)}, u32[]{:S(2)}) collective-permute-start(bf16[32,2048]{1,0:T(8,128)(2,1)S(1)} %get-tuple-element.32), channel_id=1, source_target_pairs={{0,1},{1,0},{2,3},{3,2},{4,5},{5,4},{6,7},{7,6},{8,9},{9,8},{10,11... | collective-permute-start | bytes 393224 | tf_op jit(solution)/shard_map/ppermute | solution.py:335
  22.4 1.3 %collective-permute-done.9.refs_1_ = f32[128,128]{1,0:T(8,128)S(1)} collective-permute-done((f32[128,128]{1,0:T(8,128)S(1)}, f32[128,128]{1,0:T(8,128)S(1)}, u32[]{:S(2)}, u32[]{:S(2)}) %collective-permute-start.9) | collective-permute-done | bytes 65568 | tf_op jit(solution)/shard_map/ppermute | solution.py:338
  23.8 0.5 %up_terms.1 = (f32[32,2048]{1,0:T(8,128)S(1)}, f32[64,128]{1,0:T(8,128)S(1)}, bf16[32,2304]{1,0:T(8,128)(2,1)S(1)}, bf16[2,32,512]{2,1,0:T(8,128)(2,1)S(1)}) custom-call(f32[128,128]{1,0:T(8,128)S(1)} %rank.1.refs_0_, f32[128,128]{1,0:T(8,128)S(1)} %collective-permute-done.9.refs_1_, bf16[2,16,3200]{2,1,0:T(8,128)(2,1)S(1)} %get-tuple-element.22.refs_0_.refs_2_, ...), custom_call_target="tpu_custom_call" | custom-call | tf_op jit(solution)/shard_map/up_terms/pallas_call | solution.py:436
  24.3 1.0 %collective-permute-start.13 = (bf16[32,2304]{1,0:T(8,128)(2,1)S(1)}, bf16[32,2304]{1,0:T(8,128)(2,1)S(1)}, u32[]{:S(2)}, u32[]{:S(2)}) collective-permute-start(bf16[32,2304]{1,0:T(8,128)(2,1)S(1)} %get-tuple-element.36), channel_id=1, source_target_pairs={{0,4},{4,0},{8,12},{12,8},{1,5},{5,1},{9,13},{13,9},{2,6},{6,2},{1... | collective-permute-start | bytes 442376 | tf_op jit(solution)/shard_map/ppermute | solution.py:338
  25.2 0.3 collective-permute-start.15
  25.6 1.6 %collective-permute-start.12 = (bf16[32,2048]{1,0:T(8,128)(2,1)S(1)}, bf16[32,2048]{1,0:T(8,128)(2,1)S(1)}, u32[]{:S(2)}, u32[]{:S(2)}) collective-permute-start(bf16[32,2048]{1,0:T(8,128)(2,1)S(1)} %pair.1), channel_id=1, source_target_pairs={{0,2},{1,3},{2,0},{3,1},{4,6},{5,7},{6,4},{7,5},{8,10},{9,11},{10,... | collective-permute-start | bytes 393224 | tf_op jit(solution)/shard_map/ppermute | solution.py:338
  27.2 2.5 %collective-permute-done.14.refs_0_.refs_3_ = bf16[2,32,1792]{2,1,0:T(8,128)(2,1)S(1)} collective-permute-done((bf16[2,32,1792]{2,1,0:T(8,128)(2,1)S(1)}, bf16[2,32,1792]{2,1,0:T(8,128)(2,1)S(1)}, u32[]{:S(2)}, u32[]{:S(2)}) %collective-permute-start.14) | collective-permute-done | bytes 229408 | tf_op jit(solution)/shard_map/ppermute | solution.py:346
  29.8 0.1 collective-permute-start.16
  29.8 2.4 %collective-permute-done.15.refs_0_.refs_4_ = bf16[2,32,512]{2,1,0:T(8,128)(2,1)S(1)} collective-permute-done((bf16[2,32,512]{2,1,0:T(8,128)(2,1)S(1)}, bf16[2,32,512]{2,1,0:T(8,128)(2,1)S(1)}, u32[]{:S(2)}, u32[]{:S(2)}) %collective-permute-start.15) | collective-permute-done | bytes 65568 | tf_op jit(solution)/shard_map/ppermute | solution.py:346
  32.2 0.7 %collective-permute-done.13.refs_1_.refs_2_ = bf16[32,2304]{1,0:T(8,128)(2,1)S(1)} collective-permute-done((bf16[32,2304]{1,0:T(8,128)(2,1)S(1)}, bf16[32,2304]{1,0:T(8,128)(2,1)S(1)}, u32[]{:S(2)}, u32[]{:S(2)}) %collective-permute-start.13) | collective-permute-done | bytes 147488 | tf_op jit(solution)/shard_map/ppermute | solution.py:338
  33.0 0.9 %output.1 = f32[1,32,2048]{2,1,0:T(8,128)} custom-call(f32[128,128]{1,0:T(8,128)S(1)} %rank.1.refs_0_, f32[128,128]{1,0:T(8,128)S(1)} %collective-permute-done.9.refs_1_, f32[32,2048]{1,0:T(8,128)S(1)} %get-tuple-element.29.refs_2_, bf16[32,2048]{1,0:T(8,128)(2,1)S(1)} %collective-permute-done.10.refs_3_, ...), custom_call_target="tpu_custom_call" | custom-call | tf_op jit(solution)/shard_map/output/pallas_call | solution.py:453
  33.9 0.3 collective-permute-done.17.refs_6_
  34.2 0.8 %sums.1 = (f32[1,32,2048]{2,1,0:T(8,128)}, f32[1,64,128]{2,1,0:T(8,128)}) custom-call(f32[32,2048]{1,0:T(8,128)S(1)} %get-tuple-element.34.refs_0_, f32[64,128]{1,0:T(8,128)S(1)} %get-tuple-element.35.refs_1_, bf16[32,2304]{1,0:T(8,128)(2,1)S(1)} %collective-permute-done.13.refs_1_.refs_2_, bf16[2,32,1792]{2,1,0:T(8,128)(2,1)S(1)} %collective-permute-done.14.refs_0_.refs_3_, ...), custom_call_target="tpu_custom_call" | custom-call | tf_op jit(solution)/shard_map/sums/pallas_call | solution.py:475
  (21 shorter events, 0.1 us)
Async XLA Ops:
  2.3 10.9 %collective-permute-start = (bf16[2,16,3200]{2,1,0:T(8,128)(2,1)S(1)}, bf16[2,16,3200]{2,1,0:T(8,128)(2,1)S(1)}, u32[]{:S(2)}, u32[]{:S(2)}) collective-permute-start(bf16[2,16,3200]{2,1,0:T(8,128)(2,1)S(1)} %get-tuple-element.23), channel_id=1, source_target_pairs={{0,2},{1,3},{2,0},{3,1},{16,18},{17,19},{18,16},{19,17},{4,6},{5,7... | collective-permute-start | bytes 614408 | tf_op jit(solution)/shard_map/ppermute | solution.py:338
  5.3 7.9 %collective-permute-start.1 = (bf16[2,16,2048]{2,1,0:T(8,128)(2,1)S(1)}, bf16[2,16,2048]{2,1,0:T(8,128)(2,1)S(1)}, u32[]{:S(2)}, u32[]{:S(2)}) collective-permute-start(bf16[2,16,2048]{2,1,0:T(8,128)(2,1)S(1)} %get-tuple-element.24), channel_id=1, source_target_pairs={{0,16},{1,17},{2,18},{3,19},{16,0},{17,1},{18,2},{19,3},{4,20},{5,... | collective-permute-start | bytes 393224 | tf_op jit(solution)/shard_map/ppermute | solution.py:338
  6.8 6.9 %collective-permute-start.2 = (bf16[2,16,2048]{2,1,0:T(8,128)(2,1)S(1)}, bf16[2,16,2048]{2,1,0:T(8,128)(2,1)S(1)}, u32[]{:S(2)}, u32[]{:S(2)}) collective-permute-start(bf16[2,16,2048]{2,1,0:T(8,128)(2,1)S(1)} %get-tuple-element.25), channel_id=1, source_target_pairs={{0,18},{1,19},{2,16},{3,17},{16,2},{17,3},{18,0},{19,1},{4,22},{5,... | collective-permute-start | bytes 393224 | tf_op jit(solution)/shard_map/ppermute | solution.py:338
  6.9 7.4 %collective-permute-start.3 = (bf16[2,16,3200]{2,1,0:T(8,128)(2,1)S(1)}, bf16[2,16,3200]{2,1,0:T(8,128)(2,1)S(1)}, u32[]{:S(2)}, u32[]{:S(2)}) collective-permute-start(bf16[2,16,3200]{2,1,0:T(8,128)(2,1)S(1)} %get-tuple-element.22.refs_0_.refs_2_), channel_id=1, source_target_pairs={{0,1},{1,0},{2,3},{3,2},{4,5},{5,4},{6,7},{7,6},{8,9},{9,8},{10,11... | collective-permute-start | bytes 614408 | tf_op jit(solution)/shard_map/ppermute | solution.py:335
  13.2 1.9 %collective-permute-start.4 = (bf16[2,16,3200]{2,1,0:T(8,128)(2,1)S(1)}, bf16[2,16,3200]{2,1,0:T(8,128)(2,1)S(1)}, u32[]{:S(2)}, u32[]{:S(2)}) collective-permute-start(bf16[2,16,3200]{2,1,0:T(8,128)(2,1)S(1)} %collective-permute-done.refs_1_.refs_3_), channel_id=1, source_target_pairs={{0,1},{1,0},{2,3},{3,2},{4,5},{5,4},{6,7},{7,6},{8,9},{9,8},{10,11... | collective-permute-start | bytes 614408 | tf_op jit(solution)/shard_map/ppermute | solution.py:335
  13.2 1.6 %collective-permute-start.5 = (bf16[2,16,2048]{2,1,0:T(8,128)(2,1)S(1)}, bf16[2,16,2048]{2,1,0:T(8,128)(2,1)S(1)}, u32[]{:S(2)}, u32[]{:S(2)}) collective-permute-start(bf16[2,16,2048]{2,1,0:T(8,128)(2,1)S(1)} %collective-permute-done.1.refs_2_), channel_id=1, source_target_pairs={{0,1},{1,0},{2,3},{3,2},{4,5},{5,4},{6,7},{7,6},{8,9},{9,8},{10,11... | collective-permute-start | bytes 393224 | tf_op jit(solution)/shard_map/ppermute | solution.py:335
  13.7 1.3 %collective-permute-start.6 = (bf16[2,16,2048]{2,1,0:T(8,128)(2,1)S(1)}, bf16[2,16,2048]{2,1,0:T(8,128)(2,1)S(1)}, u32[]{:S(2)}, u32[]{:S(2)}) collective-permute-start(bf16[2,16,2048]{2,1,0:T(8,128)(2,1)S(1)} %collective-permute-done.2.refs_3_), channel_id=1, source_target_pairs={{0,1},{1,0},{2,3},{3,2},{4,5},{5,4},{6,7},{7,6},{8,9},{9,8},{10,11... | collective-permute-start | bytes 393224 | tf_op jit(solution)/shard_map/ppermute | solution.py:335
  13.8 4.5 %collective-permute-start.7 = (bf16[1,1024,128]{2,1,0:T(8,128)(2,1)S(1)}, bf16[1,1024,128]{2,1,0:T(8,128)(2,1)S(1)}, u32[]{:S(2)}, u32[]{:S(2)}) collective-permute-start(bf16[1,1024,128]{2,1,0:T(8,128)(2,1)S(1)} %get-tuple-element.27.refs_0_), channel_id=1, source_target_pairs={{0,1},{1,0},{2,3},{3,2},{4,5},{5,4},{6,7},{7,6},{8,9},{9,8},{10,11... | collective-permute-start | bytes 786440 | tf_op jit(solution)/shard_map/ppermute | solution.py:335
  14.2 6.1 %slice-start = ((s8[8388608]{0:T(1024)(128)(4,1)}), s8[4194304]{0:T(1024)(128)(4,1)S(1)}, s32[]{:S(2)}) async-start(s8[8388608]{0:T(1024)(128)(4,1)} %bitcast.1), calls=%async_computation | async-start | bytes 8388608
  14.3 6.1 %slice-start.1 = ((s8[8388608]{0:T(1024)(128)(4,1)}), s8[4194304]{0:T(1024)(128)(4,1)S(1)}, s32[]{:S(2)}) async-start(s8[8388608]{0:T(1024)(128)(4,1)} %bitcast.1), calls=%async_computation.1 | async-start | bytes 8388608
  14.3 4.1 %collective-permute-start.8 = (bf16[1,1024,128]{2,1,0:T(8,128)(2,1)S(1)}, bf16[1,1024,128]{2,1,0:T(8,128)(2,1)S(1)}, u32[]{:S(2)}, u32[]{:S(2)}) collective-permute-start(bf16[1,1024,128]{2,1,0:T(8,128)(2,1)S(1)} %get-tuple-element.28.refs_1_), channel_id=1, source_target_pairs={{0,1},{1,0},{2,3},{3,2},{4,5},{5,4},{6,7},{7,6},{8,9},{9,8},{10,11... | collective-permute-start | bytes 786440 | tf_op jit(solution)/shard_map/ppermute | solution.py:335
  15.5 17.5 %copy-start = (bf16[1,64,2048]{2,1,0:T(8,128)(2,1)S(1)}, bf16[1,64,2048]{2,1,0:T(8,128)(2,1)}, u32[]{:S(2)}) copy-start(bf16[1,64,2048]{2,1,0:T(8,128)(2,1)} %refs_5_.1) | copy-start | bytes 786436
  15.5 14.3 %collective-permute-start.14 = (bf16[2,32,1792]{2,1,0:T(8,128)(2,1)S(1)}, bf16[2,32,1792]{2,1,0:T(8,128)(2,1)S(1)}, u32[]{:S(2)}, u32[]{:S(2)}) collective-permute-start(bf16[2,32,1792]{2,1,0:T(8,128)(2,1)S(1)} %get-tuple-element.37), channel_id=1, source_target_pairs={{0,8},{1,13},{2,10},{3,15},{4,12},{5,9},{6,14},{7,11},{8,0},{9,5},... | collective-permute-start | bytes 688136 | tf_op jit(solution)/shard_map/ppermute | solution.py:346
  18.8 5.0 %collective-permute-start.9 = (f32[128,128]{1,0:T(8,128)S(1)}, f32[128,128]{1,0:T(8,128)S(1)}, u32[]{:S(2)}, u32[]{:S(2)}) collective-permute-start(f32[128,128]{1,0:T(8,128)S(1)} %rank.1.refs_0_), channel_id=1, source_target_pairs={{0,2},{1,3},{2,0},{3,1},{4,6},{5,7},{6,4},{7,5},{8,10},{9,11},{10,... | collective-permute-start | bytes 196616 | tf_op jit(solution)/shard_map/ppermute | solution.py:338
  21.7 3.9 %collective-permute-start.11 = (bf16[32,2048]{1,0:T(8,128)(2,1)S(1)}, bf16[32,2048]{1,0:T(8,128)(2,1)S(1)}, u32[]{:S(2)}, u32[]{:S(2)}) collective-permute-start(bf16[32,2048]{1,0:T(8,128)(2,1)S(1)} %get-tuple-element.32), channel_id=1, source_target_pairs={{0,1},{1,0},{2,3},{3,2},{4,5},{5,4},{6,7},{7,6},{8,9},{9,8},{10,11... | collective-permute-start | bytes 393224 | tf_op jit(solution)/shard_map/ppermute | solution.py:335
  24.3 8.7 %collective-permute-start.13 = (bf16[32,2304]{1,0:T(8,128)(2,1)S(1)}, bf16[32,2304]{1,0:T(8,128)(2,1)S(1)}, u32[]{:S(2)}, u32[]{:S(2)}) collective-permute-start(bf16[32,2304]{1,0:T(8,128)(2,1)S(1)} %get-tuple-element.36), channel_id=1, source_target_pairs={{0,4},{4,0},{8,12},{12,8},{1,5},{5,1},{9,13},{13,9},{2,6},{6,2},{1... | collective-permute-start | bytes 442376 | tf_op jit(solution)/shard_map/ppermute | solution.py:338
  25.2 7.7 %collective-permute-start.10 = (bf16[32,2048]{1,0:T(8,128)(2,1)S(1)}, bf16[32,2048]{1,0:T(8,128)(2,1)S(1)}, u32[]{:S(2)}, u32[]{:S(2)}) collective-permute-start(bf16[32,2048]{1,0:T(8,128)(2,1)S(1)} %get-tuple-element.30), channel_id=1, source_target_pairs={{0,1},{1,0},{2,3},{3,2},{4,5},{5,4},{6,7},{7,6},{8,9},{9,8},{10,11... | collective-permute-start | bytes 393224 | tf_op jit(solution)/shard_map/ppermute | solution.py:335
  25.2 7.0 %collective-permute-start.15 = (bf16[2,32,512]{2,1,0:T(8,128)(2,1)S(1)}, bf16[2,32,512]{2,1,0:T(8,128)(2,1)S(1)}, u32[]{:S(2)}, u32[]{:S(2)}) collective-permute-start(bf16[2,32,512]{2,1,0:T(8,128)(2,1)S(1)} %get-tuple-element.38), channel_id=1, source_target_pairs={{0,8},{1,13},{2,10},{3,15},{4,12},{5,9},{6,14},{7,11},{8,0},{9,5},... | collective-permute-start | bytes 196616 | tf_op jit(solution)/shard_map/ppermute | solution.py:346
  25.6 7.3 %collective-permute-start.12 = (bf16[32,2048]{1,0:T(8,128)(2,1)S(1)}, bf16[32,2048]{1,0:T(8,128)(2,1)S(1)}, u32[]{:S(2)}, u32[]{:S(2)}) collective-permute-start(bf16[32,2048]{1,0:T(8,128)(2,1)S(1)} %pair.1), channel_id=1, source_target_pairs={{0,2},{1,3},{2,0},{3,1},{4,6},{5,7},{6,4},{7,5},{8,10},{9,11},{10,... | collective-permute-start | bytes 393224 | tf_op jit(solution)/shard_map/ppermute | solution.py:338
  29.8 4.4 %collective-permute-start.16 = (bf16[32,1792]{1,0:T(8,128)(2,1)S(1)}, bf16[32,1792]{1,0:T(8,128)(2,1)S(1)}, u32[]{:S(2)}, u32[]{:S(2)}) collective-permute-start(bf16[32,1792]{1,0:T(8,128)(2,1)S(1)} %split.2), channel_id=1, source_target_pairs={{0,1},{1,0},{2,3},{3,2},{4,5},{5,4},{6,7},{7,6},{8,9},{9,8},{10,11... | collective-permute-start | bytes 344072 | tf_op jit(solution)/shard_map/ppermute | solution.py:335
  32.9 1.3 %collective-permute-start.17 = (bf16[32,1024]{1,0:T(8,128)(2,1)S(1)}, bf16[32,1024]{1,0:T(8,128)(2,1)S(1)}, u32[]{:S(2)}, u32[]{:S(2)}) collective-permute-start(bf16[32,1024]{1,0:T(8,128)(2,1)S(1)} %split.3), channel_id=1, source_target_pairs={{0,1},{1,0},{2,3},{3,2},{4,5},{5,4},{6,7},{7,6},{8,9},{9,8},{10,11... | collective-permute-start | bytes 196616 | tf_op jit(solution)/shard_map/ppermute | solution.py:335

commit v4 on v3

--- a/solution.py
+++ b/solution.py
@@ -44,9 +44,9 @@
 
 
 def pick_kernel(trials, ys, dps, select, width, column_block, index_hbm, rows_hbm, gain_hbm, grad_hbm, up_hbm, down_hbm, *rest):
-    outs, rest = rest[: trials * ys], rest[trials * ys :]
-    downs = rest[:2]
-    index_ref, rows_ref, gain_ref, grad_ref, up_ref, sems = rest[2:]
+    outs, rest = rest[:ys], rest[ys:]
+    downs, normed_ref, hot_ref = rest[:2], *rest[2:4]
+    index_ref, rows_ref, gain_ref, grad_ref, up_ref, sems = rest[4:]
     copies = [
         pltpu.make_async_copy(source, target, sems.at[i])
         for i, (source, target) in enumerate(
@@ -77,7 +77,8 @@
         for i in range(select):
             picked = jnp.where(row == i, index_ref[trial ^ a, start + i], picked)
         hots.append(jnp.where(column == picked, 1.0, 0.0).astype(bf16))
-    hot = jnp.concatenate(hots, axis=0)
+    for n in range(1, trials):
+        hot_ref[(n - 1) * select : n * select, :] = hots[n]
     square = jnp.zeros((pool, 1), f32)
     chunk = 1024
     copies[1].wait()
@@ -96,9 +97,10 @@
             for f in range(0, width, chunk):
                 at = pl.multiple_of((y ^ b) * (2 * width) + core * width + f, chunk)
                 part = rows_ref[:, pl.ds(at, chunk)].astype(f32) * scale * gain_ref[:, pl.ds(at, chunk)]
-                part = jnp.dot(hot, part.astype(bf16), preferred_element_type=f32).astype(bf16)
-                for a in range(trials):
-                    outs[a * ys + b][core, :, f : f + chunk] = part[a * select : (a + 1) * select]
+                part = part.astype(bf16)
+                normed_ref[:, pl.ds(at, chunk)] = part
+                part = jnp.dot(hots[0], part, preferred_element_type=f32)
+                outs[b][core, :, f : f + chunk] = part.astype(bf16)
     group = max(column_block, lanes)
     for b in range(ys):
         for j in range(trials // 2):
@@ -116,6 +118,20 @@
                 outs[b][core, :, lane + rank : lane + 2 * rank] = values[at].astype(bf16)
     copies[5].wait()
     copies[6].wait()
+
+
+def others_kernel(trials, ys, select, normed_ref, hot_ref, *outs):
+    y = lax.axis_index("tensor") // 2
+    width = outs[0].shape[2]
+    chunk = 1024
+    for b in range(ys):
+        for core in range(2):
+            for f in range(0, width, chunk):
+                at = pl.multiple_of((y ^ b) * (2 * width) + core * width + f, chunk)
+                part = jnp.dot(hot_ref[...], normed_ref[:, pl.ds(at, chunk)], preferred_element_type=f32)
+                part = part.astype(bf16)
+                for n in range(trials - 1):
+                    outs[n * ys + b][core, :, f : f + chunk] = part[n * select : (n + 1) * select]
 
 
 def term_kernel(trials, ys, dps, select, width, *refs):
@@ -365,16 +381,30 @@
     )
     picked = pl.pallas_call(
         functools.partial(pick_kernel, trials, ys, dps, select, width, column_block),
-        out_shape=payload_shapes + [shape((1, width // 2, ranks), bf16)] * 2,
+        out_shape=payload_shapes[:ys]
+        + [shape((1, width // 2, ranks), bf16)] * 2
+        + [shape((pool, features), bf16), shape(((trials - 1) * select, pool), bf16)],
         in_specs=in_hbm(6),
-        out_specs=whole_vmem(len(payload_shapes) + 2),
+        out_specs=whole_vmem(ys + 4),
         scratch_shapes=[pltpu.SMEM(trial_row_index.shape, jnp.int32)]
         + [pltpu.VMEM(value.shape, value.dtype) for value in pick_operands[1:5]]
         + [pltpu.SemaphoreType.DMA((7,))],
         compiler_params=params(32),
         name="pick",
     )(*[pltpu.with_memory_space_constraint(value, pltpu.HBM) for value in pick_operands])
-    payloads, downs = picked[:-2], picked[-2:]
+    downs = picked[ys : ys + 2]
+    payloads = [
+        *picked[:ys],
+        *pl.pallas_call(
+            functools.partial(others_kernel, trials, ys, select),
+            out_shape=payload_shapes[ys:],
+            in_specs=whole_vmem(2),
+            out_specs=whole_vmem(len(payload_shapes) - ys),
+            compiler_params=params(8),
+            cost_estimate=cost(0, 0),
+            name="pick_others",
+        )(*picked[-2:]),
+    ]
     mine = [payloads[0]] + [None] * (trials * ys - 1)
     for mask in range(1, trials * ys):
         a, b = mask // ys, mask % ys

time: 35.1 us -> 35 us (level)
    ppermute x10, starting transfers between devices: 1.93 us -> 1.37 us  [to_core(): return lax.ppermute(value, 'tensor', [(i, i ^ 1) for i in range(tensors)])]
    ppermute x2, starting transfers between devices: 3.21 us -> 3.74 us  [far_dp(): return lax.ppermute(value, ('dp', 'tensor'), pairs)]
  transfers between devices with their start and end apart: 18 -> 18, of which waited for: 8 -> 9; matrix products, arithmetic and copies ran while one was open for 0% -> 0% of each run, Pallas kernels for 10% -> 11%
where the time goes in v4:
time: 35 us; the launch traced here: 34.9 us
  waiting for transfers between devices  14 us (40%)
  starting transfers between devices  13.9 us (40%)
  Pallas kernels  6.24 us (18%)
  between operations  0.74 us (2%)
    ppermute x6, starting transfers between devices, over(): return lax.ppermute(value, axis, [(i, i ^ mask) for i in range(size)])  8.76 us
    ppermute x6, waiting for transfers between devices, over(): return lax.ppermute(value, axis, [(i, i ^ mask) for i in range(size)])  8.04 us
    ppermute x2, waiting for transfers between devices, far_dp(): return lax.ppermute(value, ('dp', 'tensor'), pairs)  4.92 us
    ppermute x2, starting transfers between devices, far_dp(): return lax.ppermute(value, ('dp', 'tensor'), pairs)  3.74 us
    pallas_call x1, Pallas kernels, shards(): pl.pallas_call(functools.partial(pick_kernel, trials, ys, dps, select, wi...  1.63 us
    ppermute x10, starting transfers between devices, to_core(): return lax.ppermute(value, 'tensor', [(i, i ^ 1) for i in range(tensors)])  1.37 us
    pallas_call x1, Pallas kernels, shards(): pl.pallas_call(functools.partial(base_kernel, ys), out_shape=[shape((loca...  1.37 us
    ppermute x10, waiting for transfers between devices, to_core(): return lax.ppermute(value, 'tensor', [(i, i ^ 1) for i in range(tensors)])  1.04 us
  transfers between devices with their start and end apart: 18, of which 9 were waited for; matrix products, arithmetic and copies ran while one was open for 0% of the time, Pallas kernels for 11%

profile of v4, /device:TPU:0, one launch (start us, length us, event | category | flops | bytes accessed | tf_op | source)
XLA Modules:
  0.0 34.9 jit_solution(2242719580621655828)
XLA Ops:
  0.6 1.6 %pick.1 = (bf16[2,16,3200]{2,1,0:T(8,128)(2,1)S(1)}, bf16[2,16,3200]{2,1,0:T(8,128)(2,1)S(1)}, bf16[1,1024,128]{2,1,0:T(8,128)(2,1)S(1)}, bf16[1,1024,128]{2,1,0...) custom-call(s32[2,128]{1,0:T(2,128)} %index_hbm.1, bf16[32,8192]{1,0:T(8,128)(2,1)} %rows_hbm.1, ...), custom_call_target="tpu_custom_call" | custom-call | tf_op jit(solution)/shard_map/pick/pallas_call | solution.py:382
  2.3 3.0 %collective-permute-start = (bf16[2,16,3200]{2,1,0:T(8,128)(2,1)S(1)}, bf16[2,16,3200]{2,1,0:T(8,128)(2,1)S(1)}, u32[]{:S(2)}, u32[]{:S(2)}) collective-permute-start(bf16[2,16,3200]{2,1,0:T(8,128)(2,1)S(1)} %get-tuple-element.25), channel_id=1, source_target_pairs={{0,2},{1,3},{2,0},{3,1},{16,18},{17,19},{18,16},{19,17},{4,6},{5,7... | collective-permute-start | bytes 614408 | tf_op jit(solution)/shard_map/ppermute | solution.py:354
  5.3 0.2 pick_others.1
  5.5 1.6 %collective-permute-start.1 = (bf16[2,16,2048]{2,1,0:T(8,128)(2,1)S(1)}, bf16[2,16,2048]{2,1,0:T(8,128)(2,1)S(1)}, u32[]{:S(2)}, u32[]{:S(2)}) collective-permute-start(bf16[2,16,2048]{2,1,0:T(8,128)(2,1)S(1)} %get-tuple-element.28), channel_id=1, source_target_pairs={{0,16},{1,17},{2,18},{3,19},{16,0},{17,1},{18,2},{19,3},{4,20},{5,... | collective-permute-start | bytes 393224 | tf_op jit(solution)/shard_map/ppermute | solution.py:354
  7.1 0.0 collective-permute-start.2
  7.1 0.0 collective-permute-start.3
  7.1 4.0 %collective-permute-done.refs_1_.refs_3_ = bf16[2,16,3200]{2,1,0:T(8,128)(2,1)S(1)} collective-permute-done((bf16[2,16,3200]{2,1,0:T(8,128)(2,1)S(1)}, bf16[2,16,3200]{2,1,0:T(8,128)(2,1)S(1)}, u32[]{:S(2)}, u32[]{:S(2)}) %collective-permute-start) | collective-permute-done | bytes 204832 | tf_op jit(solution)/shard_map/ppermute | solution.py:354
  11.1 0.0 collective-permute-start.4
  11.1 0.9 %collective-permute-done.1.refs_2_ = bf16[2,16,2048]{2,1,0:T(8,128)(2,1)S(1)} collective-permute-done((bf16[2,16,2048]{2,1,0:T(8,128)(2,1)S(1)}, bf16[2,16,2048]{2,1,0:T(8,128)(2,1)S(1)}, u32[]{:S(2)}, u32[]{:S(2)}) %collective-permute-start.1) | collective-permute-done | bytes 131104 | tf_op jit(solution)/shard_map/ppermute | solution.py:354
  11.9 1.2 %collective-permute-done.2.refs_3_ = bf16[2,16,2048]{2,1,0:T(8,128)(2,1)S(1)} collective-permute-done((bf16[2,16,2048]{2,1,0:T(8,128)(2,1)S(1)}, bf16[2,16,2048]{2,1,0:T(8,128)(2,1)S(1)}, u32[]{:S(2)}, u32[]{:S(2)}) %collective-permute-start.2) | collective-permute-done | bytes 131104 | tf_op jit(solution)/shard_map/ppermute | solution.py:354
  13.2 0.5 %collective-permute-start.7 = (bf16[1,1024,128]{2,1,0:T(8,128)(2,1)S(1)}, bf16[1,1024,128]{2,1,0:T(8,128)(2,1)S(1)}, u32[]{:S(2)}, u32[]{:S(2)}) collective-permute-start(bf16[1,1024,128]{2,1,0:T(8,128)(2,1)S(1)} %get-tuple-element.31.refs_0_), channel_id=1, source_target_pairs={{0,1},{1,0},{2,3},{3,2},{4,5},{5,4},{6,7},{7,6},{8,9},{9,8},{10,11... | collective-permute-start | bytes 786440 | tf_op jit(solution)/shard_map/ppermute | solution.py:351
  13.7 0.1 collective-permute-start.8
  13.8 0.7 %collective-permute-done.6.refs_7_ = bf16[2,16,2048]{2,1,0:T(8,128)(2,1)S(1)} collective-permute-done((bf16[2,16,2048]{2,1,0:T(8,128)(2,1)S(1)}, bf16[2,16,2048]{2,1,0:T(8,128)(2,1)S(1)}, u32[]{:S(2)}, u32[]{:S(2)}) %collective-permute-start.6) | collective-permute-done | bytes 131104 | tf_op jit(solution)/shard_map/ppermute | solution.py:351
  14.5 0.4 %terms.1 = (bf16[2,128,2048]{2,1,0:T(8,128)(2,1)S(1)}, bf16[128,128]{1,0:T(8,128)(2,1)S(1)}, bf16[2,32,1792]{2,1,0:T(8,128)(2,1)S(1)}) custom-call(bf16[2,16,3200]{2,1,0:T(8,128)(2,1)S(1)} %get-tuple-element.24.refs_0_.refs_2_, bf16[2,16,3200]{2,1,0:T(8,128)(2,1)S(1)} %collective-permute-done.refs_1_.refs_3_, ...), custom_call_target="tpu_custom_call" | custom-call | flops 20000000000 | bytes 20000000 | tf_op jit(solution)/shard_map/terms/pallas_call | solution.py:415
  14.9 0.0 copy-start
  14.9 3.4 %collective-permute-start.14 = (bf16[2,32,1792]{2,1,0:T(8,128)(2,1)S(1)}, bf16[2,32,1792]{2,1,0:T(8,128)(2,1)S(1)}, u32[]{:S(2)}, u32[]{:S(2)}) collective-permute-start(bf16[2,32,1792]{2,1,0:T(8,128)(2,1)S(1)} %get-tuple-element.41), channel_id=1, source_target_pairs={{0,8},{1,13},{2,10},{3,15},{4,12},{5,9},{6,14},{7,11},{8,0},{9,5},... | collective-permute-start | bytes 688136 | tf_op jit(solution)/shard_map/ppermute | solution.py:362
  18.3 0.4 %rank.1.refs_0_ = f32[128,128]{1,0:T(8,128)S(1)} custom-call(bf16[2,128,2048]{2,1,0:T(8,128)(2,1)S(1)} %get-tuple-element.30.pair.refs_6_, bf16[1,1024,128]{2,1,0:T(8,128)(2,1)S(1)} %get-tuple-element.31.refs_0_, bf16[1,1024,128]{2,1,0:T(8,128)(2,1)S(1)} %get-tuple-element.32.refs_1_, bf16[1,1024,128]{2,1,0:T(8,128)(2,1)S(1)} %collective-permute-done.7.refs_2_, ...), custom_call_target="tpu_custom_call" | custom-call | tf_op jit(solution)/shard_map/rank/pallas_call | solution.py:427
  18.8 1.6 %collective-permute-start.9 = (f32[128,128]{1,0:T(8,128)S(1)}, f32[128,128]{1,0:T(8,128)S(1)}, u32[]{:S(2)}, u32[]{:S(2)}) collective-permute-start(f32[128,128]{1,0:T(8,128)S(1)} %rank.1.refs_0_), channel_id=1, source_target_pairs={{0,2},{1,3},{2,0},{3,1},{4,6},{5,7},{6,4},{7,5},{8,10},{9,11},{10,... | collective-permute-start | bytes 196616 | tf_op jit(solution)/shard_map/ppermute | solution.py:354
  20.3 1.4 %base.1 = (f32[32,2048]{1,0:T(8,128)S(1)}, f32[32,2048]{1,0:T(8,128)S(1)}, bf16[32,2048]{1,0:T(8,128)(2,1)S(1)}, bf16[32,2048]{1,0:T(8,128)(2,1)S(1)}) custom-call(bf16[2,128,2048]{2,1,0:T(8,128)(2,1)S(1)} %get-tuple-element.30.pair.refs_6_, bf16[2048,2048]{1,0:T(8,128)(2,1)S(1)} %bitcast.2), custom_call_target="tpu_custom_call" | custom-call | tf_op jit(solution)/shard_map/base/pallas_call | solution.py:438
  21.7 0.7 %collective-permute-start.11 = (bf16[32,2048]{1,0:T(8,128)(2,1)S(1)}, bf16[32,2048]{1,0:T(8,128)(2,1)S(1)}, u32[]{:S(2)}, u32[]{:S(2)}) collective-permute-start(bf16[32,2048]{1,0:T(8,128)(2,1)S(1)} %get-tuple-element.36), channel_id=1, source_target_pairs={{0,1},{1,0},{2,3},{3,2},{4,5},{5,4},{6,7},{7,6},{8,9},{9,8},{10,11... | collective-permute-start | bytes 393224 | tf_op jit(solution)/shard_map/ppermute | solution.py:351
  22.4 1.3 %collective-permute-done.9.refs_1_ = f32[128,128]{1,0:T(8,128)S(1)} collective-permute-done((f32[128,128]{1,0:T(8,128)S(1)}, f32[128,128]{1,0:T(8,128)S(1)}, u32[]{:S(2)}, u32[]{:S(2)}) %collective-permute-start.9) | collective-permute-done | bytes 65568 | tf_op jit(solution)/shard_map/ppermute | solution.py:354
  23.7 0.5 %up_terms.1 = (f32[32,2048]{1,0:T(8,128)S(1)}, f32[64,128]{1,0:T(8,128)S(1)}, bf16[32,2304]{1,0:T(8,128)(2,1)S(1)}, bf16[2,32,512]{2,1,0:T(8,128)(2,1)S(1)}) custom-call(f32[128,128]{1,0:T(8,128)S(1)} %rank.1.refs_0_, f32[128,128]{1,0:T(8,128)S(1)} %collective-permute-done.9.refs_1_, bf16[2,16,3200]{2,1,0:T(8,128)(2,1)S(1)} %get-tuple-element.24.refs_0_.refs_2_, ...), custom_call_target="tpu_custom_call" | custom-call | tf_op jit(solution)/shard_map/up_terms/pallas_call | solution.py:466
  24.2 1.0 %collective-permute-start.13 = (bf16[32,2304]{1,0:T(8,128)(2,1)S(1)}, bf16[32,2304]{1,0:T(8,128)(2,1)S(1)}, u32[]{:S(2)}, u32[]{:S(2)}) collective-permute-start(bf16[32,2304]{1,0:T(8,128)(2,1)S(1)} %get-tuple-element.40), channel_id=1, source_target_pairs={{0,4},{4,0},{8,12},{12,8},{1,5},{5,1},{9,13},{13,9},{2,6},{6,2},{1... | collective-permute-start | bytes 442376 | tf_op jit(solution)/shard_map/ppermute | solution.py:354
  25.2 0.3 collective-permute-start.15
  25.6 1.6 %collective-permute-start.12 = (bf16[32,2048]{1,0:T(8,128)(2,1)S(1)}, bf16[32,2048]{1,0:T(8,128)(2,1)S(1)}, u32[]{:S(2)}, u32[]{:S(2)}) collective-permute-start(bf16[32,2048]{1,0:T(8,128)(2,1)S(1)} %pair.1), channel_id=1, source_target_pairs={{0,2},{1,3},{2,0},{3,1},{4,6},{5,7},{6,4},{7,5},{8,10},{9,11},{10,... | collective-permute-start | bytes 393224 | tf_op jit(solution)/shard_map/ppermute | solution.py:354
  27.2 2.4 %collective-permute-done.14.refs_0_.refs_3_ = bf16[2,32,1792]{2,1,0:T(8,128)(2,1)S(1)} collective-permute-done((bf16[2,32,1792]{2,1,0:T(8,128)(2,1)S(1)}, bf16[2,32,1792]{2,1,0:T(8,128)(2,1)S(1)}, u32[]{:S(2)}, u32[]{:S(2)}) %collective-permute-start.14) | collective-permute-done | bytes 229408 | tf_op jit(solution)/shard_map/ppermute | solution.py:362
  29.6 0.1 collective-permute-start.16
  29.7 2.5 %collective-permute-done.15.refs_0_.refs_4_ = bf16[2,32,512]{2,1,0:T(8,128)(2,1)S(1)} collective-permute-done((bf16[2,32,512]{2,1,0:T(8,128)(2,1)S(1)}, bf16[2,32,512]{2,1,0:T(8,128)(2,1)S(1)}, u32[]{:S(2)}, u32[]{:S(2)}) %collective-permute-start.15) | collective-permute-done | bytes 65568 | tf_op jit(solution)/shard_map/ppermute | solution.py:362
  32.2 0.6 %collective-permute-done.13.refs_1_.refs_2_ = bf16[32,2304]{1,0:T(8,128)(2,1)S(1)} collective-permute-done((bf16[32,2304]{1,0:T(8,128)(2,1)S(1)}, bf16[32,2304]{1,0:T(8,128)(2,1)S(1)}, u32[]{:S(2)}, u32[]{:S(2)}) %collective-permute-start.13) | collective-permute-done | bytes 147488 | tf_op jit(solution)/shard_map/ppermute | solution.py:354
  32.9 0.9 %output.1 = f32[1,32,2048]{2,1,0:T(8,128)} custom-call(f32[128,128]{1,0:T(8,128)S(1)} %rank.1.refs_0_, f32[128,128]{1,0:T(8,128)S(1)} %collective-permute-done.9.refs_1_, f32[32,2048]{1,0:T(8,128)S(1)} %get-tuple-element.33.refs_2_, bf16[32,2048]{1,0:T(8,128)(2,1)S(1)} %collective-permute-done.10.refs_3_, ...), custom_call_target="tpu_custom_call" | custom-call | tf_op jit(solution)/shard_map/output/pallas_call | solution.py:483
  33.8 0.3 collective-permute-done.17.refs_6_
  34.1 0.8 %sums.1 = (f32[1,32,2048]{2,1,0:T(8,128)}, f32[1,64,128]{2,1,0:T(8,128)}) custom-call(f32[32,2048]{1,0:T(8,128)S(1)} %get-tuple-element.38.refs_0_, f32[64,128]{1,0:T(8,128)S(1)} %get-tuple-element.39.refs_1_, bf16[32,2304]{1,0:T(8,128)(2,1)S(1)} %collective-permute-done.13.refs_1_.refs_2_, bf16[2,32,1792]{2,1,0:T(8,128)(2,1)S(1)} %collective-permute-done.14.refs_0_.refs_3_, ...), custom_call_target="tpu_custom_call" | custom-call | tf_op jit(solution)/shard_map/sums/pallas_call | solution.py:505
  (22 shorter events, 0.1 us)
Async XLA Ops:
  2.3 8.8 %collective-permute-start = (bf16[2,16,3200]{2,1,0:T(8,128)(2,1)S(1)}, bf16[2,16,3200]{2,1,0:T(8,128)(2,1)S(1)}, u32[]{:S(2)}, u32[]{:S(2)}) collective-permute-start(bf16[2,16,3200]{2,1,0:T(8,128)(2,1)S(1)} %get-tuple-element.25), channel_id=1, source_target_pairs={{0,2},{1,3},{2,0},{3,1},{16,18},{17,19},{18,16},{19,17},{4,6},{5,7... | collective-permute-start | bytes 614408 | tf_op jit(solution)/shard_map/ppermute | solution.py:354
  5.5 6.4 %collective-permute-start.1 = (bf16[2,16,2048]{2,1,0:T(8,128)(2,1)S(1)}, bf16[2,16,2048]{2,1,0:T(8,128)(2,1)S(1)}, u32[]{:S(2)}, u32[]{:S(2)}) collective-permute-start(bf16[2,16,2048]{2,1,0:T(8,128)(2,1)S(1)} %get-tuple-element.28), channel_id=1, source_target_pairs={{0,16},{1,17},{2,18},{3,19},{16,0},{17,1},{18,2},{19,3},{4,20},{5,... | collective-permute-start | bytes 393224 | tf_op jit(solution)/shard_map/ppermute | solution.py:354
  7.1 6.1 %collective-permute-start.2 = (bf16[2,16,2048]{2,1,0:T(8,128)(2,1)S(1)}, bf16[2,16,2048]{2,1,0:T(8,128)(2,1)S(1)}, u32[]{:S(2)}, u32[]{:S(2)}) collective-permute-start(bf16[2,16,2048]{2,1,0:T(8,128)(2,1)S(1)} %get-tuple-element.29), channel_id=1, source_target_pairs={{0,18},{1,19},{2,16},{3,17},{16,2},{17,3},{18,0},{19,1},{4,22},{5,... | collective-permute-start | bytes 393224 | tf_op jit(solution)/shard_map/ppermute | solution.py:354
  7.1 6.6 %collective-permute-start.3 = (bf16[2,16,3200]{2,1,0:T(8,128)(2,1)S(1)}, bf16[2,16,3200]{2,1,0:T(8,128)(2,1)S(1)}, u32[]{:S(2)}, u32[]{:S(2)}) collective-permute-start(bf16[2,16,3200]{2,1,0:T(8,128)(2,1)S(1)} %get-tuple-element.24.refs_0_.refs_2_), channel_id=1, source_target_pairs={{0,1},{1,0},{2,3},{3,2},{4,5},{5,4},{6,7},{7,6},{8,9},{9,8},{10,11... | collective-permute-start | bytes 614408 | tf_op jit(solution)/shard_map/ppermute | solution.py:351
  11.1 3.5 %collective-permute-start.4 = (bf16[2,16,3200]{2,1,0:T(8,128)(2,1)S(1)}, bf16[2,16,3200]{2,1,0:T(8,128)(2,1)S(1)}, u32[]{:S(2)}, u32[]{:S(2)}) collective-permute-start(bf16[2,16,3200]{2,1,0:T(8,128)(2,1)S(1)} %collective-permute-done.refs_1_.refs_3_), channel_id=1, source_target_pairs={{0,1},{1,0},{2,3},{3,2},{4,5},{5,4},{6,7},{7,6},{8,9},{9,8},{10,11... | collective-permute-start | bytes 614408 | tf_op jit(solution)/shard_map/ppermute | solution.py:351
  11.9 1.9 %collective-permute-start.5 = (bf16[2,16,2048]{2,1,0:T(8,128)(2,1)S(1)}, bf16[2,16,2048]{2,1,0:T(8,128)(2,1)S(1)}, u32[]{:S(2)}, u32[]{:S(2)}) collective-permute-start(bf16[2,16,2048]{2,1,0:T(8,128)(2,1)S(1)} %collective-permute-done.1.refs_2_), channel_id=1, source_target_pairs={{0,1},{1,0},{2,3},{3,2},{4,5},{5,4},{6,7},{7,6},{8,9},{9,8},{10,11... | collective-permute-start | bytes 393224 | tf_op jit(solution)/shard_map/ppermute | solution.py:351
  13.2 1.3 %collective-permute-start.6 = (bf16[2,16,2048]{2,1,0:T(8,128)(2,1)S(1)}, bf16[2,16,2048]{2,1,0:T(8,128)(2,1)S(1)}, u32[]{:S(2)}, u32[]{:S(2)}) collective-permute-start(bf16[2,16,2048]{2,1,0:T(8,128)(2,1)S(1)} %collective-permute-done.2.refs_3_), channel_id=1, source_target_pairs={{0,1},{1,0},{2,3},{3,2},{4,5},{5,4},{6,7},{7,6},{8,9},{9,8},{10,11... | collective-permute-start | bytes 393224 | tf_op jit(solution)/shard_map/ppermute | solution.py:351
  13.2 5.1 %collective-permute-start.7 = (bf16[1,1024,128]{2,1,0:T(8,128)(2,1)S(1)}, bf16[1,1024,128]{2,1,0:T(8,128)(2,1)S(1)}, u32[]{:S(2)}, u32[]{:S(2)}) collective-permute-start(bf16[1,1024,128]{2,1,0:T(8,128)(2,1)S(1)} %get-tuple-element.31.refs_0_), channel_id=1, source_target_pairs={{0,1},{1,0},{2,3},{3,2},{4,5},{5,4},{6,7},{7,6},{8,9},{9,8},{10,11... | collective-permute-start | bytes 786440 | tf_op jit(solution)/shard_map/ppermute | solution.py:351
  13.7 6.6 %slice-start = ((s8[8388608]{0:T(1024)(128)(4,1)}), s8[4194304]{0:T(1024)(128)(4,1)S(1)}, s32[]{:S(2)}) async-start(s8[8388608]{0:T(1024)(128)(4,1)} %bitcast.1), calls=%async_computation | async-start | bytes 8388608
  13.7 6.6 %slice-start.1 = ((s8[8388608]{0:T(1024)(128)(4,1)}), s8[4194304]{0:T(1024)(128)(4,1)S(1)}, s32[]{:S(2)}) async-start(s8[8388608]{0:T(1024)(128)(4,1)} %bitcast.1), calls=%async_computation.1 | async-start | bytes 8388608
  13.7 4.6 %collective-permute-start.8 = (bf16[1,1024,128]{2,1,0:T(8,128)(2,1)S(1)}, bf16[1,1024,128]{2,1,0:T(8,128)(2,1)S(1)}, u32[]{:S(2)}, u32[]{:S(2)}) collective-permute-start(bf16[1,1024,128]{2,1,0:T(8,128)(2,1)S(1)} %get-tuple-element.32.refs_1_), channel_id=1, source_target_pairs={{0,1},{1,0},{2,3},{3,2},{4,5},{5,4},{6,7},{7,6},{8,9},{9,8},{10,11... | collective-permute-start | bytes 786440 | tf_op jit(solution)/shard_map/ppermute | solution.py:351
  14.9 18.0 %copy-start = (bf16[1,64,2048]{2,1,0:T(8,128)(2,1)S(1)}, bf16[1,64,2048]{2,1,0:T(8,128)(2,1)}, u32[]{:S(2)}) copy-start(bf16[1,64,2048]{2,1,0:T(8,128)(2,1)} %refs_5_.1) | copy-start | bytes 786436
  14.9 14.7 %collective-permute-start.14 = (bf16[2,32,1792]{2,1,0:T(8,128)(2,1)S(1)}, bf16[2,32,1792]{2,1,0:T(8,128)(2,1)S(1)}, u32[]{:S(2)}, u32[]{:S(2)}) collective-permute-start(bf16[2,32,1792]{2,1,0:T(8,128)(2,1)S(1)} %get-tuple-element.41), channel_id=1, source_target_pairs={{0,8},{1,13},{2,10},{3,15},{4,12},{5,9},{6,14},{7,11},{8,0},{9,5},... | collective-permute-start | bytes 688136 | tf_op jit(solution)/shard_map/ppermute | solution.py:362
  18.8 5.0 %collective-permute-start.9 = (f32[128,128]{1,0:T(8,128)S(1)}, f32[128,128]{1,0:T(8,128)S(1)}, u32[]{:S(2)}, u32[]{:S(2)}) collective-permute-start(f32[128,128]{1,0:T(8,128)S(1)} %rank.1.refs_0_), channel_id=1, source_target_pairs={{0,2},{1,3},{2,0},{3,1},{4,6},{5,7},{6,4},{7,5},{8,10},{9,11},{10,... | collective-permute-start | bytes 196616 | tf_op jit(solution)/shard_map/ppermute | solution.py:354
  21.7 3.9 %collective-permute-start.11 = (bf16[32,2048]{1,0:T(8,128)(2,1)S(1)}, bf16[32,2048]{1,0:T(8,128)(2,1)S(1)}, u32[]{:S(2)}, u32[]{:S(2)}) collective-permute-start(bf16[32,2048]{1,0:T(8,128)(2,1)S(1)} %get-tuple-element.36), channel_id=1, source_target_pairs={{0,1},{1,0},{2,3},{3,2},{4,5},{5,4},{6,7},{7,6},{8,9},{9,8},{10,11... | collective-permute-start | bytes 393224 | tf_op jit(solution)/shard_map/ppermute | solution.py:351
  24.2 8.6 %collective-permute-start.13 = (bf16[32,2304]{1,0:T(8,128)(2,1)S(1)}, bf16[32,2304]{1,0:T(8,128)(2,1)S(1)}, u32[]{:S(2)}, u32[]{:S(2)}) collective-permute-start(bf16[32,2304]{1,0:T(8,128)(2,1)S(1)} %get-tuple-element.40), channel_id=1, source_target_pairs={{0,4},{4,0},{8,12},{12,8},{1,5},{5,1},{9,13},{13,9},{2,6},{6,2},{1... | collective-permute-start | bytes 442376 | tf_op jit(solution)/shard_map/ppermute | solution.py:354
  25.2 7.6 %collective-permute-start.10 = (bf16[32,2048]{1,0:T(8,128)(2,1)S(1)}, bf16[32,2048]{1,0:T(8,128)(2,1)S(1)}, u32[]{:S(2)}, u32[]{:S(2)}) collective-permute-start(bf16[32,2048]{1,0:T(8,128)(2,1)S(1)} %get-tuple-element.34), channel_id=1, source_target_pairs={{0,1},{1,0},{2,3},{3,2},{4,5},{5,4},{6,7},{7,6},{8,9},{9,8},{10,11... | collective-permute-start | bytes 393224 | tf_op jit(solution)/shard_map/ppermute | solution.py:351
  25.2 7.0 %collective-permute-start.15 = (bf16[2,32,512]{2,1,0:T(8,128)(2,1)S(1)}, bf16[2,32,512]{2,1,0:T(8,128)(2,1)S(1)}, u32[]{:S(2)}, u32[]{:S(2)}) collective-permute-start(bf16[2,32,512]{2,1,0:T(8,128)(2,1)S(1)} %get-tuple-element.42), channel_id=1, source_target_pairs={{0,8},{1,13},{2,10},{3,15},{4,12},{5,9},{6,14},{7,11},{8,0},{9,5},... | collective-permute-start | bytes 196616 | tf_op jit(solution)/shard_map/ppermute | solution.py:362
  25.6 7.3 %collective-permute-start.12 = (bf16[32,2048]{1,0:T(8,128)(2,1)S(1)}, bf16[32,2048]{1,0:T(8,128)(2,1)S(1)}, u32[]{:S(2)}, u32[]{:S(2)}) collective-permute-start(bf16[32,2048]{1,0:T(8,128)(2,1)S(1)} %pair.1), channel_id=1, source_target_pairs={{0,2},{1,3},{2,0},{3,1},{4,6},{5,7},{6,4},{7,5},{8,10},{9,11},{10,... | collective-permute-start | bytes 393224 | tf_op jit(solution)/shard_map/ppermute | solution.py:354
  29.6 4.5 %collective-permute-start.16 = (bf16[32,1792]{1,0:T(8,128)(2,1)S(1)}, bf16[32,1792]{1,0:T(8,128)(2,1)S(1)}, u32[]{:S(2)}, u32[]{:S(2)}) collective-permute-start(bf16[32,1792]{1,0:T(8,128)(2,1)S(1)} %split.2), channel_id=1, source_target_pairs={{0,1},{1,0},{2,3},{3,2},{4,5},{5,4},{6,7},{7,6},{8,9},{9,8},{10,11... | collective-permute-start | bytes 344072 | tf_op jit(solution)/shard_map/ppermute | solution.py:351
  32.8 1.3 %collective-permute-start.17 = (bf16[32,1024]{1,0:T(8,128)(2,1)S(1)}, bf16[32,1024]{1,0:T(8,128)(2,1)S(1)}, u32[]{:S(2)}, u32[]{:S(2)}) collective-permute-start(bf16[32,1024]{1,0:T(8,128)(2,1)S(1)} %split.3), channel_id=1, source_target_pairs={{0,1},{1,0},{2,3},{3,2},{4,5},{5,4},{6,7},{7,6},{8,9},{9,8},{10,11... | collective-permute-start | bytes 196616 | tf_op jit(solution)/shard_map/ppermute | solution.py:351

commit v5 on v4

--- a/solution.py
+++ b/solution.py
@@ -281,7 +281,7 @@
     ranks = rank_refs[0][pl.ds(at, local), :]
     for ref in rank_refs[1:]:
         ranks = ranks + ref[pl.ds(at, local), :]
-    high, low = two_terms(adapter_scale * ranks)
+    terms_both = jnp.concatenate(two_terms(adapter_scale * ranks), axis=0)
     chunk = 512
     for f in range(0, width, chunk):
         side = rank * (f // half)
@@ -289,9 +289,8 @@
         result = terms[0][:, f : f + chunk]
         for ref in terms[1:]:
             result = result + ref[:, f : f + chunk].astype(f32)
-        result = result + jnp.dot(high[:, side : side + rank], up, preferred_element_type=f32)
-        result = result + jnp.dot(low[:, side : side + rank], up, preferred_element_type=f32)
-        out_ref[0, :, f : f + chunk] = result
+        both = jnp.dot(terms_both[:, side : side + rank], up, preferred_element_type=f32)
+        out_ref[0, :, f : f + chunk] = result + both[:local] + both[local:]
 
 
 def split_kernel(*refs):

time: 35 us -> 35 us (level)
  no operation moved by 1% of the time
where the time goes in v5:
time: 35 us; the launch traced here: 34.9 us
  waiting for transfers between devices  14 us (40%)
  starting transfers between devices  13.9 us (40%)
  Pallas kernels  6.24 us (18%)
  between operations  0.74 us (2%)
    ppermute x6, starting transfers between devices, over(): return lax.ppermute(value, axis, [(i, i ^ mask) for i in range(size)])  8.76 us
    ppermute x6, waiting for transfers between devices, over(): return lax.ppermute(value, axis, [(i, i ^ mask) for i in range(size)])  8.04 us
    ppermute x2, waiting for transfers between devices, far_dp(): return lax.ppermute(value, ('dp', 'tensor'), pairs)  4.92 us
    ppermute x2, starting transfers between devices, far_dp(): return lax.ppermute(value, ('dp', 'tensor'), pairs)  3.74 us
    pallas_call x1, Pallas kernels, shards(): pl.pallas_call(functools.partial(pick_kernel, trials, ys, dps, select, wi...  1.63 us
    ppermute x10, starting transfers between devices, to_core(): return lax.ppermute(value, 'tensor', [(i, i ^ 1) for i in range(tensors)])  1.37 us
    pallas_call x1, Pallas kernels, shards(): pl.pallas_call(functools.partial(base_kernel, ys), out_shape=[shape((loca...  1.37 us
    ppermute x10, waiting for transfers between devices, to_core(): return lax.ppermute(value, 'tensor', [(i, i ^ 1) for i in range(tensors)])  1.04 us
  transfers between devices with their start and end apart: 18, of which 9 were waited for; matrix products, arithmetic and copies ran while one was open for 0% of the time, Pallas kernels for 11%

profile of v5, /device:TPU:0, one launch (start us, length us, event | category | flops | bytes accessed | tf_op | source)
XLA Modules:
  0.0 34.9 jit_solution(8564330573403895091)
XLA Ops:
  0.6 1.6 %pick.1 = (bf16[2,16,3200]{2,1,0:T(8,128)(2,1)S(1)}, bf16[2,16,3200]{2,1,0:T(8,128)(2,1)S(1)}, bf16[1,1024,128]{2,1,0:T(8,128)(2,1)S(1)}, bf16[1,1024,128]{2,1,0...) custom-call(s32[2,128]{1,0:T(2,128)} %index_hbm.1, bf16[32,8192]{1,0:T(8,128)(2,1)} %rows_hbm.1, ...), custom_call_target="tpu_custom_call" | custom-call | tf_op jit(solution)/shard_map/pick/pallas_call | solution.py:381
  2.3 3.0 %collective-permute-start = (bf16[2,16,3200]{2,1,0:T(8,128)(2,1)S(1)}, bf16[2,16,3200]{2,1,0:T(8,128)(2,1)S(1)}, u32[]{:S(2)}, u32[]{:S(2)}) collective-permute-start(bf16[2,16,3200]{2,1,0:T(8,128)(2,1)S(1)} %get-tuple-element.25), channel_id=1, source_target_pairs={{0,2},{1,3},{2,0},{3,1},{16,18},{17,19},{18,16},{19,17},{4,6},{5,7... | collective-permute-start | bytes 614408 | tf_op jit(solution)/shard_map/ppermute | solution.py:353
  5.3 0.2 pick_others.1
  5.5 1.6 %collective-permute-start.1 = (bf16[2,16,2048]{2,1,0:T(8,128)(2,1)S(1)}, bf16[2,16,2048]{2,1,0:T(8,128)(2,1)S(1)}, u32[]{:S(2)}, u32[]{:S(2)}) collective-permute-start(bf16[2,16,2048]{2,1,0:T(8,128)(2,1)S(1)} %get-tuple-element.28), channel_id=1, source_target_pairs={{0,16},{1,17},{2,18},{3,19},{16,0},{17,1},{18,2},{19,3},{4,20},{5,... | collective-permute-start | bytes 393224 | tf_op jit(solution)/shard_map/ppermute | solution.py:353
  7.1 0.0 collective-permute-start.2
  7.1 0.0 collective-permute-start.3
  7.1 4.0 %collective-permute-done.refs_1_.refs_3_ = bf16[2,16,3200]{2,1,0:T(8,128)(2,1)S(1)} collective-permute-done((bf16[2,16,3200]{2,1,0:T(8,128)(2,1)S(1)}, bf16[2,16,3200]{2,1,0:T(8,128)(2,1)S(1)}, u32[]{:S(2)}, u32[]{:S(2)}) %collective-permute-start) | collective-permute-done | bytes 204832 | tf_op jit(solution)/shard_map/ppermute | solution.py:353
  11.1 0.0 collective-permute-start.4
  11.1 0.9 %collective-permute-done.1.refs_2_ = bf16[2,16,2048]{2,1,0:T(8,128)(2,1)S(1)} collective-permute-done((bf16[2,16,2048]{2,1,0:T(8,128)(2,1)S(1)}, bf16[2,16,2048]{2,1,0:T(8,128)(2,1)S(1)}, u32[]{:S(2)}, u32[]{:S(2)}) %collective-permute-start.1) | collective-permute-done | bytes 131104 | tf_op jit(solution)/shard_map/ppermute | solution.py:353
  11.9 1.2 %collective-permute-done.2.refs_3_ = bf16[2,16,2048]{2,1,0:T(8,128)(2,1)S(1)} collective-permute-done((bf16[2,16,2048]{2,1,0:T(8,128)(2,1)S(1)}, bf16[2,16,2048]{2,1,0:T(8,128)(2,1)S(1)}, u32[]{:S(2)}, u32[]{:S(2)}) %collective-permute-start.2) | collective-permute-done | bytes 131104 | tf_op jit(solution)/shard_map/ppermute | solution.py:353
  13.2 0.5 %collective-permute-start.7 = (bf16[1,1024,128]{2,1,0:T(8,128)(2,1)S(1)}, bf16[1,1024,128]{2,1,0:T(8,128)(2,1)S(1)}, u32[]{:S(2)}, u32[]{:S(2)}) collective-permute-start(bf16[1,1024,128]{2,1,0:T(8,128)(2,1)S(1)} %get-tuple-element.31.refs_0_), channel_id=1, source_target_pairs={{0,1},{1,0},{2,3},{3,2},{4,5},{5,4},{6,7},{7,6},{8,9},{9,8},{10,11... | collective-permute-start | bytes 786440 | tf_op jit(solution)/shard_map/ppermute | solution.py:350
  13.7 0.1 collective-permute-start.8
  13.8 0.7 %collective-permute-done.6.refs_7_ = bf16[2,16,2048]{2,1,0:T(8,128)(2,1)S(1)} collective-permute-done((bf16[2,16,2048]{2,1,0:T(8,128)(2,1)S(1)}, bf16[2,16,2048]{2,1,0:T(8,128)(2,1)S(1)}, u32[]{:S(2)}, u32[]{:S(2)}) %collective-permute-start.6) | collective-permute-done | bytes 131104 | tf_op jit(solution)/shard_map/ppermute | solution.py:350
  14.5 0.4 %terms.1 = (bf16[2,128,2048]{2,1,0:T(8,128)(2,1)S(1)}, bf16[128,128]{1,0:T(8,128)(2,1)S(1)}, bf16[2,32,1792]{2,1,0:T(8,128)(2,1)S(1)}) custom-call(bf16[2,16,3200]{2,1,0:T(8,128)(2,1)S(1)} %get-tuple-element.24.refs_0_.refs_2_, bf16[2,16,3200]{2,1,0:T(8,128)(2,1)S(1)} %collective-permute-done.refs_1_.refs_3_, ...), custom_call_target="tpu_custom_call" | custom-call | flops 20000000000 | bytes 20000000 | tf_op jit(solution)/shard_map/terms/pallas_call | solution.py:414
  14.9 0.0 copy-start
  14.9 3.4 %collective-permute-start.14 = (bf16[2,32,1792]{2,1,0:T(8,128)(2,1)S(1)}, bf16[2,32,1792]{2,1,0:T(8,128)(2,1)S(1)}, u32[]{:S(2)}, u32[]{:S(2)}) collective-permute-start(bf16[2,32,1792]{2,1,0:T(8,128)(2,1)S(1)} %get-tuple-element.41), channel_id=1, source_target_pairs={{0,8},{1,13},{2,10},{3,15},{4,12},{5,9},{6,14},{7,11},{8,0},{9,5},... | collective-permute-start | bytes 688136 | tf_op jit(solution)/shard_map/ppermute | solution.py:361
  18.3 0.4 %rank.1.refs_0_ = f32[128,128]{1,0:T(8,128)S(1)} custom-call(bf16[2,128,2048]{2,1,0:T(8,128)(2,1)S(1)} %get-tuple-element.30.pair.refs_6_, bf16[1,1024,128]{2,1,0:T(8,128)(2,1)S(1)} %get-tuple-element.31.refs_0_, bf16[1,1024,128]{2,1,0:T(8,128)(2,1)S(1)} %get-tuple-element.32.refs_1_, bf16[1,1024,128]{2,1,0:T(8,128)(2,1)S(1)} %collective-permute-done.7.refs_2_, ...), custom_call_target="tpu_custom_call" | custom-call | tf_op jit(solution)/shard_map/rank/pallas_call | solution.py:426
  18.8 1.6 %collective-permute-start.9 = (f32[128,128]{1,0:T(8,128)S(1)}, f32[128,128]{1,0:T(8,128)S(1)}, u32[]{:S(2)}, u32[]{:S(2)}) collective-permute-start(f32[128,128]{1,0:T(8,128)S(1)} %rank.1.refs_0_), channel_id=1, source_target_pairs={{0,2},{1,3},{2,0},{3,1},{4,6},{5,7},{6,4},{7,5},{8,10},{9,11},{10,... | collective-permute-start | bytes 196616 | tf_op jit(solution)/shard_map/ppermute | solution.py:353
  20.3 1.4 %base.1 = (f32[32,2048]{1,0:T(8,128)S(1)}, f32[32,2048]{1,0:T(8,128)S(1)}, bf16[32,2048]{1,0:T(8,128)(2,1)S(1)}, bf16[32,2048]{1,0:T(8,128)(2,1)S(1)}) custom-call(bf16[2,128,2048]{2,1,0:T(8,128)(2,1)S(1)} %get-tuple-element.30.pair.refs_6_, bf16[2048,2048]{1,0:T(8,128)(2,1)S(1)} %bitcast.2), custom_call_target="tpu_custom_call" | custom-call | tf_op jit(solution)/shard_map/base/pallas_call | solution.py:437
  21.7 0.7 %collective-permute-start.11 = (bf16[32,2048]{1,0:T(8,128)(2,1)S(1)}, bf16[32,2048]{1,0:T(8,128)(2,1)S(1)}, u32[]{:S(2)}, u32[]{:S(2)}) collective-permute-start(bf16[32,2048]{1,0:T(8,128)(2,1)S(1)} %get-tuple-element.36), channel_id=1, source_target_pairs={{0,1},{1,0},{2,3},{3,2},{4,5},{5,4},{6,7},{7,6},{8,9},{9,8},{10,11... | collective-permute-start | bytes 393224 | tf_op jit(solution)/shard_map/ppermute | solution.py:350
  22.4 1.3 %collective-permute-done.9.refs_1_ = f32[128,128]{1,0:T(8,128)S(1)} collective-permute-done((f32[128,128]{1,0:T(8,128)S(1)}, f32[128,128]{1,0:T(8,128)S(1)}, u32[]{:S(2)}, u32[]{:S(2)}) %collective-permute-start.9) | collective-permute-done | bytes 65568 | tf_op jit(solution)/shard_map/ppermute | solution.py:353
  23.7 0.5 %up_terms.1 = (f32[32,2048]{1,0:T(8,128)S(1)}, f32[64,128]{1,0:T(8,128)S(1)}, bf16[32,2304]{1,0:T(8,128)(2,1)S(1)}, bf16[2,32,512]{2,1,0:T(8,128)(2,1)S(1)}) custom-call(f32[128,128]{1,0:T(8,128)S(1)} %rank.1.refs_0_, f32[128,128]{1,0:T(8,128)S(1)} %collective-permute-done.9.refs_1_, bf16[2,16,3200]{2,1,0:T(8,128)(2,1)S(1)} %get-tuple-element.24.refs_0_.refs_2_, ...), custom_call_target="tpu_custom_call" | custom-call | tf_op jit(solution)/shard_map/up_terms/pallas_call | solution.py:465
  24.2 1.0 %collective-permute-start.13 = (bf16[32,2304]{1,0:T(8,128)(2,1)S(1)}, bf16[32,2304]{1,0:T(8,128)(2,1)S(1)}, u32[]{:S(2)}, u32[]{:S(2)}) collective-permute-start(bf16[32,2304]{1,0:T(8,128)(2,1)S(1)} %get-tuple-element.40), channel_id=1, source_target_pairs={{0,4},{4,0},{8,12},{12,8},{1,5},{5,1},{9,13},{13,9},{2,6},{6,2},{1... | collective-permute-start | bytes 442376 | tf_op jit(solution)/shard_map/ppermute | solution.py:353
  25.2 0.3 collective-permute-start.15
  25.6 1.6 %collective-permute-start.12 = (bf16[32,2048]{1,0:T(8,128)(2,1)S(1)}, bf16[32,2048]{1,0:T(8,128)(2,1)S(1)}, u32[]{:S(2)}, u32[]{:S(2)}) collective-permute-start(bf16[32,2048]{1,0:T(8,128)(2,1)S(1)} %pair.1), channel_id=1, source_target_pairs={{0,2},{1,3},{2,0},{3,1},{4,6},{5,7},{6,4},{7,5},{8,10},{9,11},{10,... | collective-permute-start | bytes 393224 | tf_op jit(solution)/shard_map/ppermute | solution.py:353
  27.2 2.4 %collective-permute-done.14.refs_0_.refs_3_ = bf16[2,32,1792]{2,1,0:T(8,128)(2,1)S(1)} collective-permute-done((bf16[2,32,1792]{2,1,0:T(8,128)(2,1)S(1)}, bf16[2,32,1792]{2,1,0:T(8,128)(2,1)S(1)}, u32[]{:S(2)}, u32[]{:S(2)}) %collective-permute-start.14) | collective-permute-done | bytes 229408 | tf_op jit(solution)/shard_map/ppermute | solution.py:361
  29.6 0.1 collective-permute-start.16
  29.7 2.5 %collective-permute-done.15.refs_0_.refs_4_ = bf16[2,32,512]{2,1,0:T(8,128)(2,1)S(1)} collective-permute-done((bf16[2,32,512]{2,1,0:T(8,128)(2,1)S(1)}, bf16[2,32,512]{2,1,0:T(8,128)(2,1)S(1)}, u32[]{:S(2)}, u32[]{:S(2)}) %collective-permute-start.15) | collective-permute-done | bytes 65568 | tf_op jit(solution)/shard_map/ppermute | solution.py:361
  32.2 0.6 %collective-permute-done.13.refs_1_.refs_2_ = bf16[32,2304]{1,0:T(8,128)(2,1)S(1)} collective-permute-done((bf16[32,2304]{1,0:T(8,128)(2,1)S(1)}, bf16[32,2304]{1,0:T(8,128)(2,1)S(1)}, u32[]{:S(2)}, u32[]{:S(2)}) %collective-permute-start.13) | collective-permute-done | bytes 147488 | tf_op jit(solution)/shard_map/ppermute | solution.py:353
  32.9 0.9 %output.1 = f32[1,32,2048]{2,1,0:T(8,128)} custom-call(f32[128,128]{1,0:T(8,128)S(1)} %rank.1.refs_0_, f32[128,128]{1,0:T(8,128)S(1)} %collective-permute-done.9.refs_1_, f32[32,2048]{1,0:T(8,128)S(1)} %get-tuple-element.33.refs_2_, bf16[32,2048]{1,0:T(8,128)(2,1)S(1)} %collective-permute-done.10.refs_3_, ...), custom_call_target="tpu_custom_call" | custom-call | tf_op jit(solution)/shard_map/output/pallas_call | solution.py:482
  33.8 0.3 collective-permute-done.17.refs_6_
  34.1 0.8 %sums.1 = (f32[1,32,2048]{2,1,0:T(8,128)}, f32[1,64,128]{2,1,0:T(8,128)}) custom-call(f32[32,2048]{1,0:T(8,128)S(1)} %get-tuple-element.38.refs_0_, f32[64,128]{1,0:T(8,128)S(1)} %get-tuple-element.39.refs_1_, bf16[32,2304]{1,0:T(8,128)(2,1)S(1)} %collective-permute-done.13.refs_1_.refs_2_, bf16[2,32,1792]{2,1,0:T(8,128)(2,1)S(1)} %collective-permute-done.14.refs_0_.refs_3_, ...), custom_call_target="tpu_custom_call" | custom-call | tf_op jit(solution)/shard_map/sums/pallas_call | solution.py:504
  (22 shorter events, 0.1 us)
Async XLA Ops:
  2.3 8.8 %collective-permute-start = (bf16[2,16,3200]{2,1,0:T(8,128)(2,1)S(1)}, bf16[2,16,3200]{2,1,0:T(8,128)(2,1)S(1)}, u32[]{:S(2)}, u32[]{:S(2)}) collective-permute-start(bf16[2,16,3200]{2,1,0:T(8,128)(2,1)S(1)} %get-tuple-element.25), channel_id=1, source_target_pairs={{0,2},{1,3},{2,0},{3,1},{16,18},{17,19},{18,16},{19,17},{4,6},{5,7... | collective-permute-start | bytes 614408 | tf_op jit(solution)/shard_map/ppermute | solution.py:353
  5.5 6.4 %collective-permute-start.1 = (bf16[2,16,2048]{2,1,0:T(8,128)(2,1)S(1)}, bf16[2,16,2048]{2,1,0:T(8,128)(2,1)S(1)}, u32[]{:S(2)}, u32[]{:S(2)}) collective-permute-start(bf16[2,16,2048]{2,1,0:T(8,128)(2,1)S(1)} %get-tuple-element.28), channel_id=1, source_target_pairs={{0,16},{1,17},{2,18},{3,19},{16,0},{17,1},{18,2},{19,3},{4,20},{5,... | collective-permute-start | bytes 393224 | tf_op jit(solution)/shard_map/ppermute | solution.py:353
  7.1 6.1 %collective-permute-start.2 = (bf16[2,16,2048]{2,1,0:T(8,128)(2,1)S(1)}, bf16[2,16,2048]{2,1,0:T(8,128)(2,1)S(1)}, u32[]{:S(2)}, u32[]{:S(2)}) collective-permute-start(bf16[2,16,2048]{2,1,0:T(8,128)(2,1)S(1)} %get-tuple-element.29), channel_id=1, source_target_pairs={{0,18},{1,19},{2,16},{3,17},{16,2},{17,3},{18,0},{19,1},{4,22},{5,... | collective-permute-start | bytes 393224 | tf_op jit(solution)/shard_map/ppermute | solution.py:353
  7.1 6.6 %collective-permute-start.3 = (bf16[2,16,3200]{2,1,0:T(8,128)(2,1)S(1)}, bf16[2,16,3200]{2,1,0:T(8,128)(2,1)S(1)}, u32[]{:S(2)}, u32[]{:S(2)}) collective-permute-start(bf16[2,16,3200]{2,1,0:T(8,128)(2,1)S(1)} %get-tuple-element.24.refs_0_.refs_2_), channel_id=1, source_target_pairs={{0,1},{1,0},{2,3},{3,2},{4,5},{5,4},{6,7},{7,6},{8,9},{9,8},{10,11... | collective-permute-start | bytes 614408 | tf_op jit(solution)/shard_map/ppermute | solution.py:350
  11.1 3.5 %collective-permute-start.4 = (bf16[2,16,3200]{2,1,0:T(8,128)(2,1)S(1)}, bf16[2,16,3200]{2,1,0:T(8,128)(2,1)S(1)}, u32[]{:S(2)}, u32[]{:S(2)}) collective-permute-start(bf16[2,16,3200]{2,1,0:T(8,128)(2,1)S(1)} %collective-permute-done.refs_1_.refs_3_), channel_id=1, source_target_pairs={{0,1},{1,0},{2,3},{3,2},{4,5},{5,4},{6,7},{7,6},{8,9},{9,8},{10,11... | collective-permute-start | bytes 614408 | tf_op jit(solution)/shard_map/ppermute | solution.py:350
  11.9 1.9 %collective-permute-start.5 = (bf16[2,16,2048]{2,1,0:T(8,128)(2,1)S(1)}, bf16[2,16,2048]{2,1,0:T(8,128)(2,1)S(1)}, u32[]{:S(2)}, u32[]{:S(2)}) collective-permute-start(bf16[2,16,2048]{2,1,0:T(8,128)(2,1)S(1)} %collective-permute-done.1.refs_2_), channel_id=1, source_target_pairs={{0,1},{1,0},{2,3},{3,2},{4,5},{5,4},{6,7},{7,6},{8,9},{9,8},{10,11... | collective-permute-start | bytes 393224 | tf_op jit(solution)/shard_map/ppermute | solution.py:350
  13.2 1.3 %collective-permute-start.6 = (bf16[2,16,2048]{2,1,0:T(8,128)(2,1)S(1)}, bf16[2,16,2048]{2,1,0:T(8,128)(2,1)S(1)}, u32[]{:S(2)}, u32[]{:S(2)}) collective-permute-start(bf16[2,16,2048]{2,1,0:T(8,128)(2,1)S(1)} %collective-permute-done.2.refs_3_), channel_id=1, source_target_pairs={{0,1},{1,0},{2,3},{3,2},{4,5},{5,4},{6,7},{7,6},{8,9},{9,8},{10,11... | collective-permute-start | bytes 393224 | tf_op jit(solution)/shard_map/ppermute | solution.py:350
  13.2 5.1 %collective-permute-start.7 = (bf16[1,1024,128]{2,1,0:T(8,128)(2,1)S(1)}, bf16[1,1024,128]{2,1,0:T(8,128)(2,1)S(1)}, u32[]{:S(2)}, u32[]{:S(2)}) collective-permute-start(bf16[1,1024,128]{2,1,0:T(8,128)(2,1)S(1)} %get-tuple-element.31.refs_0_), channel_id=1, source_target_pairs={{0,1},{1,0},{2,3},{3,2},{4,5},{5,4},{6,7},{7,6},{8,9},{9,8},{10,11... | collective-permute-start | bytes 786440 | tf_op jit(solution)/shard_map/ppermute | solution.py:350
  13.7 6.6 %slice-start = ((s8[8388608]{0:T(1024)(128)(4,1)}), s8[4194304]{0:T(1024)(128)(4,1)S(1)}, s32[]{:S(2)}) async-start(s8[8388608]{0:T(1024)(128)(4,1)} %bitcast.1), calls=%async_computation | async-start | bytes 8388608
  13.7 6.6 %slice-start.1 = ((s8[8388608]{0:T(1024)(128)(4,1)}), s8[4194304]{0:T(1024)(128)(4,1)S(1)}, s32[]{:S(2)}) async-start(s8[8388608]{0:T(1024)(128)(4,1)} %bitcast.1), calls=%async_computation.1 | async-start | bytes 8388608
  13.7 4.6 %collective-permute-start.8 = (bf16[1,1024,128]{2,1,0:T(8,128)(2,1)S(1)}, bf16[1,1024,128]{2,1,0:T(8,128)(2,1)S(1)}, u32[]{:S(2)}, u32[]{:S(2)}) collective-permute-start(bf16[1,1024,128]{2,1,0:T(8,128)(2,1)S(1)} %get-tuple-element.32.refs_1_), channel_id=1, source_target_pairs={{0,1},{1,0},{2,3},{3,2},{4,5},{5,4},{6,7},{7,6},{8,9},{9,8},{10,11... | collective-permute-start | bytes 786440 | tf_op jit(solution)/shard_map/ppermute | solution.py:350
  14.9 18.0 %copy-start = (bf16[1,64,2048]{2,1,0:T(8,128)(2,1)S(1)}, bf16[1,64,2048]{2,1,0:T(8,128)(2,1)}, u32[]{:S(2)}) copy-start(bf16[1,64,2048]{2,1,0:T(8,128)(2,1)} %refs_5_.1) | copy-start | bytes 786436
  14.9 14.7 %collective-permute-start.14 = (bf16[2,32,1792]{2,1,0:T(8,128)(2,1)S(1)}, bf16[2,32,1792]{2,1,0:T(8,128)(2,1)S(1)}, u32[]{:S(2)}, u32[]{:S(2)}) collective-permute-start(bf16[2,32,1792]{2,1,0:T(8,128)(2,1)S(1)} %get-tuple-element.41), channel_id=1, source_target_pairs={{0,8},{1,13},{2,10},{3,15},{4,12},{5,9},{6,14},{7,11},{8,0},{9,5},... | collective-permute-start | bytes 688136 | tf_op jit(solution)/shard_map/ppermute | solution.py:361
  18.8 5.0 %collective-permute-start.9 = (f32[128,128]{1,0:T(8,128)S(1)}, f32[128,128]{1,0:T(8,128)S(1)}, u32[]{:S(2)}, u32[]{:S(2)}) collective-permute-start(f32[128,128]{1,0:T(8,128)S(1)} %rank.1.refs_0_), channel_id=1, source_target_pairs={{0,2},{1,3},{2,0},{3,1},{4,6},{5,7},{6,4},{7,5},{8,10},{9,11},{10,... | collective-permute-start | bytes 196616 | tf_op jit(solution)/shard_map/ppermute | solution.py:353
  21.7 3.9 %collective-permute-start.11 = (bf16[32,2048]{1,0:T(8,128)(2,1)S(1)}, bf16[32,2048]{1,0:T(8,128)(2,1)S(1)}, u32[]{:S(2)}, u32[]{:S(2)}) collective-permute-start(bf16[32,2048]{1,0:T(8,128)(2,1)S(1)} %get-tuple-element.36), channel_id=1, source_target_pairs={{0,1},{1,0},{2,3},{3,2},{4,5},{5,4},{6,7},{7,6},{8,9},{9,8},{10,11... | collective-permute-start | bytes 393224 | tf_op jit(solution)/shard_map/ppermute | solution.py:350
  24.2 8.6 %collective-permute-start.13 = (bf16[32,2304]{1,0:T(8,128)(2,1)S(1)}, bf16[32,2304]{1,0:T(8,128)(2,1)S(1)}, u32[]{:S(2)}, u32[]{:S(2)}) collective-permute-start(bf16[32,2304]{1,0:T(8,128)(2,1)S(1)} %get-tuple-element.40), channel_id=1, source_target_pairs={{0,4},{4,0},{8,12},{12,8},{1,5},{5,1},{9,13},{13,9},{2,6},{6,2},{1... | collective-permute-start | bytes 442376 | tf_op jit(solution)/shard_map/ppermute | solution.py:353
  25.2 7.6 %collective-permute-start.10 = (bf16[32,2048]{1,0:T(8,128)(2,1)S(1)}, bf16[32,2048]{1,0:T(8,128)(2,1)S(1)}, u32[]{:S(2)}, u32[]{:S(2)}) collective-permute-start(bf16[32,2048]{1,0:T(8,128)(2,1)S(1)} %get-tuple-element.34), channel_id=1, source_target_pairs={{0,1},{1,0},{2,3},{3,2},{4,5},{5,4},{6,7},{7,6},{8,9},{9,8},{10,11... | collective-permute-start | bytes 393224 | tf_op jit(solution)/shard_map/ppermute | solution.py:350
  25.2 7.0 %collective-permute-start.15 = (bf16[2,32,512]{2,1,0:T(8,128)(2,1)S(1)}, bf16[2,32,512]{2,1,0:T(8,128)(2,1)S(1)}, u32[]{:S(2)}, u32[]{:S(2)}) collective-permute-start(bf16[2,32,512]{2,1,0:T(8,128)(2,1)S(1)} %get-tuple-element.42), channel_id=1, source_target_pairs={{0,8},{1,13},{2,10},{3,15},{4,12},{5,9},{6,14},{7,11},{8,0},{9,5},... | collective-permute-start | bytes 196616 | tf_op jit(solution)/shard_map/ppermute | solution.py:361
  25.6 7.3 %collective-permute-start.12 = (bf16[32,2048]{1,0:T(8,128)(2,1)S(1)}, bf16[32,2048]{1,0:T(8,128)(2,1)S(1)}, u32[]{:S(2)}, u32[]{:S(2)}) collective-permute-start(bf16[32,2048]{1,0:T(8,128)(2,1)S(1)} %pair.1), channel_id=1, source_target_pairs={{0,2},{1,3},{2,0},{3,1},{4,6},{5,7},{6,4},{7,5},{8,10},{9,11},{10,... | collective-permute-start | bytes 393224 | tf_op jit(solution)/shard_map/ppermute | solution.py:353
  29.6 4.5 %collective-permute-start.16 = (bf16[32,1792]{1,0:T(8,128)(2,1)S(1)}, bf16[32,1792]{1,0:T(8,128)(2,1)S(1)}, u32[]{:S(2)}, u32[]{:S(2)}) collective-permute-start(bf16[32,1792]{1,0:T(8,128)(2,1)S(1)} %split.2), channel_id=1, source_target_pairs={{0,1},{1,0},{2,3},{3,2},{4,5},{5,4},{6,7},{7,6},{8,9},{9,8},{10,11... | collective-permute-start | bytes 344072 | tf_op jit(solution)/shard_map/ppermute | solution.py:350
  32.8 1.3 %collective-permute-start.17 = (bf16[32,1024]{1,0:T(8,128)(2,1)S(1)}, bf16[32,1024]{1,0:T(8,128)(2,1)S(1)}, u32[]{:S(2)}, u32[]{:S(2)}) collective-permute-start(bf16[32,1024]{1,0:T(8,128)(2,1)S(1)} %split.3), channel_id=1, source_target_pairs={{0,1},{1,0},{2,3},{3,2},{4,5},{5,4},{6,7},{7,6},{8,9},{9,8},{10,11... | collective-permute-start | bytes 196616 | tf_op jit(solution)/shard_map/ppermute | solution.py:350

commit v6 on v5

--- a/solution.py
+++ b/solution.py
@@ -218,7 +218,7 @@
     ranks_sum = rank_refs[0][...]
     for ref in rank_refs[1:]:
         ranks_sum = ranks_sum + ref[...]
-    high, low = two_terms(adapter_scale * ranks_sum.T)
+    terms_both = jnp.concatenate(two_terms(adapter_scale * ranks_sum.T), axis=0)
     for i in range(2):
         for b in range(ys):
             for ref, from_core in ((mine[b], core), (other[b], 1 - core)):
@@ -230,9 +230,8 @@
                         gradient[i, pl.ds(at, select), :] = ref[n, :, lane : lane + dps * group]
     for i in range(2):
         values = gradient[i]
-        product[i] = jnp.dot(high, values, preferred_element_type=f32) + jnp.dot(
-            low, values, preferred_element_type=f32
-        )
+        both = jnp.dot(terms_both, values, preferred_element_type=f32)
+        product[i] = both[:ranks] + both[ranks:]
 
     def up_part(target, i):
         column = (target * tensors + 2 * y + i) * block

time: 35 us -> 35 us (level)
  no operation moved by 1% of the time
where the time goes in v6:
time: 35 us; the launch traced here: 34.9 us
  waiting for transfers between devices  14 us (40%)
  starting transfers between devices  13.9 us (40%)
  Pallas kernels  6.24 us (18%)
  between operations  0.74 us (2%)
    ppermute x6, starting transfers between devices, over(): return lax.ppermute(value, axis, [(i, i ^ mask) for i in range(size)])  8.76 us
    ppermute x6, waiting for transfers between devices, over(): return lax.ppermute(value, axis, [(i, i ^ mask) for i in range(size)])  8.04 us
    ppermute x2, waiting for transfers between devices, far_dp(): return lax.ppermute(value, ('dp', 'tensor'), pairs)  4.92 us
    ppermute x2, starting transfers between devices, far_dp(): return lax.ppermute(value, ('dp', 'tensor'), pairs)  3.75 us
    pallas_call x1, Pallas kernels, shards(): pl.pallas_call(functools.partial(pick_kernel, trials, ys, dps, select, wi...  1.63 us
    ppermute x10, starting transfers between devices, to_core(): return lax.ppermute(value, 'tensor', [(i, i ^ 1) for i in range(tensors)])  1.37 us
    pallas_call x1, Pallas kernels, shards(): pl.pallas_call(functools.partial(base_kernel, ys), out_shape=[shape((loca...  1.37 us
    ppermute x10, waiting for transfers between devices, to_core(): return lax.ppermute(value, 'tensor', [(i, i ^ 1) for i in range(tensors)])  1.04 us
  transfers between devices with their start and end apart: 18, of which 9 were waited for; matrix products, arithmetic and copies ran while one was open for 0% of the time, Pallas kernels for 11%

profile of v6, /device:TPU:0, one launch (start us, length us, event | category | flops | bytes accessed | tf_op | source)
XLA Modules:
  0.0 34.9 jit_solution(12135060103365965851)
XLA Ops:
  0.6 1.6 %pick.1 = (bf16[2,16,3200]{2,1,0:T(8,128)(2,1)S(1)}, bf16[2,16,3200]{2,1,0:T(8,128)(2,1)S(1)}, bf16[1,1024,128]{2,1,0:T(8,128)(2,1)S(1)}, bf16[1,1024,128]{2,1,0...) custom-call(s32[2,128]{1,0:T(2,128)} %index_hbm.1, bf16[32,8192]{1,0:T(8,128)(2,1)} %rows_hbm.1, ...), custom_call_target="tpu_custom_call" | custom-call | tf_op jit(solution)/shard_map/pick/pallas_call | solution.py:380
  2.3 3.0 %collective-permute-start = (bf16[2,16,3200]{2,1,0:T(8,128)(2,1)S(1)}, bf16[2,16,3200]{2,1,0:T(8,128)(2,1)S(1)}, u32[]{:S(2)}, u32[]{:S(2)}) collective-permute-start(bf16[2,16,3200]{2,1,0:T(8,128)(2,1)S(1)} %get-tuple-element.25), channel_id=1, source_target_pairs={{0,2},{1,3},{2,0},{3,1},{16,18},{17,19},{18,16},{19,17},{4,6},{5,7... | collective-permute-start | bytes 614408 | tf_op jit(solution)/shard_map/ppermute | solution.py:352
  5.3 0.2 pick_others.1
  5.5 1.6 %collective-permute-start.1 = (bf16[2,16,2048]{2,1,0:T(8,128)(2,1)S(1)}, bf16[2,16,2048]{2,1,0:T(8,128)(2,1)S(1)}, u32[]{:S(2)}, u32[]{:S(2)}) collective-permute-start(bf16[2,16,2048]{2,1,0:T(8,128)(2,1)S(1)} %get-tuple-element.28), channel_id=1, source_target_pairs={{0,16},{1,17},{2,18},{3,19},{16,0},{17,1},{18,2},{19,3},{4,20},{5,... | collective-permute-start | bytes 393224 | tf_op jit(solution)/shard_map/ppermute | solution.py:352
  7.1 0.0 collective-permute-start.2
  7.1 4.0 %collective-permute-done.refs_1_.refs_3_ = bf16[2,16,3200]{2,1,0:T(8,128)(2,1)S(1)} collective-permute-done((bf16[2,16,3200]{2,1,0:T(8,128)(2,1)S(1)}, bf16[2,16,3200]{2,1,0:T(8,128)(2,1)S(1)}, u32[]{:S(2)}, u32[]{:S(2)}) %collective-permute-start) | collective-permute-done | bytes 204832 | tf_op jit(solution)/shard_map/ppermute | solution.py:352
  11.1 0.9 %collective-permute-done.1.refs_2_ = bf16[2,16,2048]{2,1,0:T(8,128)(2,1)S(1)} collective-permute-done((bf16[2,16,2048]{2,1,0:T(8,128)(2,1)S(1)}, bf16[2,16,2048]{2,1,0:T(8,128)(2,1)S(1)}, u32[]{:S(2)}, u32[]{:S(2)}) %collective-permute-start.1) | collective-permute-done | bytes 131104 | tf_op jit(solution)/shard_map/ppermute | solution.py:352
  11.9 1.2 %collective-permute-done.2.refs_3_ = bf16[2,16,2048]{2,1,0:T(8,128)(2,1)S(1)} collective-permute-done((bf16[2,16,2048]{2,1,0:T(8,128)(2,1)S(1)}, bf16[2,16,2048]{2,1,0:T(8,128)(2,1)S(1)}, u32[]{:S(2)}, u32[]{:S(2)}) %collective-permute-start.2) | collective-permute-done | bytes 131104 | tf_op jit(solution)/shard_map/ppermute | solution.py:352
  13.2 0.0 collective-permute-start.6
  13.2 0.5 %collective-permute-start.7 = (bf16[1,1024,128]{2,1,0:T(8,128)(2,1)S(1)}, bf16[1,1024,128]{2,1,0:T(8,128)(2,1)S(1)}, u32[]{:S(2)}, u32[]{:S(2)}) collective-permute-start(bf16[1,1024,128]{2,1,0:T(8,128)(2,1)S(1)} %get-tuple-element.31.refs_0_), channel_id=1, source_target_pairs={{0,1},{1,0},{2,3},{3,2},{4,5},{5,4},{6,7},{7,6},{8,9},{9,8},{10,11... | collective-permute-start | bytes 786440 | tf_op jit(solution)/shard_map/ppermute | solution.py:349
  13.7 0.0 collective-permute-done.3.refs_4_
  13.7 0.1 collective-permute-start.8
  13.8 0.7 %collective-permute-done.6.refs_7_ = bf16[2,16,2048]{2,1,0:T(8,128)(2,1)S(1)} collective-permute-done((bf16[2,16,2048]{2,1,0:T(8,128)(2,1)S(1)}, bf16[2,16,2048]{2,1,0:T(8,128)(2,1)S(1)}, u32[]{:S(2)}, u32[]{:S(2)}) %collective-permute-start.6) | collective-permute-done | bytes 131104 | tf_op jit(solution)/shard_map/ppermute | solution.py:349
  14.5 0.4 %terms.1 = (bf16[2,128,2048]{2,1,0:T(8,128)(2,1)S(1)}, bf16[128,128]{1,0:T(8,128)(2,1)S(1)}, bf16[2,32,1792]{2,1,0:T(8,128)(2,1)S(1)}) custom-call(bf16[2,16,3200]{2,1,0:T(8,128)(2,1)S(1)} %get-tuple-element.24.refs_0_.refs_2_, bf16[2,16,3200]{2,1,0:T(8,128)(2,1)S(1)} %collective-permute-done.refs_1_.refs_3_, ...), custom_call_target="tpu_custom_call" | custom-call | flops 20000000000 | bytes 20000000 | tf_op jit(solution)/shard_map/terms/pallas_call | solution.py:413
  14.9 0.0 copy-start
  14.9 3.4 %collective-permute-start.14 = (bf16[2,32,1792]{2,1,0:T(8,128)(2,1)S(1)}, bf16[2,32,1792]{2,1,0:T(8,128)(2,1)S(1)}, u32[]{:S(2)}, u32[]{:S(2)}) collective-permute-start(bf16[2,32,1792]{2,1,0:T(8,128)(2,1)S(1)} %get-tuple-element.41), channel_id=1, source_target_pairs={{0,8},{1,13},{2,10},{3,15},{4,12},{5,9},{6,14},{7,11},{8,0},{9,5},... | collective-permute-start | bytes 688136 | tf_op jit(solution)/shard_map/ppermute | solution.py:360
  18.3 0.4 %rank.1.refs_0_ = f32[128,128]{1,0:T(8,128)S(1)} custom-call(bf16[2,128,2048]{2,1,0:T(8,128)(2,1)S(1)} %get-tuple-element.30.pair.refs_6_, bf16[1,1024,128]{2,1,0:T(8,128)(2,1)S(1)} %get-tuple-element.31.refs_0_, bf16[1,1024,128]{2,1,0:T(8,128)(2,1)S(1)} %get-tuple-element.32.refs_1_, bf16[1,1024,128]{2,1,0:T(8,128)(2,1)S(1)} %collective-permute-done.7.refs_2_, ...), custom_call_target="tpu_custom_call" | custom-call | tf_op jit(solution)/shard_map/rank/pallas_call | solution.py:425
  18.8 1.6 %collective-permute-start.9 = (f32[128,128]{1,0:T(8,128)S(1)}, f32[128,128]{1,0:T(8,128)S(1)}, u32[]{:S(2)}, u32[]{:S(2)}) collective-permute-start(f32[128,128]{1,0:T(8,128)S(1)} %rank.1.refs_0_), channel_id=1, source_target_pairs={{0,2},{1,3},{2,0},{3,1},{4,6},{5,7},{6,4},{7,5},{8,10},{9,11},{10,... | collective-permute-start | bytes 196616 | tf_op jit(solution)/shard_map/ppermute | solution.py:352
  20.3 1.4 %base.1 = (f32[32,2048]{1,0:T(8,128)S(1)}, f32[32,2048]{1,0:T(8,128)S(1)}, bf16[32,2048]{1,0:T(8,128)(2,1)S(1)}, bf16[32,2048]{1,0:T(8,128)(2,1)S(1)}) custom-call(bf16[2,128,2048]{2,1,0:T(8,128)(2,1)S(1)} %get-tuple-element.30.pair.refs_6_, bf16[2048,2048]{1,0:T(8,128)(2,1)S(1)} %bitcast.2), custom_call_target="tpu_custom_call" | custom-call | tf_op jit(solution)/shard_map/base/pallas_call | solution.py:436
  21.7 0.7 %collective-permute-start.11 = (bf16[32,2048]{1,0:T(8,128)(2,1)S(1)}, bf16[32,2048]{1,0:T(8,128)(2,1)S(1)}, u32[]{:S(2)}, u32[]{:S(2)}) collective-permute-start(bf16[32,2048]{1,0:T(8,128)(2,1)S(1)} %get-tuple-element.36), channel_id=1, source_target_pairs={{0,1},{1,0},{2,3},{3,2},{4,5},{5,4},{6,7},{7,6},{8,9},{9,8},{10,11... | collective-permute-start | bytes 393224 | tf_op jit(solution)/shard_map/ppermute | solution.py:349
  22.4 1.3 %collective-permute-done.9.refs_1_ = f32[128,128]{1,0:T(8,128)S(1)} collective-permute-done((f32[128,128]{1,0:T(8,128)S(1)}, f32[128,128]{1,0:T(8,128)S(1)}, u32[]{:S(2)}, u32[]{:S(2)}) %collective-permute-start.9) | collective-permute-done | bytes 65568 | tf_op jit(solution)/shard_map/ppermute | solution.py:352
  23.7 0.5 %up_terms.1 = (f32[32,2048]{1,0:T(8,128)S(1)}, f32[64,128]{1,0:T(8,128)S(1)}, bf16[32,2304]{1,0:T(8,128)(2,1)S(1)}, bf16[2,32,512]{2,1,0:T(8,128)(2,1)S(1)}) custom-call(f32[128,128]{1,0:T(8,128)S(1)} %rank.1.refs_0_, f32[128,128]{1,0:T(8,128)S(1)} %collective-permute-done.9.refs_1_, bf16[2,16,3200]{2,1,0:T(8,128)(2,1)S(1)} %get-tuple-element.24.refs_0_.refs_2_, ...), custom_call_target="tpu_custom_call" | custom-call | tf_op jit(solution)/shard_map/up_terms/pallas_call | solution.py:464
  24.2 1.0 %collective-permute-start.13 = (bf16[32,2304]{1,0:T(8,128)(2,1)S(1)}, bf16[32,2304]{1,0:T(8,128)(2,1)S(1)}, u32[]{:S(2)}, u32[]{:S(2)}) collective-permute-start(bf16[32,2304]{1,0:T(8,128)(2,1)S(1)} %get-tuple-element.40), channel_id=1, source_target_pairs={{0,4},{4,0},{8,12},{12,8},{1,5},{5,1},{9,13},{13,9},{2,6},{6,2},{1... | collective-permute-start | bytes 442376 | tf_op jit(solution)/shard_map/ppermute | solution.py:352
  25.2 0.4 %collective-permute-start.15 = (bf16[2,32,512]{2,1,0:T(8,128)(2,1)S(1)}, bf16[2,32,512]{2,1,0:T(8,128)(2,1)S(1)}, u32[]{:S(2)}, u32[]{:S(2)}) collective-permute-start(bf16[2,32,512]{2,1,0:T(8,128)(2,1)S(1)} %get-tuple-element.42), channel_id=1, source_target_pairs={{0,8},{1,13},{2,10},{3,15},{4,12},{5,9},{6,14},{7,11},{8,0},{9,5},... | collective-permute-start | bytes 196616 | tf_op jit(solution)/shard_map/ppermute | solution.py:360
  25.6 1.6 %collective-permute-start.12 = (bf16[32,2048]{1,0:T(8,128)(2,1)S(1)}, bf16[32,2048]{1,0:T(8,128)(2,1)S(1)}, u32[]{:S(2)}, u32[]{:S(2)}) collective-permute-start(bf16[32,2048]{1,0:T(8,128)(2,1)S(1)} %pair.1), channel_id=1, source_target_pairs={{0,2},{1,3},{2,0},{3,1},{4,6},{5,7},{6,4},{7,5},{8,10},{9,11},{10,... | collective-permute-start | bytes 393224 | tf_op jit(solution)/shard_map/ppermute | solution.py:352
  27.2 2.4 %collective-permute-done.14.refs_0_.refs_3_ = bf16[2,32,1792]{2,1,0:T(8,128)(2,1)S(1)} collective-permute-done((bf16[2,32,1792]{2,1,0:T(8,128)(2,1)S(1)}, bf16[2,32,1792]{2,1,0:T(8,128)(2,1)S(1)}, u32[]{:S(2)}, u32[]{:S(2)}) %collective-permute-start.14) | collective-permute-done | bytes 229408 | tf_op jit(solution)/shard_map/ppermute | solution.py:360
  29.6 0.1 collective-permute-start.16
  29.7 2.5 %collective-permute-done.15.refs_0_.refs_4_ = bf16[2,32,512]{2,1,0:T(8,128)(2,1)S(1)} collective-permute-done((bf16[2,32,512]{2,1,0:T(8,128)(2,1)S(1)}, bf16[2,32,512]{2,1,0:T(8,128)(2,1)S(1)}, u32[]{:S(2)}, u32[]{:S(2)}) %collective-permute-start.15) | collective-permute-done | bytes 65568 | tf_op jit(solution)/shard_map/ppermute | solution.py:360
  32.2 0.6 %collective-permute-done.13.refs_1_.refs_2_ = bf16[32,2304]{1,0:T(8,128)(2,1)S(1)} collective-permute-done((bf16[32,2304]{1,0:T(8,128)(2,1)S(1)}, bf16[32,2304]{1,0:T(8,128)(2,1)S(1)}, u32[]{:S(2)}, u32[]{:S(2)}) %collective-permute-start.13) | collective-permute-done | bytes 147488 | tf_op jit(solution)/shard_map/ppermute | solution.py:352
  32.9 0.9 %output.1 = f32[1,32,2048]{2,1,0:T(8,128)} custom-call(f32[128,128]{1,0:T(8,128)S(1)} %rank.1.refs_0_, f32[128,128]{1,0:T(8,128)S(1)} %collective-permute-done.9.refs_1_, f32[32,2048]{1,0:T(8,128)S(1)} %get-tuple-element.33.refs_2_, bf16[32,2048]{1,0:T(8,128)(2,1)S(1)} %collective-permute-done.10.refs_3_, ...), custom_call_target="tpu_custom_call" | custom-call | tf_op jit(solution)/shard_map/output/pallas_call | solution.py:481
  33.8 0.3 collective-permute-done.17.refs_6_
  34.1 0.8 %sums.1 = (f32[1,32,2048]{2,1,0:T(8,128)}, f32[1,64,128]{2,1,0:T(8,128)}) custom-call(f32[32,2048]{1,0:T(8,128)S(1)} %get-tuple-element.38.refs_0_, f32[64,128]{1,0:T(8,128)S(1)} %get-tuple-element.39.refs_1_, bf16[32,2304]{1,0:T(8,128)(2,1)S(1)} %collective-permute-done.13.refs_1_.refs_2_, bf16[2,32,1792]{2,1,0:T(8,128)(2,1)S(1)} %collective-permute-done.14.refs_0_.refs_3_, ...), custom_call_target="tpu_custom_call" | custom-call | tf_op jit(solution)/shard_map/sums/pallas_call | solution.py:503
  (22 shorter events, 0.1 us)
Async XLA Ops:
  2.3 8.8 %collective-permute-start = (bf16[2,16,3200]{2,1,0:T(8,128)(2,1)S(1)}, bf16[2,16,3200]{2,1,0:T(8,128)(2,1)S(1)}, u32[]{:S(2)}, u32[]{:S(2)}) collective-permute-start(bf16[2,16,3200]{2,1,0:T(8,128)(2,1)S(1)} %get-tuple-element.25), channel_id=1, source_target_pairs={{0,2},{1,3},{2,0},{3,1},{16,18},{17,19},{18,16},{19,17},{4,6},{5,7... | collective-permute-start | bytes 614408 | tf_op jit(solution)/shard_map/ppermute | solution.py:352
  5.5 6.4 %collective-permute-start.1 = (bf16[2,16,2048]{2,1,0:T(8,128)(2,1)S(1)}, bf16[2,16,2048]{2,1,0:T(8,128)(2,1)S(1)}, u32[]{:S(2)}, u32[]{:S(2)}) collective-permute-start(bf16[2,16,2048]{2,1,0:T(8,128)(2,1)S(1)} %get-tuple-element.28), channel_id=1, source_target_pairs={{0,16},{1,17},{2,18},{3,19},{16,0},{17,1},{18,2},{19,3},{4,20},{5,... | collective-permute-start | bytes 393224 | tf_op jit(solution)/shard_map/ppermute | solution.py:352
  7.1 6.1 %collective-permute-start.2 = (bf16[2,16,2048]{2,1,0:T(8,128)(2,1)S(1)}, bf16[2,16,2048]{2,1,0:T(8,128)(2,1)S(1)}, u32[]{:S(2)}, u32[]{:S(2)}) collective-permute-start(bf16[2,16,2048]{2,1,0:T(8,128)(2,1)S(1)} %get-tuple-element.29), channel_id=1, source_target_pairs={{0,18},{1,19},{2,16},{3,17},{16,2},{17,3},{18,0},{19,1},{4,22},{5,... | collective-permute-start | bytes 393224 | tf_op jit(solution)/shard_map/ppermute | solution.py:352
  7.1 6.6 %collective-permute-start.3 = (bf16[2,16,3200]{2,1,0:T(8,128)(2,1)S(1)}, bf16[2,16,3200]{2,1,0:T(8,128)(2,1)S(1)}, u32[]{:S(2)}, u32[]{:S(2)}) collective-permute-start(bf16[2,16,3200]{2,1,0:T(8,128)(2,1)S(1)} %get-tuple-element.24.refs_0_.refs_2_), channel_id=1, source_target_pairs={{0,1},{1,0},{2,3},{3,2},{4,5},{5,4},{6,7},{7,6},{8,9},{9,8},{10,11... | collective-permute-start | bytes 614408 | tf_op jit(solution)/shard_map/ppermute | solution.py:349
  11.1 3.5 %collective-permute-start.4 = (bf16[2,16,3200]{2,1,0:T(8,128)(2,1)S(1)}, bf16[2,16,3200]{2,1,0:T(8,128)(2,1)S(1)}, u32[]{:S(2)}, u32[]{:S(2)}) collective-permute-start(bf16[2,16,3200]{2,1,0:T(8,128)(2,1)S(1)} %collective-permute-done.refs_1_.refs_3_), channel_id=1, source_target_pairs={{0,1},{1,0},{2,3},{3,2},{4,5},{5,4},{6,7},{7,6},{8,9},{9,8},{10,11... | collective-permute-start | bytes 614408 | tf_op jit(solution)/shard_map/ppermute | solution.py:349
  11.9 1.9 %collective-permute-start.5 = (bf16[2,16,2048]{2,1,0:T(8,128)(2,1)S(1)}, bf16[2,16,2048]{2,1,0:T(8,128)(2,1)S(1)}, u32[]{:S(2)}, u32[]{:S(2)}) collective-permute-start(bf16[2,16,2048]{2,1,0:T(8,128)(2,1)S(1)} %collective-permute-done.1.refs_2_), channel_id=1, source_target_pairs={{0,1},{1,0},{2,3},{3,2},{4,5},{5,4},{6,7},{7,6},{8,9},{9,8},{10,11... | collective-permute-start | bytes 393224 | tf_op jit(solution)/shard_map/ppermute | solution.py:349
  13.2 1.3 %collective-permute-start.6 = (bf16[2,16,2048]{2,1,0:T(8,128)(2,1)S(1)}, bf16[2,16,2048]{2,1,0:T(8,128)(2,1)S(1)}, u32[]{:S(2)}, u32[]{:S(2)}) collective-permute-start(bf16[2,16,2048]{2,1,0:T(8,128)(2,1)S(1)} %collective-permute-done.2.refs_3_), channel_id=1, source_target_pairs={{0,1},{1,0},{2,3},{3,2},{4,5},{5,4},{6,7},{7,6},{8,9},{9,8},{10,11... | collective-permute-start | bytes 393224 | tf_op jit(solution)/shard_map/ppermute | solution.py:349
  13.2 5.1 %collective-permute-start.7 = (bf16[1,1024,128]{2,1,0:T(8,128)(2,1)S(1)}, bf16[1,1024,128]{2,1,0:T(8,128)(2,1)S(1)}, u32[]{:S(2)}, u32[]{:S(2)}) collective-permute-start(bf16[1,1024,128]{2,1,0:T(8,128)(2,1)S(1)} %get-tuple-element.31.refs_0_), channel_id=1, source_target_pairs={{0,1},{1,0},{2,3},{3,2},{4,5},{5,4},{6,7},{7,6},{8,9},{9,8},{10,11... | collective-permute-start | bytes 786440 | tf_op jit(solution)/shard_map/ppermute | solution.py:349
  13.7 6.6 %slice-start = ((s8[8388608]{0:T(1024)(128)(4,1)}), s8[4194304]{0:T(1024)(128)(4,1)S(1)}, s32[]{:S(2)}) async-start(s8[8388608]{0:T(1024)(128)(4,1)} %bitcast.1), calls=%async_computation | async-start | bytes 8388608
  13.7 6.6 %slice-start.1 = ((s8[8388608]{0:T(1024)(128)(4,1)}), s8[4194304]{0:T(1024)(128)(4,1)S(1)}, s32[]{:S(2)}) async-start(s8[8388608]{0:T(1024)(128)(4,1)} %bitcast.1), calls=%async_computation.1 | async-start | bytes 8388608
  13.7 4.6 %collective-permute-start.8 = (bf16[1,1024,128]{2,1,0:T(8,128)(2,1)S(1)}, bf16[1,1024,128]{2,1,0:T(8,128)(2,1)S(1)}, u32[]{:S(2)}, u32[]{:S(2)}) collective-permute-start(bf16[1,1024,128]{2,1,0:T(8,128)(2,1)S(1)} %get-tuple-element.32.refs_1_), channel_id=1, source_target_pairs={{0,1},{1,0},{2,3},{3,2},{4,5},{5,4},{6,7},{7,6},{8,9},{9,8},{10,11... | collective-permute-start | bytes 786440 | tf_op jit(solution)/shard_map/ppermute | solution.py:349
  14.9 18.0 %copy-start = (bf16[1,64,2048]{2,1,0:T(8,128)(2,1)S(1)}, bf16[1,64,2048]{2,1,0:T(8,128)(2,1)}, u32[]{:S(2)}) copy-start(bf16[1,64,2048]{2,1,0:T(8,128)(2,1)} %refs_5_.1) | copy-start | bytes 786436
  14.9 14.7 %collective-permute-start.14 = (bf16[2,32,1792]{2,1,0:T(8,128)(2,1)S(1)}, bf16[2,32,1792]{2,1,0:T(8,128)(2,1)S(1)}, u32[]{:S(2)}, u32[]{:S(2)}) collective-permute-start(bf16[2,32,1792]{2,1,0:T(8,128)(2,1)S(1)} %get-tuple-element.41), channel_id=1, source_target_pairs={{0,8},{1,13},{2,10},{3,15},{4,12},{5,9},{6,14},{7,11},{8,0},{9,5},... | collective-permute-start | bytes 688136 | tf_op jit(solution)/shard_map/ppermute | solution.py:360
  18.8 5.0 %collective-permute-start.9 = (f32[128,128]{1,0:T(8,128)S(1)}, f32[128,128]{1,0:T(8,128)S(1)}, u32[]{:S(2)}, u32[]{:S(2)}) collective-permute-start(f32[128,128]{1,0:T(8,128)S(1)} %rank.1.refs_0_), channel_id=1, source_target_pairs={{0,2},{1,3},{2,0},{3,1},{4,6},{5,7},{6,4},{7,5},{8,10},{9,11},{10,... | collective-permute-start | bytes 196616 | tf_op jit(solution)/shard_map/ppermute | solution.py:352
  21.7 3.9 %collective-permute-start.11 = (bf16[32,2048]{1,0:T(8,128)(2,1)S(1)}, bf16[32,2048]{1,0:T(8,128)(2,1)S(1)}, u32[]{:S(2)}, u32[]{:S(2)}) collective-permute-start(bf16[32,2048]{1,0:T(8,128)(2,1)S(1)} %get-tuple-element.36), channel_id=1, source_target_pairs={{0,1},{1,0},{2,3},{3,2},{4,5},{5,4},{6,7},{7,6},{8,9},{9,8},{10,11... | collective-permute-start | bytes 393224 | tf_op jit(solution)/shard_map/ppermute | solution.py:349
  24.2 8.6 %collective-permute-start.13 = (bf16[32,2304]{1,0:T(8,128)(2,1)S(1)}, bf16[32,2304]{1,0:T(8,128)(2,1)S(1)}, u32[]{:S(2)}, u32[]{:S(2)}) collective-permute-start(bf16[32,2304]{1,0:T(8,128)(2,1)S(1)} %get-tuple-element.40), channel_id=1, source_target_pairs={{0,4},{4,0},{8,12},{12,8},{1,5},{5,1},{9,13},{13,9},{2,6},{6,2},{1... | collective-permute-start | bytes 442376 | tf_op jit(solution)/shard_map/ppermute | solution.py:352
  25.2 7.6 %collective-permute-start.10 = (bf16[32,2048]{1,0:T(8,128)(2,1)S(1)}, bf16[32,2048]{1,0:T(8,128)(2,1)S(1)}, u32[]{:S(2)}, u32[]{:S(2)}) collective-permute-start(bf16[32,2048]{1,0:T(8,128)(2,1)S(1)} %get-tuple-element.34), channel_id=1, source_target_pairs={{0,1},{1,0},{2,3},{3,2},{4,5},{5,4},{6,7},{7,6},{8,9},{9,8},{10,11... | collective-permute-start | bytes 393224 | tf_op jit(solution)/shard_map/ppermute | solution.py:349
  25.2 7.0 %collective-permute-start.15 = (bf16[2,32,512]{2,1,0:T(8,128)(2,1)S(1)}, bf16[2,32,512]{2,1,0:T(8,128)(2,1)S(1)}, u32[]{:S(2)}, u32[]{:S(2)}) collective-permute-start(bf16[2,32,512]{2,1,0:T(8,128)(2,1)S(1)} %get-tuple-element.42), channel_id=1, source_target_pairs={{0,8},{1,13},{2,10},{3,15},{4,12},{5,9},{6,14},{7,11},{8,0},{9,5},... | collective-permute-start | bytes 196616 | tf_op jit(solution)/shard_map/ppermute | solution.py:360
  25.6 7.3 %collective-permute-start.12 = (bf16[32,2048]{1,0:T(8,128)(2,1)S(1)}, bf16[32,2048]{1,0:T(8,128)(2,1)S(1)}, u32[]{:S(2)}, u32[]{:S(2)}) collective-permute-start(bf16[32,2048]{1,0:T(8,128)(2,1)S(1)} %pair.1), channel_id=1, source_target_pairs={{0,2},{1,3},{2,0},{3,1},{4,6},{5,7},{6,4},{7,5},{8,10},{9,11},{10,... | collective-permute-start | bytes 393224 | tf_op jit(solution)/shard_map/ppermute | solution.py:352
  29.6 4.5 %collective-permute-start.16 = (bf16[32,1792]{1,0:T(8,128)(2,1)S(1)}, bf16[32,1792]{1,0:T(8,128)(2,1)S(1)}, u32[]{:S(2)}, u32[]{:S(2)}) collective-permute-start(bf16[32,1792]{1,0:T(8,128)(2,1)S(1)} %split.2), channel_id=1, source_target_pairs={{0,1},{1,0},{2,3},{3,2},{4,5},{5,4},{6,7},{7,6},{8,9},{9,8},{10,11... | collective-permute-start | bytes 344072 | tf_op jit(solution)/shard_map/ppermute | solution.py:349
  32.8 1.3 %collective-permute-start.17 = (bf16[32,1024]{1,0:T(8,128)(2,1)S(1)}, bf16[32,1024]{1,0:T(8,128)(2,1)S(1)}, u32[]{:S(2)}, u32[]{:S(2)}) collective-permute-start(bf16[32,1024]{1,0:T(8,128)(2,1)S(1)} %split.3), channel_id=1, source_target_pairs={{0,1},{1,0},{2,3},{3,2},{4,5},{5,4},{6,7},{7,6},{8,9},{9,8},{10,11... | collective-permute-start | bytes 196616 | tf_op jit(solution)/shard_map/ppermute | solution.py:349
